TPU v7x, 32 devices: a whole 2x2x4 slice. The times are simulated.
32 devices in a mesh: dp: 4 (over z), mp: 2 (over x), dmod: 4 (over y, core).
Axes of the slice: x: 2, y: 2, z: 4, core: 2. Of those that a mesh axis runs over, the one named last changes fastest.
Arguments:
- block_input: bfloat16 [2, 4, 256, 2048], P(None, 'dp', None, 'dmod'), may hold values from -6 to 6
- segment_ids: int32 [2, 4, 256], P(None, 'dp'), may hold values from 0 to 5, never falling along the last dimension, each value on 1 to 128 neighbouring positions
- group_ids: int32 [2, 4, 256], P(None, 'dp'), may hold values from 0 to 7
- group_weight: float32 [8], replicated, may hold values from 0.5 to 2
- mixer_norm: bfloat16 [2048], P(('dmod', 'dp')), may hold values from 0.5 to 1.5
- w_mix: bfloat16 [2048, 4, 2048], P(('dmod', 'dp'), None, 'mp'), may hold values from -0.125 to 0.125
- w_beta: bfloat16 [2048, 16], P(('dmod', 'dp'), 'mp'), may hold values from -0.125 to 0.125
- conv_kernel: bfloat16 [3, 4, 2048], P(None, None, ('mp', 'dmod', 'dp')), may hold values from -3 to 3
- head_norm: bfloat16 [128], P('dp'), may hold values from 0.5 to 1.5
- w_out: bfloat16 [2048, 2048], P('mp', ('dmod', 'dp')), may hold values from -0.1875 to 0.1875
- ffn_norm: bfloat16 [2048], P(('dmod', 'dp')), may hold values from 0.5 to 1.5
- w_ffn_in: bfloat16 [2048, 2, 5632], P(('dmod', 'dp'), None, 'mp'), may hold values from -0.125 to 0.125
- w_ffn_down: bfloat16 [5632, 2048], P('mp', ('dmod', 'dp')), may hold values from -0.109375 to 0.109375
- cotangent: bfloat16 [2, 4, 256, 2048], P(None, 'dp', None, 'dmod'), may hold values from -6 to 6
Outputs:
- out: bfloat16 [2, 4, 256, 2048], P(None, 'dp', None, 'dmod')
- grad_input: float32 [2, 4, 256, 2048], P(None, 'dp', None, 'dmod')
- grad_mixer_norm: float32 [2048], P(('dmod', 'dp'))
- grad_w_mix: float32 [2048, 4, 2048], P(('dmod', 'dp'), None, 'mp')
- grad_w_beta: float32 [2048, 16], P(('dmod', 'dp'), 'mp')
- grad_conv_kernel: float32 [3, 4, 2048], P(None, None, ('mp', 'dmod', 'dp'))
- grad_head_norm: float32 [128], P('dp')
- grad_w_out: float32 [2048, 2048], P('mp', ('dmod', 'dp'))
- grad_ffn_norm: float32 [2048], P(('dmod', 'dp'))
- grad_w_ffn_in: float32 [2048, 2, 5632], P(('dmod', 'dp'), None, 'mp')
- grad_w_ffn_down: float32 [5632, 2048], P('mp', ('dmod', 'dp'))
Inputs may be any that keep to these rules, and one draw needn't show every extreme that they name: `segment_ids`: never falls along a sequence; a document holds at most 128 tokens, and one holds exactly that many.
All inputs are finite; a program needn't handle non-finite values.
Results may differ from a plain program's by a relative error of at most 0.017.
Values may be sent and summed in bfloat16 or wider, within the bound.
No kernel may reach another device: no remote copies, remote signals or barrier semaphores. Data moves between devices by JAX's collectives and lax.ppermute only.
A program may use at most 192 MiB of HBM per device.

v0:
```python
from functools import partial

import jax
import jax.numpy as jnp
from jax import lax
from jax.sharding import PartitionSpec as P

D = 2048
BLOCK = 64


def short_conv(signal, kernel, segment):
    length = signal.shape[0]
    total = signal * kernel[-1]
    for shift in range(1, kernel.shape[0]):
        moved = jnp.concatenate(
            [jnp.zeros((shift, signal.shape[1]), signal.dtype), signal[: length - shift]], 0
        )
        earlier = jnp.concatenate([jnp.full((shift,), -1, jnp.int32), segment[: length - shift]], 0)
        keep = (earlier == segment).astype(signal.dtype)
        total = total + moved * keep[:, None] * kernel[-1 - shift]
    return total


def delta_block(carry, inputs):
    state, previous = carry
    query, key, value, beta, segment = inputs
    highest = lax.Precision.HIGHEST
    size = segment.shape[0]
    same = (segment[:, None] == segment[None, :]).astype(query.dtype)
    carried = (segment == previous).astype(query.dtype)
    strict = jnp.tril(jnp.ones((size, size), query.dtype), -1)
    inclusive = jnp.tril(jnp.ones((size, size), query.dtype))
    gram = jnp.einsum("ihd,jhd->hij", key, key, precision=highest)
    system = (
        jnp.eye(size, dtype=query.dtype)[None] + gram * beta.T[:, :, None] * (same * strict)[None]
    )
    recalled = jnp.einsum("hvk,ihk->hiv", state, key, precision=highest) * carried[None, :, None]
    target = beta.T[:, :, None] * (jnp.transpose(value, (1, 0, 2)) - recalled)
    solver = jax.vmap(partial(jax.scipy.linalg.solve_triangular, lower=True, unit_diagonal=True))
    update = solver(system, target)
    scores = jnp.einsum("ihd,jhd->hij", query, key, precision=highest) * (same * inclusive)[None]
    output = jnp.einsum("hvk,ihk->hiv", state, query, precision=highest) * carried[None, :, None]
    output = output + jnp.einsum("hij,hjv->hiv", scores, update, precision=highest)
    last = (segment == segment[-1]).astype(query.dtype)
    state = carried[-1] * state + jnp.einsum(
        "hjv,jhk->hvk", update * last[None, :, None], key, precision=highest
    )
    return ((state, segment[-1]), jnp.transpose(output, (1, 0, 2)))


def delta_rule(query, key, value, beta, segment):
    length, heads, size = query.shape
    blocks = length // BLOCK

    def blocked(values):
        return values.reshape((blocks, BLOCK) + values.shape[1:])

    start = (jnp.zeros((heads, size, size), query.dtype), jnp.array(-1, dtype=jnp.int32))
    carry_out, outputs = lax.scan(
        jax.checkpoint(delta_block),
        start,
        (blocked(query), blocked(key), blocked(value), blocked(beta), blocked(segment)),
    )
    return outputs.reshape(length, heads, size)


def unit_heads(values, heads):
    split_view = values.reshape(values.shape[0], heads, -1)
    return split_view * lax.rsqrt(jnp.sum(split_view * split_view, -1, keepdims=True) + 1e-06)


def mixer_local(projected, beta_in, kernels, head_gain, segment):
    length = projected.shape[0]
    heads = beta_in.shape[1]
    size = head_gain.shape[0]
    convolved = [
        jax.nn.silu(short_conv(projected[:, part], kernels[part], segment)) for part in range(3)
    ]
    query = unit_heads(convolved[0], heads) * size ** (-0.5)
    key = unit_heads(convolved[1], heads)
    value = convolved[2].reshape(length, heads, size)
    beta = jax.nn.sigmoid(beta_in)
    mixed = delta_rule(query, key, value, beta, segment)
    normed = mixed * lax.rsqrt(jnp.mean(mixed * mixed, -1, keepdims=True) + 1e-05) * head_gain
    return normed.reshape(length, -1) * jax.nn.silu(projected[:, 3])


def contract(left, right, left_dim, right_dim):
    return lax.dot_general(
        left, right, (((left_dim,), (right_dim,)), ((), ())), preferred_element_type=jnp.float32
    )


def row_total(values):
    return lax.psum(values, "dmod")


def sum_widths(values):
    return lax.psum(values, "mp")


def gather_features(values):
    return lax.all_gather(values, "dmod", axis=1, tiled=True)


def share_features(values):
    return lax.psum_scatter(values, "dmod", scatter_dimension=1, tiled=True)


def fetch_block(params):
    (
        norm_one,
        mix_weights,
        beta_weights,
        kernels,
        head_gain,
        out_weights,
        norm_two,
        ffn_weights,
        down_weights,
    ) = params
    return (
        lax.all_gather(norm_one, "dp", axis=0, tiled=True),
        lax.all_gather(mix_weights, "dp", axis=0, tiled=True),
        lax.all_gather(beta_weights, "dp", axis=0, tiled=True),
        lax.all_gather(kernels, "dp", axis=2, tiled=True),
        lax.all_gather(head_gain, "dp", axis=0, tiled=True),
        lax.all_gather(out_weights, "dp", axis=1, tiled=True),
        lax.all_gather(norm_two, "dp", axis=0, tiled=True),
        lax.all_gather(ffn_weights, "dp", axis=0, tiled=True),
        lax.all_gather(down_weights, "dp", axis=1, tiled=True),
    )


def reduce_grads(pieces):
    (
        grad_norm_one,
        grad_mix,
        grad_beta,
        grad_kernels,
        grad_head,
        grad_out,
        grad_norm_two,
        grad_ffn,
        grad_down,
    ) = pieces
    return (
        lax.psum_scatter(
            grad_norm_one.astype(jnp.bfloat16), "dp", scatter_dimension=0, tiled=True
        ).astype(jnp.float32),
        lax.psum_scatter(
            grad_mix.astype(jnp.bfloat16), "dp", scatter_dimension=0, tiled=True
        ).astype(jnp.float32),
        lax.psum_scatter(
            grad_beta.astype(jnp.bfloat16), "dp", scatter_dimension=0, tiled=True
        ).astype(jnp.float32),
        lax.psum_scatter(
            grad_kernels.astype(jnp.bfloat16), "dp", scatter_dimension=2, tiled=True
        ).astype(jnp.float32),
        lax.psum_scatter(
            grad_head.astype(jnp.bfloat16), "dp", scatter_dimension=0, tiled=True
        ).astype(jnp.float32),
        lax.psum_scatter(
            grad_out.astype(jnp.bfloat16), "dp", scatter_dimension=1, tiled=True
        ).astype(jnp.float32),
        lax.psum_scatter(
            grad_norm_two.astype(jnp.bfloat16), "dp", scatter_dimension=0, tiled=True
        ).astype(jnp.float32),
        lax.psum_scatter(
            grad_ffn.astype(jnp.bfloat16), "dp", scatter_dimension=0, tiled=True
        ).astype(jnp.float32),
        lax.psum_scatter(
            grad_down.astype(jnp.bfloat16), "dp", scatter_dimension=1, tiled=True
        ).astype(jnp.float32),
    )


def body(
    block_input,
    segment_ids,
    group_ids,
    group_weight,
    mixer_norm,
    w_mix,
    w_beta,
    conv_kernel,
    head_norm,
    w_out,
    ffn_norm,
    w_ffn_in,
    w_ffn_down,
    cotangent,
):
    micro = block_input.shape[0]
    length = block_input.shape[2]
    groups = group_weight.shape[0]
    data_size = lax.axis_size("dp")
    marks = (group_ids[..., None] == jnp.arange(groups, dtype=jnp.int32)).astype(jnp.float32)
    counts = lax.psum(jnp.sum(marks.reshape(-1, groups), 0), "dp")
    total_tokens = micro * length * data_size
    table = group_weight * (total_tokens / groups) / counts
    scales = jnp.sum(marks * table, -1)
    params = (
        mixer_norm,
        w_mix,
        w_beta,
        conv_kernel,
        head_norm,
        w_out,
        ffn_norm,
        w_ffn_in,
        w_ffn_down,
    )

    def fetch_arranged():
        block = fetch_block(params)
        return block

    outputs = []
    input_grads = []
    totals = None
    summed = None
    for index in range(micro):
        forward_set = fetch_arranged()
        (
            norm_one,
            mix_weights,
            beta_weights,
            kernels,
            head_gain,
            out_weights,
            norm_two,
            ffn_weights,
            down_weights,
        ) = forward_set
        rows = block_input[index, 0].astype(jnp.float32)
        segment = segment_ids[index, 0]
        width_rows = mix_weights.shape[0]
        first_scale = lax.rsqrt(row_total(jnp.sum(rows * rows, -1)) / D + 1e-06)
        gain_one = norm_one.astype(jnp.float32)
        mixer_in = (rows * first_scale[:, None] * gain_one).astype(jnp.bfloat16)
        projected_part = jnp.dot(
            mixer_in, mix_weights.reshape(width_rows, -1), preferred_element_type=jnp.float32
        ).reshape(length, 4, -1)
        beta_part = jnp.dot(mixer_in, beta_weights, preferred_element_type=jnp.float32)
        projected, beta_in = (
            lax.psum_scatter(projected_part, "dmod", scatter_dimension=2, tiled=True),
            lax.psum_scatter(beta_part, "dmod", scatter_dimension=1, tiled=True),
        )
        gated, mixer_back = jax.vjp(
            partial(mixer_local, segment=segment),
            projected,
            beta_in,
            kernels.astype(jnp.float32),
            head_gain.astype(jnp.float32),
        )
        gated_low = gated.astype(jnp.bfloat16)
        gated_keep = gather_features(gated_low)
        branch_sum = jnp.dot(gated_keep, out_weights, preferred_element_type=jnp.float32)
        middle = rows + sum_widths(branch_sum)
        second_scale = lax.rsqrt(row_total(jnp.sum(middle * middle, -1)) / D + 1e-06)
        gain_two = norm_two.astype(jnp.float32)
        ffn_in = (middle * second_scale[:, None] * gain_two).astype(jnp.bfloat16)
        gate_part = jnp.dot(
            ffn_in, ffn_weights.reshape(width_rows, -1), preferred_element_type=jnp.float32
        ).reshape(length, 2, -1)
        gate_up = lax.psum_scatter(gate_part, "dmod", scatter_dimension=2, tiled=True)
        gate = gate_up[:, 0]
        upward = gate_up[:, 1]
        sigma = jax.nn.sigmoid(gate)
        active_low = (gate * sigma * upward).astype(jnp.bfloat16)
        active_keep = gather_features(active_low)
        down_sum = jnp.dot(active_keep, down_weights, preferred_element_type=jnp.float32)
        result = middle + sum_widths(down_sum)
        outputs.append(result.astype(jnp.bfloat16))
        backward_set = fetch_arranged()
        (
            norm_one,
            mix_weights,
            beta_weights,
            kernels,
            head_gain,
            out_weights,
            norm_two,
            ffn_weights,
            down_weights,
        ) = backward_set
        gain_one = norm_one.astype(jnp.float32)
        gain_two = norm_two.astype(jnp.float32)
        direction = cotangent[index, 0].astype(jnp.float32) * scales[index, 0][:, None]
        direction_low = direction.astype(jnp.bfloat16)
        down_grad = contract(active_keep, direction_low, 0, 0)
        active_grad = share_features(contract(direction_low, down_weights, 1, 1))
        gate_grad = active_grad * upward * sigma * (1.0 + gate * (1.0 - sigma))
        upward_grad = active_grad * gate * sigma
        gate_up_low = jnp.stack([gate_grad, upward_grad], 1).astype(jnp.bfloat16)
        gate_up_all = lax.all_gather(gate_up_low, "dmod", axis=2, tiled=True)
        gate_up_flat = gate_up_all.reshape(length, -1)
        ffn_part = contract(gate_up_flat, ffn_weights.reshape(width_rows, -1), 1, 1)
        ffn_grad = contract(ffn_in, gate_up_flat, 0, 0).reshape(width_rows, 2, -1)
        ffn_in_grad = sum_widths(ffn_part)
        weighted_two = ffn_in_grad * gain_two
        norm_two_grad = jnp.sum(ffn_in_grad * middle * second_scale[:, None], 0)
        inner_two = row_total(jnp.sum(weighted_two * middle, -1))
        middle_grad = (
            direction
            + second_scale[:, None] * weighted_two
            - middle * (second_scale**3 * inner_two / D)[:, None]
        )
        branch_low = middle_grad.astype(jnp.bfloat16)
        out_grad = contract(gated_keep, branch_low, 0, 0)
        gated_grad = share_features(contract(branch_low, out_weights, 1, 1))
        projected_grad, beta_grad, kernel_grad, head_grad = mixer_back(gated_grad)
        projected_all, beta_all = (
            lax.all_gather(projected_grad.astype(jnp.bfloat16), "dmod", axis=2, tiled=True),
            lax.all_gather(beta_grad.astype(jnp.bfloat16), "dmod", axis=1, tiled=True),
        )
        projected_flat = projected_all.reshape(length, -1)
        mixer_part = contract(projected_flat, mix_weights.reshape(width_rows, -1), 1, 1) + contract(
            beta_all, beta_weights, 1, 1
        )
        mix_grad = contract(mixer_in, projected_flat, 0, 0).reshape(width_rows, 4, -1)
        beta_weight_grad = contract(mixer_in, beta_all, 0, 0)
        mixer_grad, head_partial = (
            lax.psum(mixer_part.astype(jnp.bfloat16), "mp").astype(jnp.float32),
            lax.psum(head_grad.astype(jnp.bfloat16), "mp").astype(jnp.float32),
        )
        weighted_one = mixer_grad * gain_one
        norm_one_grad = jnp.sum(mixer_grad * rows * first_scale[:, None], 0)
        inner_one, head_total = row_total((jnp.sum(weighted_one * rows, -1), head_partial))
        input_grads.append(
            middle_grad
            + first_scale[:, None] * weighted_one
            - rows * (first_scale**3 * inner_one / D)[:, None]
        )
        pieces = (
            norm_one_grad,
            mix_grad,
            beta_weight_grad,
            kernel_grad,
            head_total,
            out_grad,
            norm_two_grad,
            ffn_grad,
            down_grad,
        )
        totals = (
            pieces
            if totals is None
            else tuple((left + right for left, right in zip(totals, pieces)))
        )
    summed = reduce_grads(totals)
    return (jnp.stack(outputs)[:, None], jnp.stack(input_grads)[:, None]) + tuple(summed)


def solution(mesh):
    placed = (
        P(None, "dp", None, "dmod"),
        P(None, "dp", None),
        P(None, "dp", None),
        P(),
        P(("dmod", "dp")),
        P(("dmod", "dp"), None, "mp"),
        P(("dmod", "dp"), "mp"),
        P(None, None, ("mp", "dmod", "dp")),
        P("dp"),
        P("mp", ("dmod", "dp")),
        P(("dmod", "dp")),
        P(("dmod", "dp"), None, "mp"),
        P("mp", ("dmod", "dp")),
        P(None, "dp", None, "dmod"),
    )
    return jax.shard_map(
        body,
        mesh=mesh,
        in_specs=placed,
        out_specs=(
            P(None, "dp", None, "dmod"),
            P(None, "dp", None, "dmod"),
            P(("dmod", "dp")),
            P(("dmod", "dp"), None, "mp"),
            P(("dmod", "dp"), "mp"),
            P(None, None, ("mp", "dmod", "dp")),
            P("dp"),
            P("mp", ("dmod", "dp")),
            P(("dmod", "dp")),
            P(("dmod", "dp"), None, "mp"),
            P("mp", ("dmod", "dp")),
        ),
        check_vma=False,
    )
```

profile of v0, /device:TPU:16, one launch (start us, length us, event | category | flops | bytes accessed | tf_op | source)
XLA Modules:
  0.0 1666.9 jit_solution(10881042022695400373)
XLA Ops:
  23.9 66.6 %all-gather.15.cloned.1.call-done = bf16[512,4,1024]{2,0,1:T(8,128)(2,1)} async-done(((bf16[128,4,1024]{2,0,1:T(8,128)(2,1)}), bf16[512,4,1024]{2,0,1:T(8,128)(2,1)}) %all-gather.15.cloned.1.call-update) | async-done | bytes 4194320 | tf_op jit(solution)/shard_map/all_gather | solution.py:125
  110.9 12.1 all_gather.41
  134.1 15.0 all_gather.40
  149.2 12.4 slice_reduce_fusion.3
  162.3 11.2 all-reduce.87
  181.5 13.0 reduce-scatter.23.cloned.1.call-done
  221.9 87.4 %while.85 = (s32[]{:T(128)}, f32[2,128,128]{2,1,0:T(8,128)S(1)}, s32[]{:T(128)}, f32[4,64,2,128]{3,1,2,0:T(8,128)}, f32[4,2,128,128]{3,2,1,0:T(8,128)}, /*index=...) while((s32[]{:T(128)}, f32[2,128,128]{2,1,0:T(8,128)S(1)}, ...), condition=%wide.region_21.23_spmd.clone, body=%wide.region_20.22_spmd.clone.sunk | while | flops 126222656 | bytes 2118885 | solution.py:60
  334.4 103.4 %while.84 = (s32[]{:T(128)}, f32[2,128,128]{2,1,0:T(8,128)S(1)}, s32[]{:T(128)}, f32[4,64,2,128]{3,1,2,0:T(8,128)S(1)}, f32[4,2,128,128]{3,2,1,0:T(8,128)}, /*in...) while((s32[]{:T(128)}, f32[2,128,128]{2,1,0:T(8,128)S(1)}, ...), condition=%wide.region_7.0_spmd.clone, body=%wide.region_6.8_spmd.clone.sunk | while | flops 126222656 | bytes 2080993 | solution.py:60
  340.9 11.2 custom-call.26
  366.7 11.2 custom-call.26
  392.6 11.2 custom-call.26
  418.4 11.2 custom-call.26
  542.6 57.5 %reduce-scatter.29.cloned.1.call-done = f32[256,2,704]{0,2,1:T(8,128)} async-done(((f32[256,2,2816]{0,2,1:T(8,128)}), f32[256,2,704]{0,2,1:T(8,128)}) %reduce-scatter.29.cloned.1.call-update) | async-done | bytes 1441808 | tf_op jit(solution)/shard_map/reduce_scatter | solution.py:268
  603.0 36.6 %reduce-scatter.31.cloned.1.call-done = f32[256,704]{0,1:T(8,128)} async-done(((f32[256,2816]{0,1:T(8,128)}), f32[256,704]{0,1:T(8,128)}) %reduce-scatter.31.cloned.1.call-update) | async-done | bytes 720912 | tf_op jit(solution)/shard_map/reduce_scatter | solution.py:108
  639.5 57.5 %reduce-scatter.25.cloned.1.call-done = f32[256,2,704]{0,2,1:T(8,128)} async-done(((f32[256,2,2816]{0,2,1:T(8,128)}), f32[256,2,704]{0,2,1:T(8,128)}) %reduce-scatter.25.cloned.1.call-update) | async-done | bytes 1441808 | tf_op jit(solution)/shard_map/reduce_scatter | solution.py:268
  704.0 13.4 all-gather.25.cloned.1.call-done
  721.4 16.6 all-gather.21.cloned.1.call-done
  742.0 25.2 %all-gather.27.cloned.1.call-done = bf16[256,2,2816]{0,2,1:T(8,128)(2,1)} async-done(((bf16[256,2,704]{0,2,1:T(8,128)(2,1)}), bf16[256,2,2816]{0,2,1:T(8,128)(2,1)}) %all-gather.27.cloned.1.call-update) | async-done | bytes 2883600 | tf_op jit(solution)/shard_map/all_gather | solution.py:298
  773.2 23.1 %all-gather.31.cloned.1.call-done = bf16[256,2,2816]{0,2,1:T(8,128)(2,1)} async-done(((bf16[256,2,704]{0,2,1:T(8,128)(2,1)}), bf16[256,2,2816]{0,2,1:T(8,128)(2,1)}) %all-gather.31.cloned.1.call-update) | async-done | bytes 2883600 | tf_op jit(solution)/shard_map/all_gather | solution.py:298
  802.4 63.6 %all-reduce.98.cloned.1.call-done = (f32[256,512]{1,0:T(8,128)}, f32[256,512]{1,0:T(8,128)}, f32[256,512]{1,0:T(8,128)}, f32[256,512]{1,0:T(8,128)}) async-done(((f32[256,512]{1,0:T(8,128)}, f32[256,512]{1,0:T(8,128)}, f32[256,512]{1,0:T(8,128)}, f32[256,512]{1,0:T(8,128)}), (f32[256,512]{1,0:T(8,128)}, f32[256,512]{1,0:T(8,128)}, f32[256,512]{1,0:T(8,128)}, ...) | async-done | bytes 2097168 | tf_op jit(solution)/shard_map/psum | solution.py:100
  889.7 15.5 reduce-scatter.37.cloned.1.call-done
  905.3 28.0 %reduce-scatter.33.cloned.1.call-done = f32[256,256]{1,0:T(8,128)} async-done(((f32[256,1024]{1,0:T(8,128)}), f32[256,256]{1,0:T(8,128)}) %reduce-scatter.33.cloned.1.call-update) | async-done | bytes 262160 | tf_op jit(solution)/shard_map/reduce_scatter | solution.py:108
  946.4 139.4 %while.86 = (s32[]{:T(128)}, f32[2,128,128]{2,1,0:T(8,128)}, f32[4,64,2,128]{3,1,2,0:T(8,128)}, f32[4,64,2,128]{3,1,2,0:T(8,128)}, f32[4,64,2,128]{3,2,1,0:T(2,1...) while((s32[]{:T(128)}, f32[2,128,128]{2,1,0:T(8,128)}, ...), condition=%wide.region_40.43_spmd.clone, body=%wide.region_37.42_spmd.clone.sunk | while | flops 321519808 | bytes 6251895 | solution.py:60
  958.7 10.6 custom-call.28
  1095.7 139.3 %while.87 = (s32[]{:T(128)}, f32[2,128,128]{2,1,0:T(8,128)}, f32[4,64,2,128]{3,1,2,0:T(8,128)}, f32[4,64,2,128]{3,1,2,0:T(8,128)}, f32[4,64,2,128]{3,2,1,0:T(2,1...) while((s32[]{:T(128)}, f32[2,128,128]{2,1,0:T(8,128)}, ...), condition=%wide.region_55.58_spmd.clone, body=%wide.region_52.57_spmd.clone.sunk | while | flops 321519808 | bytes 6251895 | solution.py:60
  1346.4 26.4 %reduce-scatter.49.cloned.1.call-done = bf16[128,2816]{1,0:T(8,128)(2,1)} async-done(((bf16[512,2816]{1,0:T(8,128)(2,1)}), bf16[128,2816]{1,0:T(8,128)(2,1)}) %reduce-scatter.49.cloned.1.call-update) | async-done | bytes 720912
  1375.5 25.4 %reduce-scatter.47.cloned.1.call-done = bf16[128,1024]{1,0:T(8,128)(2,1)} async-done(((bf16[512,1024]{1,0:T(8,128)(2,1)}), bf16[128,1024]{1,0:T(8,128)(2,1)}) %reduce-scatter.47.cloned.1.call-update) | async-done | bytes 262160
  1408.1 12.4 reduce-scatter.45.cloned.1.call-done
  1422.0 18.0 %reduce-scatter.43.cloned.1.call-done = bf16[128,8]{1,0:T(8,128)(2,1)} async-done(((bf16[512,8]{1,0:T(8,128)(2,1)}), bf16[128,8]{1,0:T(8,128)(2,1)}) %reduce-scatter.43.cloned.1.call-update) | async-done | bytes 2064
  1441.4 30.4 %all-reduce.102.cloned.1.call-done = (bf16[256,512]{1,0:T(8,128)(2,1)}, bf16[256,512]{1,0:T(8,128)(2,1)}) async-done(((bf16[256,512]{1,0:T(8,128)(2,1)}, bf16[256,512]{1,0:T(8,128)(2,1)}), (bf16[256,512]{1,0:T(8,128)(2,1)}, bf16[256,512]{1,0:T(8,128)(2,1)})) %all-reduce.102.cloned.1.call-update) | async-done | bytes 524304 | tf_op jit(solution)/shard_map/psum | solution.py:326
  1494.4 82.7 %reduce-scatter.41.cloned.1.call-done = bf16[128,2,2816]{2,0,1:T(8,128)(2,1)} async-done(((bf16[512,2,2816]{2,0,1:T(8,128)(2,1)}), bf16[128,2,2816]{2,0,1:T(8,128)(2,1)}) %reduce-scatter.41.cloned.1.call-update) | async-done | bytes 1441808 | tf_op jit(solution)/shard_map/reduce_scatter | solution.py:170
  1581.5 75.0 %reduce-scatter.39.cloned.1.call-done = bf16[128,4,1024]{2,0,1:T(8,128)(2,1)} async-done(((bf16[512,4,1024]{2,0,1:T(8,128)(2,1)}), bf16[128,4,1024]{2,0,1:T(8,128)(2,1)}) %reduce-scatter.39.cloned.1.call-update) | async-done | bytes 1048592 | tf_op jit(solution)/shard_map/reduce_scatter | solution.py:152
  (1183 shorter events, 846.4 us)
Async XLA Ops:
  7.2 83.4 %all-gather.15.cloned.1.call-start = ((), (), s32[]{:S(2)}) async-start(), calls=%async_computation.14 | async-start | bytes 5242880 | tf_op jit(solution)/shard_map/all_gather | solution.py:125
  9.8 166.6 %reduce-scatter.27.cloned.1.call-start = ((), (), s32[]{:S(2)}) async-start(), calls=%async_computation.21 | async-start | bytes 5242880 | tf_op jit(solution)/shard_map/reduce_scatter | solution.py:248
  102.4 92.0 %reduce-scatter.23.cloned.1.call-start = ((), (), s32[]{:S(2)}) async-start(), calls=%async_computation.15 | async-start | bytes 5242880 | tf_op jit(solution)/shard_map/reduce_scatter | solution.py:248
  108.0 349.5 %all-gather.17.cloned.1.call-start = ((), (), s32[]{:S(2)}) async-start(), calls=%async_computation.16 | async-start | bytes 1310720 | tf_op jit(solution)/shard_map/all_gather | solution.py:129
  108.6 363.4 %all-gather.23.cloned.1.call-start = ((), (), s32[]{:S(2)}) async-start(), calls=%async_computation.20 | async-start | bytes 3604480 | tf_op jit(solution)/shard_map/all_gather | solution.py:132
  109.2 376.1 %all-gather.19.cloned.1.call-start = ((), (), s32[]{:S(2)}) async-start(), calls=%async_computation.17 | async-start | bytes 7208960 | tf_op jit(solution)/shard_map/all_gather | solution.py:131
  110.7 392.8 %all-reduce.100.cloned.1.call-start = ((), (), s32[]{:S(2)}) async-start(), calls=%async_computation.39 | async-start | bytes 2097152 | tf_op jit(solution)/shard_map/psum | solution.py:100
  462.8 79.8 %reduce-scatter.35.cloned.1.call-start = ((), (), s32[]{:S(2)}) async-start(), calls=%async_computation.28 | async-start | bytes 3604480 | tf_op jit(solution)/shard_map/reduce_scatter | solution.py:108
  471.9 403.4 %copy-start.94 = (f32[1,256]{1,0:T(1,128)}, f32[1,256]{1,0:T(1,128)S(1)}, u32[]{:S(2)}) copy-start(f32[1,256]{1,0:T(1,128)S(1)} %get-tuple-element.1688) | copy-start | bytes 3076
  471.9 403.4 %copy-start.100 = (f32[1,256]{1,0:T(1,128)}, f32[1,256]{1,0:T(1,128)S(1)}, u32[]{:S(2)}) copy-start(f32[1,256]{1,0:T(1,128)S(1)} %get-tuple-element.1687) | copy-start | bytes 3076
  476.5 123.6 %reduce-scatter.29.cloned.1.call-start = ((), (), s32[]{:S(2)}) async-start(), calls=%async_computation.22 | async-start | bytes 7208960 | tf_op jit(solution)/shard_map/reduce_scatter | solution.py:268
  485.3 390.0 %copy-start.60 = (f32[4,1,128]{2,1,0:T(1,128)}, f32[4,1,128]{2,1,0:T(1,128)S(1)}, u32[]{:S(2)}) copy-start(f32[4,1,128]{2,1,0:T(1,128)S(1)} %convert_element_type.424) | copy-start | bytes 6148
  512.7 362.7 %copy-start.68 = (f32[256]{0:T(256)}, f32[256]{0:T(256)S(1)}, u32[]{:S(2)}) copy-start(f32[256]{0:T(256)S(1)} %add_rsqrt_fusion.4) | copy-start | bytes 3076
  520.6 119.0 %reduce-scatter.31.cloned.1.call-start = ((), (), s32[]{:S(2)}) async-start(), calls=%async_computation.24 | async-start | bytes 3604480 | tf_op jit(solution)/shard_map/reduce_scatter | solution.py:108
  525.1 171.8 %reduce-scatter.25.cloned.1.call-start = ((), (), s32[]{:S(2)}) async-start(), calls=%async_computation.18 | async-start | bytes 7208960 | tf_op jit(solution)/shard_map/reduce_scatter | solution.py:268
  525.2 350.2 %copy-start.70 = (f32[256]{0:T(256)}, f32[256]{0:T(256)S(1)}, u32[]{:S(2)}) copy-start(f32[256]{0:T(256)S(1)} %add_rsqrt_fusion.6) | copy-start | bytes 3076
  532.3 185.2 %all-gather.25.cloned.1.call-start = ((), (), s32[]{:S(2)}) async-start(), calls=%async_computation.23 | async-start | bytes 1802240 | tf_op jit(solution)/shard_map/all_gather | solution.py:104
  602.9 135.1 %all-gather.21.cloned.1.call-start = ((), (), s32[]{:S(2)}) async-start(), calls=%async_computation.19 | async-start | bytes 1802240 | tf_op jit(solution)/shard_map/all_gather | solution.py:104
  699.9 67.3 %all-gather.27.cloned.1.call-start = ((), (), s32[]{:S(2)}) async-start(), calls=%async_computation.25 | async-start | bytes 3604480 | tf_op jit(solution)/shard_map/all_gather | solution.py:298
  702.0 94.4 %all-gather.31.cloned.1.call-start = ((), (), s32[]{:S(2)}) async-start(), calls=%async_computation.29 | async-start | bytes 3604480 | tf_op jit(solution)/shard_map/all_gather | solution.py:298
  704.0 162.1 %all-reduce.98.cloned.1.call-start = ((), (), s32[]{:S(2)}) async-start(), calls=%async_computation.38 | async-start | bytes 4194304 | tf_op jit(solution)/shard_map/psum | solution.py:100
  802.4 102.9 %reduce-scatter.37.cloned.1.call-start = ((), (), s32[]{:S(2)}) async-start(), calls=%async_computation.30 | async-start | bytes 1310720 | tf_op jit(solution)/shard_map/reduce_scatter | solution.py:108
  881.1 52.2 %reduce-scatter.33.cloned.1.call-start = ((), (), s32[]{:S(2)}) async-start(), calls=%async_computation.26 | async-start | bytes 1310720 | tf_op jit(solution)/shard_map/reduce_scatter | solution.py:108
  884.0 421.3 %all-gather.33.cloned.1.call-start = ((), (), s32[]{:S(2)}) async-start(), calls=%async_computation.31 | async-start | bytes 2621440 | tf_op jit(solution)/shard_map/all_gather | solution.py:316
  1266.6 47.9 %all-gather.29.cloned.1.call-start = ((), (), s32[]{:S(2)}) async-start(), calls=%async_computation.27 | async-start | bytes 2621440 | tf_op jit(solution)/shard_map/all_gather | solution.py:316
  1268.6 104.2 %reduce-scatter.49.cloned.1.call-start = ((), (), s32[]{:S(2)}) async-start(), calls=%async_computation.37 | async-start | bytes 3604480
  1277.3 123.6 %reduce-scatter.47.cloned.1.call-start = ((), (), s32[]{:S(2)}) async-start(), calls=%async_computation.36 | async-start | bytes 1310720
  1282.8 137.7 %reduce-scatter.45.cloned.1.call-start = ((), (), s32[]{:S(2)}) async-start(), calls=%async_computation.35 | async-start | bytes 81920
  1304.1 135.9 %reduce-scatter.43.cloned.1.call-start = ((), (), s32[]{:S(2)}) async-start(), calls=%async_computation.34 | async-start | bytes 163840
  1305.3 166.6 %all-reduce.102.cloned.1.call-start = ((), (), s32[]{:S(2)}) async-start(), calls=%async_computation.40 | async-start | bytes 1048576 | tf_op jit(solution)/shard_map/psum | solution.py:326
  1319.5 257.5 %reduce-scatter.41.cloned.1.call-start = ((), (), s32[]{:S(2)}) async-start(), calls=%async_computation.33 | async-start | bytes 7208960 | tf_op jit(solution)/shard_map/reduce_scatter | solution.py:170
  1329.6 326.9 %reduce-scatter.39.cloned.1.call-start = ((), (), s32[]{:S(2)}) async-start(), calls=%async_computation.32 | async-start | bytes 5242880 | tf_op jit(solution)/shard_map/reduce_scatter | solution.py:152
  (191 other events, 3446.5 us)
Sparse Core Ops, SparseCore 0:
  10.2 80.3 all-gather.14
  102.5 44.4 reduce-scatter.26
  149.7 44.6 reduce-scatter.22
  195.9 27.5 all-gather.16
  224.8 58.6 all-gather.22
  285.5 104.9 all-gather.18
  462.9 40.5 all-reduce.99
  506.2 36.3 reduce-scatter.34
  545.1 54.8 reduce-scatter.28
  603.2 36.3 reduce-scatter.30
  642.1 54.8 reduce-scatter.24
  698.5 18.9 all-gather.24
  719.1 18.9 all-gather.20
  740.1 27.0 all-gather.26
  769.2 27.0 all-gather.30
  802.5 63.4 all-reduce.97
  881.2 23.9 reduce-scatter.36
  908.4 24.8 reduce-scatter.32
  1266.7 22.8 all-gather.32
  1291.5 22.8 all-gather.28
  1316.7 56.0 reduce-scatter.48
  1375.1 25.7 reduce-scatter.46
  1403.2 17.2 reduce-scatter.44
  1422.6 17.3 reduce-scatter.42
  1443.1 28.7 all-reduce.101
  1474.0 102.9 reduce-scatter.40
  1579.2 77.2 reduce-scatter.38
where the time goes:
time: 1680 us; the launch traced here: 1670 us
  waiting for transfers between devices  712 us (42%)
  other arithmetic  287 us (17%)
  matrix products  260 us (15%)
  local copies, waits for them, and re-layouts  240 us (14%)
  blocking collectives  138 us (8%)
  between operations  19.6 us (1%)
    another operation x64, other arithmetic, delta_block(): update = solver(system, target)  176 us
    reduce_scatter x2, waiting for transfers between devices, body(): lax.psum_scatter(gate_part, 'dmod', scatter_dimension=2, tiled=True)  115 us
    reduce_scatter x4, waiting for transfers between devices, share_features(): return lax.psum_scatter(values, 'dmod', scatter_dimension=1, tiled=True)  90.4 us
    unnamed x31, waiting for transfers between devices  83.7 us
    reduce_scatter x1, waiting for transfers between devices, reduce_grads(): lax.psum_scatter(grad_ffn.astype(jnp.bfloat16), 'dp', scatter_dimension=0...  82.7 us
    reduce_scatter x1, waiting for transfers between devices, reduce_grads(): lax.psum_scatter(grad_mix.astype(jnp.bfloat16), 'dp', scatter_dimension=0...  75 us
    psum x2, waiting for transfers between devices, sum_widths(): return lax.psum(values, 'mp')  73.3 us
    all_gather x1, waiting for transfers between devices, fetch_block(): lax.all_gather(mix_weights, 'dp', axis=0, tiled=True)  66.6 us
  transfers between devices with their start and end apart: 27, of which 22 were waited for; matrix products, arithmetic and copies ran while one was open for 25% of the time, Pallas kernels for 0%

commit v1 on v0

v1 whole, which is shorter than its diff:
```python
import jax
import jax.numpy as jnp
from jax import lax
from jax.experimental import pallas as pl
from jax.experimental.pallas import tpu as pltpu
from jax.sharding import PartitionSpec as P

D = 2048
HEAD = 128
LOW = jnp.bfloat16
WIDE = jnp.float32
LONGEST_RING = 1
CORE = [(i, i ^ 1) for i in range(4)]
ACROSS = [(i, i ^ 2) for i in range(4)]
SWAP = [(0, 1), (1, 0)]


def halves(values):
    high = values.astype(LOW)
    return high, (values - high.astype(WIDE)).astype(LOW)


def product(left, right, left_dim, right_dim):
    def one(a, b):
        return lax.dot_general(
            a, b, (((left_dim,), (right_dim,)), ((), ())), preferred_element_type=WIDE
        )

    return one(left[0], right[0]) + (one(left[0], right[1]) + one(left[1], right[0]))


def sigmoid(values):
    return 1.0 / (1.0 + jnp.exp(-values))


def masks_of(seg_col, seg_row):
    length = seg_col.shape[0]
    rows = lax.broadcasted_iota(jnp.int32, (length, length), 0)
    cols = lax.broadcasted_iota(jnp.int32, (length, length), 1)
    same = seg_col == seg_row
    return rows, cols, same & (cols < rows), same & (cols <= rows)


def kept_of(seg_col, taps):
    length = seg_col.shape[0]
    wide = jnp.broadcast_to(seg_col, (length, HEAD))
    place = lax.broadcasted_iota(jnp.int32, (length, HEAD), 0)
    return [
        ((pltpu.roll(wide, shift, 0) == wide) & (place >= shift)).astype(WIDE)
        for shift in range(1, taps)
    ]


def convolve(signal, kernel, kept):
    taps = kernel.shape[0]
    total = signal * kernel[taps - 1 : taps]
    for shift in range(1, taps):
        moved = pltpu.roll(signal, shift, 0) * kept[shift - 1]
        total = total + moved * kernel[taps - 1 - shift : taps - shift]
    return total


def invert(lower, rows, cols):
    length = lower.shape[0]
    eye = (rows == cols).astype(WIDE)
    base = -jnp.where((rows // 8) == (cols // 8), lower, 0.0)
    parts = halves(base)
    second = product(parts, parts, 1, 0)
    second_parts = halves(second)
    third = product(parts, second_parts, 1, 0)
    fourth = product(second_parts, second_parts, 1, 0)
    inverse = eye + base + second + third
    inverse = inverse + product(halves(inverse), halves(fourth), 1, 0)
    size = 8
    while size < length:
        cross = ((rows // (2 * size)) == (cols // (2 * size))) & ((rows // size) != (cols // size))
        off = halves(jnp.where(cross, lower, 0.0))
        own = halves(inverse)
        inverse = inverse - product(halves(product(own, off, 1, 0)), own, 1, 0)
        size *= 2
    return inverse


def mixer_forward_kernel(
    first_ref, second_ref, beta_ref, col_ref, row_ref, conv_ref, head_ref,
    gated_ref, inverse_ref, update_ref, mixed_ref,
):
    seg_col = col_ref[...]
    rows, cols, strict, inclusive = masks_of(seg_col, row_ref[0])
    taps = conv_ref.shape[0] // 3
    kept = kept_of(seg_col, taps)
    heads = gated_ref.shape[1] // HEAD
    span = heads * HEAD
    gain = head_ref[...]
    for head in range(heads):
        own = slice(head * HEAD, (head + 1) * HEAD)
        past = slice(span + head * HEAD, span + (head + 1) * HEAD)
        signals = [first_ref[:, own], first_ref[:, past], second_ref[:, own]]
        convolved = []
        for part in range(3):
            pre = convolve(signals[part], conv_ref[part * taps : (part + 1) * taps, own], kept)
            convolved.append(pre * sigmoid(pre))
        query = convolved[0] * (
            lax.rsqrt(jnp.sum(convolved[0] * convolved[0], 1, keepdims=True) + 1e-06) * HEAD**-0.5
        )
        key = convolved[1] * lax.rsqrt(
            jnp.sum(convolved[1] * convolved[1], 1, keepdims=True) + 1e-06
        )
        beta = sigmoid(beta_ref[:, head : head + 1])
        key_parts = halves(key)
        gram = product(key_parts, key_parts, 1, 1)
        inverse = invert(jnp.where(strict, gram * beta, 0.0), rows, cols)
        update = product(halves(inverse), halves(convolved[2] * beta), 1, 0)
        scores = jnp.where(inclusive, product(halves(query), key_parts, 1, 1), 0.0)
        mixed = product(halves(scores), halves(update), 1, 0)
        scale = lax.rsqrt(jnp.sum(mixed * mixed, 1, keepdims=True) * (1.0 / HEAD) + 1e-05)
        gate = second_ref[:, past]
        gated_ref[:, own] = (mixed * scale * gain * (gate * sigmoid(gate))).astype(LOW)
        inverse_ref[0, head] = inverse
        update_ref[:, own] = update
        mixed_ref[:, own] = mixed


def mixer_backward_kernel(
    first_ref, second_ref, beta_ref, col_ref, row_ref, conv_ref, head_ref,
    inverse_ref, update_ref, mixed_ref, grad_ref,
    out_ref, beta_grad_ref, conv_grad_ref, head_grad_ref,
):
    seg_col = col_ref[...]
    rows, cols, strict, inclusive = masks_of(seg_col, row_ref[0])
    length = seg_col.shape[0]
    taps = conv_ref.shape[0] // 3
    kept = kept_of(seg_col, taps)
    heads = grad_ref.shape[1] // HEAD
    span = heads * HEAD
    gain = head_ref[...]
    head_grad = jnp.zeros((1, HEAD), WIDE)
    for head in range(heads):
        own = slice(head * HEAD, (head + 1) * HEAD)
        past = slice(span + head * HEAD, span + (head + 1) * HEAD)
        signals = [first_ref[:, own], first_ref[:, past], second_ref[:, own]]
        before, gates, convolved = [], [], []
        for part in range(3):
            pre = convolve(signals[part], conv_ref[part * taps : (part + 1) * taps, own], kept)
            before.append(pre)
            gates.append(sigmoid(pre))
            convolved.append(pre * gates[part])
        query_unit = lax.rsqrt(jnp.sum(convolved[0] * convolved[0], 1, keepdims=True) + 1e-06)
        key_unit = lax.rsqrt(jnp.sum(convolved[1] * convolved[1], 1, keepdims=True) + 1e-06)
        query = convolved[0] * (query_unit * HEAD**-0.5)
        key = convolved[1] * key_unit
        beta = sigmoid(beta_ref[:, head : head + 1])
        mixed = mixed_ref[:, own]
        update = update_ref[:, own]
        grad = grad_ref[:, own]
        gate = second_ref[:, past]
        gate_sigma = sigmoid(gate)
        opened = gate * gate_sigma
        scale = lax.rsqrt(jnp.sum(mixed * mixed, 1, keepdims=True) * (1.0 / HEAD) + 1e-05)
        normed = mixed * scale
        head_grad = head_grad + jnp.sum(grad * opened * normed, 0, keepdims=True)
        inner = grad * opened * gain
        mixed_grad = scale * inner - mixed * (
            scale * scale * scale * (jnp.sum(inner * mixed, 1, keepdims=True) * (1.0 / HEAD))
        )
        gate_grad = grad * normed * gain * gate_sigma * (1.0 + gate * (1.0 - gate_sigma))
        key_parts = halves(key)
        query_parts = halves(query)
        update_parts = halves(update)
        mixed_parts = halves(mixed_grad)
        gram = product(key_parts, key_parts, 1, 1)
        scores = jnp.where(inclusive, product(query_parts, key_parts, 1, 1), 0.0)
        scores_grad = halves(jnp.where(inclusive, product(mixed_parts, update_parts, 1, 1), 0.0))
        update_grad = product(halves(scores), mixed_parts, 0, 0)
        solved = product(halves(inverse_ref[0, head]), halves(update_grad), 0, 0)
        system_grad = jnp.where(strict, -product(halves(solved), update_parts, 1, 1), 0.0)
        gram_grad = halves(system_grad * beta)
        query_grad = product(scores_grad, key_parts, 1, 0)
        key_grad = (
            product(scores_grad, query_parts, 0, 0)
            + product(gram_grad, key_parts, 1, 0)
            + product(gram_grad, key_parts, 0, 0)
        )
        beta_grad = jnp.sum(system_grad * gram, 1, keepdims=True) + jnp.sum(
            solved * convolved[2], 1, keepdims=True
        )
        beta_grad_ref[:, head : head + 1] = beta_grad * beta * (1.0 - beta)
        conv_grads = [
            HEAD**-0.5
            * (
                query_grad * query_unit
                - convolved[0]
                * (
                    query_unit * query_unit * query_unit
                    * jnp.sum(convolved[0] * query_grad, 1, keepdims=True)
                )
            ),
            key_grad * key_unit
            - convolved[1]
            * (
                key_unit * key_unit * key_unit
                * jnp.sum(convolved[1] * key_grad, 1, keepdims=True)
            ),
            solved * beta,
        ]
        for part in range(3):
            sigma = gates[part]
            error = conv_grads[part] * sigma * (1.0 + before[part] * (1.0 - sigma))
            kernel = conv_ref[part * taps : (part + 1) * taps, own]
            total = error * kernel[taps - 1 : taps]
            line = part * taps + taps - 1
            conv_grad_ref[0, line : line + 1, own] = jnp.sum(
                error * signals[part], 0, keepdims=True
            )
            for shift in range(1, taps):
                held = error * kept[shift - 1]
                line = part * taps + taps - 1 - shift
                conv_grad_ref[0, line : line + 1, own] = jnp.sum(
                    held * pltpu.roll(signals[part], shift, 0), 0, keepdims=True
                )
                total = total + pltpu.roll(held, length - shift, 0) * (
                    kernel[taps - 1 - shift : taps - shift]
                )
            start = part * span + head * HEAD
            out_ref[:, start : start + HEAD] = total.astype(LOW)
        start = 3 * span + head * HEAD
        out_ref[:, start : start + HEAD] = gate_grad.astype(LOW)
    head_grad_ref[0] = head_grad


def mixer_specs(length, span, lines):
    return [
        pl.BlockSpec((length, 2 * span), lambda i: (i, 0)),
        pl.BlockSpec((length, 2 * span), lambda i: (i, 0)),
        pl.BlockSpec((length, span // HEAD), lambda i: (i, 0)),
        pl.BlockSpec((length, 1), lambda i: (i, 0)),
        pl.BlockSpec((1, 1, length), lambda i: (i, 0, 0)),
        pl.BlockSpec((lines, span), lambda i: (0, 0)),
        pl.BlockSpec((1, HEAD), lambda i: (0, 0)),
    ]


def mixer_forward(first, second, beta_in, seg_col, seg_row, conv, head_gain):
    tokens = first.shape[0]
    count, _, length = seg_row.shape
    span = conv.shape[1]
    heads = span // HEAD
    return pl.pallas_call(
        mixer_forward_kernel,
        grid=(count,),
        in_specs=mixer_specs(length, span, conv.shape[0]),
        out_specs=[
            pl.BlockSpec((length, span), lambda i: (i, 0)),
            pl.BlockSpec((1, heads, length, length), lambda i: (i, 0, 0, 0)),
            pl.BlockSpec((length, span), lambda i: (i, 0)),
            pl.BlockSpec((length, span), lambda i: (i, 0)),
        ],
        out_shape=[
            jax.ShapeDtypeStruct((tokens, span), LOW),
            jax.ShapeDtypeStruct((count, heads, length, length), WIDE),
            jax.ShapeDtypeStruct((tokens, span), WIDE),
            jax.ShapeDtypeStruct((tokens, span), WIDE),
        ],
        compiler_params=pltpu.CompilerParams(vmem_limit_bytes=32 << 20),
        cost_estimate=pl.CostEstimate(
            flops=count * heads * 100 * length**3, bytes_accessed=8 << 20, transcendentals=0
        ),
        name="mixer_forward",
    )(first, second, beta_in, seg_col, seg_row, conv, head_gain)


def mixer_backward(first, second, beta_in, seg_col, seg_row, conv, head_gain, saved, grad):
    tokens = first.shape[0]
    count, _, length = seg_row.shape
    lines, span = conv.shape
    heads = span // HEAD
    return pl.pallas_call(
        mixer_backward_kernel,
        grid=(count,),
        in_specs=mixer_specs(length, span, lines)
        + [
            pl.BlockSpec((1, heads, length, length), lambda i: (i, 0, 0, 0)),
            pl.BlockSpec((length, span), lambda i: (i, 0)),
            pl.BlockSpec((length, span), lambda i: (i, 0)),
            pl.BlockSpec((length, span), lambda i: (i, 0)),
        ],
        out_specs=[
            pl.BlockSpec((length, 4 * span), lambda i: (i, 0)),
            pl.BlockSpec((length, heads), lambda i: (i, 0)),
            pl.BlockSpec((1, lines, span), lambda i: (i, 0, 0)),
            pl.BlockSpec((1, 1, HEAD), lambda i: (i, 0, 0)),
        ],
        out_shape=[
            jax.ShapeDtypeStruct((tokens, 4 * span), LOW),
            jax.ShapeDtypeStruct((tokens, heads), WIDE),
            jax.ShapeDtypeStruct((count, lines, span), WIDE),
            jax.ShapeDtypeStruct((count, 1, HEAD), WIDE),
        ],
        compiler_params=pltpu.CompilerParams(vmem_limit_bytes=32 << 20),
        cost_estimate=pl.CostEstimate(
            flops=count * heads * 100 * length**3, bytes_accessed=8 << 20, transcendentals=0
        ),
        name="mixer_backward",
    )(first, second, beta_in, seg_col, seg_row, conv, head_gain, *saved, grad)


def contract(left, right, left_dim, right_dim):
    return lax.dot_general(
        left, right, (((left_dim,), (right_dim,)), ((), ())), preferred_element_type=WIDE
    )


def after(values, earlier):
    return lax.optimization_barrier((values, earlier))[0]


def exclusive_order(blocks):
    place = lax.axis_index("dmod")
    for bit in (1, 2):
        flip = (place & bit) != 0
        blocks = [jnp.where(flip, blocks[i ^ bit], blocks[i]) for i in range(4)]
    return blocks


def trade(blocks):
    return [blocks[0]] + [
        lax.ppermute(blocks[m], "dmod", [(i, i ^ m) for i in range(4)]) for m in (1, 2, 3)
    ]


def gather_width(values):
    far = lax.ppermute(values, "dmod", ACROSS)
    near = lax.ppermute(values, "dmod", CORE)
    return [values, near, far, lax.ppermute(far, "dmod", CORE)]


def scatter_width(blocks):
    near = lax.ppermute(blocks[1].astype(LOW), "dmod", CORE)
    cross = lax.ppermute(blocks[3].astype(LOW), "dmod", CORE)
    far = lax.ppermute((blocks[2] + cross.astype(WIDE)).astype(LOW), "dmod", ACROSS)
    return blocks[0] + near.astype(WIDE) + far.astype(WIDE)


def sum_pair(values):
    low = values.astype(LOW)
    return low.astype(WIDE) + lax.ppermute(low, "mp", SWAP).astype(WIDE)


def row_total(values):
    return lax.psum(values, "dmod")


class Ring:
    def __init__(self):
        self.size = lax.axis_size("dp")
        self.short = self.size <= LONGEST_RING
        self.parts = self.size if self.short else 1
        self.steps = [(i, (i + 1) % self.size) for i in range(self.size)]

    def order(self, values):
        if not self.short:
            return values
        place = lax.axis_index("dp")
        blocks = jnp.split(values, self.size, axis=-1)
        blocks = [blocks[-k % self.size] for k in range(self.size)]
        bit = 1
        while bit < self.size:
            turn = (place & bit) != 0
            blocks = [
                jnp.where(turn, blocks[(k - bit) % self.size], blocks[k]) for k in range(self.size)
            ]
            bit *= 2
        return jnp.concatenate(blocks, -1)

    def gather(self, values):
        if not self.short:
            return [lax.all_gather(values, "dp", axis=1, tiled=True)]
        parts = [values]
        for _ in range(self.size - 1):
            parts.append(lax.ppermute(parts[-1], "dp", self.steps))
        return parts

    def scatter(self, make):
        if not self.short:
            return lax.psum_scatter(
                make(0).astype(LOW), "dp", scatter_dimension=1, tiled=True
            ).astype(WIDE)
        total = make(1)
        for k in range(2, self.size + 1):
            total = lax.ppermute(total.astype(LOW), "dp", self.steps).astype(WIDE) + make(
                k % self.size
            )
        return total


def body(
    block_input,
    segment_ids,
    group_ids,
    group_weight,
    mixer_norm,
    w_mix,
    w_beta,
    conv_kernel,
    head_norm,
    w_out,
    ffn_norm,
    w_ffn_in,
    w_ffn_down,
    cotangent,
):
    ring = Ring()
    parts = ring.parts
    micro, seqs, length, width = block_input.shape
    tokens = micro * seqs * length
    block = width // parts
    strip = w_mix.shape[0]
    span = w_mix.shape[2] // 4
    hidden = w_ffn_in.shape[2] // 4
    dmod = lax.axis_index("dmod")
    data_size = ring.size
    place = lax.axis_index("dp")

    lines = conv_kernel.shape[0] * conv_kernel.shape[1]
    pack = jnp.concatenate(
        [
            conv_kernel.reshape(-1),
            head_norm,
            mixer_norm,
            ffn_norm,
            w_beta.T.reshape(-1),
        ]
    )
    packs = lax.all_gather(pack, "dp", axis=0)
    sizes = [conv_kernel.size, head_norm.size, strip, strip, w_beta.size]
    cuts = [sum(sizes[:i]) for i in range(6)]
    conv = (
        packs[:, cuts[0] : cuts[1]]
        .reshape(data_size, lines, -1)
        .transpose(1, 0, 2)
        .reshape(lines, span)
        .astype(WIDE)
    )
    head_gain = packs[:, cuts[1] : cuts[2]].reshape(1, -1).astype(WIDE)
    gain_one = ring.order(packs[:, cuts[2] : cuts[3]].reshape(1, -1).astype(WIDE))
    gain_two = ring.order(packs[:, cuts[3] : cuts[4]].reshape(1, -1).astype(WIDE))
    beta_weights = ring.order(
        packs[:, cuts[4] : cuts[5]]
        .reshape(data_size, -1, strip)
        .transpose(1, 0, 2)
        .reshape(-1, width)
    )

    out_rows = jnp.concatenate(exclusive_order(jnp.split(w_out, 4, axis=0)), 0)
    out_halves = jnp.split(out_rows.T, 2, axis=1)
    mix_own = jnp.stack(trade(exclusive_order(jnp.split(w_mix, 4, axis=2))))
    mix_halves = [
        mix_own[:, :, :2].reshape(4, strip, 2 * span),
        mix_own[:, :, 2:].reshape(4, strip, 2 * span),
    ]
    ffn_own = jnp.stack(trade(exclusive_order(jnp.split(w_ffn_in, 4, axis=2))))
    ffn_halves = [ffn_own[:, :, 0], ffn_own[:, :, 1]]
    down_own = trade(exclusive_order(jnp.split(w_ffn_down, 4, axis=0)))
    down_halves = [
        jnp.stack([down_own[0].T, down_own[1].T]),
        jnp.stack([down_own[2].T, down_own[3].T]),
    ]

    def chain(half):
        first = ring.gather(out_halves[half][None])
        second = ring.gather(after(mix_halves[half], first[-1]))
        third = ring.gather(after(ffn_halves[half], second[-1]))
        fourth = ring.gather(after(down_halves[half], third[-1]))
        return first, second, third, fourth

    chains = [chain(0), chain(1)]
    out_weights = jnp.concatenate(
        [
            jnp.concatenate([part[0] for part in chains[0][0]], 0),
            jnp.concatenate([part[0] for part in chains[1][0]], 0),
        ],
        1,
    )
    mix_parts = [[part.reshape(4 * block, -1) for part in each[1]] for each in chains]
    ffn_parts = [[part.reshape(4 * block, -1) for part in each[2]] for each in chains]
    down_parts = [[part.reshape(2 * block, -1) for part in each[3]] for each in chains]

    marks = (group_ids.reshape(tokens, 1) == jnp.arange(group_weight.shape[0])[None]).astype(WIDE)
    counts = lax.psum(jnp.sum(marks, 0), "dp")
    table = group_weight * (tokens * data_size / group_weight.shape[0]) / counts
    scales = jnp.sum(marks * table, -1, keepdims=True)
    direction = ring.order(cotangent.reshape(tokens, width).astype(WIDE)) * scales
    direction_low = direction.astype(LOW)

    def by_part(slots):
        return [
            jnp.concatenate([slot[:, k * block : (k + 1) * block] for slot in slots], 1)
            for k in range(parts)
        ]

    def by_slot(pieces):
        return [
            jnp.concatenate([piece[:, m * block : (m + 1) * block] for piece in pieces], 1)
            for m in range(pieces[0].shape[1] // block)
        ]

    direction_parts = by_part(gather_width(direction_low))

    rows = ring.order(block_input.reshape(tokens, width).astype(WIDE))
    first_scale = lax.rsqrt(row_total(jnp.sum(rows * rows, -1, keepdims=True)) / D + 1e-06)
    mixer_in = (rows * first_scale * gain_one).astype(LOW)
    mixer_parts = by_part(gather_width(mixer_in))
    projected = [
        sum(jnp.dot(mixer_parts[k], mix_parts[half][k], preferred_element_type=WIDE) for k in range(parts))
        for half in (0, 1)
    ]
    beta_all = row_total(contract(beta_weights, mixer_in, 1, 1))
    heads = span // HEAD
    beta_in = lax.dynamic_slice_in_dim(beta_all, dmod * heads, heads, 0).T
    seg_col = segment_ids.reshape(tokens, 1)
    seg_row = segment_ids.reshape(micro * seqs, 1, length)
    mixer_args = (projected[0], projected[1], beta_in, seg_col, seg_row, conv, head_gain)
    gated, *saved = mixer_forward(*mixer_args)
    gated_all = jnp.concatenate(gather_width(gated), 1)
    middle = rows + sum_pair(contract(gated_all, out_weights, 1, 1))

    second_scale = lax.rsqrt(row_total(jnp.sum(middle * middle, -1, keepdims=True)) / D + 1e-06)
    ffn_in = (middle * second_scale * gain_two).astype(LOW)
    ffn_in_parts = by_part(gather_width(ffn_in))
    gate, upward = (
        sum(jnp.dot(ffn_in_parts[k], ffn_parts[half][k], preferred_element_type=WIDE) for k in range(parts))
        for half in (0, 1)
    )
    sigma = sigmoid(gate)
    active = (gate * sigma * upward).astype(LOW)
    down_slots = sum(
        (
            by_slot([contract(active, down_parts[half][k], 1, 1) for k in range(parts)])
            for half in (0, 1)
        ),
        [],
    )
    result = middle + sum_pair(scatter_width(down_slots))
    out = ring.order(result).astype(LOW).reshape(block_input.shape)

    down_grads = [
        ring.scatter(
            lambda k: contract(
                direction_parts[k][:, 2 * half * block : 2 * (half + 1) * block], active, 0, 0
            ).reshape(2, block, hidden)
        )
        for half in (0, 1)
    ]
    active_grad = sum(
        jnp.dot(
            direction_parts[k][:, 2 * half * block : 2 * (half + 1) * block],
            down_parts[half][k],
            preferred_element_type=WIDE,
        )
        for k in range(parts)
        for half in (0, 1)
    )
    gate_grad = (active_grad * upward * sigma * (1.0 + gate * (1.0 - sigma))).astype(LOW)
    upward_grad = (active_grad * gate * sigma).astype(LOW)
    ffn_slots = by_slot(
        [
            contract(gate_grad, ffn_parts[0][k], 1, 1) + contract(upward_grad, ffn_parts[1][k], 1, 1)
            for k in range(parts)
        ]
    )
    ffn_grads = [
        ring.scatter(lambda k: contract(ffn_in_parts[k], grad, 0, 0).reshape(4, block, hidden))
        for grad in (gate_grad, upward_grad)
    ]
    ffn_in_grad = sum_pair(scatter_width(ffn_slots))
    weighted_two = ffn_in_grad * gain_two
    norm_two_grad = jnp.sum(ffn_in_grad * middle * second_scale, 0)
    inner_two = row_total(jnp.sum(weighted_two * middle, -1, keepdims=True))
    middle_grad = (
        direction + second_scale * weighted_two - middle * (second_scale**3 * inner_two / D)
    )

    branch_low = middle_grad.astype(LOW)
    out_grads = [
        ring.scatter(
            lambda k: contract(
                branch_low[:, k * block : (k + 1) * block],
                gated_all[:, 2 * half * span : 2 * (half + 1) * span],
                0,
                0,
            )[None]
        )
        for half in (0, 1)
    ]
    gated_slots = jnp.split(jnp.dot(branch_low, out_weights, preferred_element_type=WIDE), 4, axis=1)
    gated_grad = scatter_width(gated_slots)
    projected_grad, beta_grad, conv_grad, head_grad = mixer_backward(
        *mixer_args, saved, gated_grad
    )
    projected_slots = gather_width(projected_grad)
    mix_grads = [
        ring.scatter(
            lambda k: contract(
                mixer_in[:, k * block : (k + 1) * block],
                jnp.concatenate(projected_slots[2 * half : 2 * half + 2], 1),
                0,
                0,
            )[None]
        )
        for half in (0, 1)
    ]
    beta_slots = jnp.concatenate(
        exclusive_order(gather_width(beta_grad.T.astype(LOW))), 0
    )
    beta_weight_grad = contract(beta_slots, mixer_in, 1, 0)
    mixer_slots = by_slot(
        [
            contract(projected_grad[:, : 2 * span], mix_parts[0][k], 1, 1)
            + contract(projected_grad[:, 2 * span :], mix_parts[1][k], 1, 1)
            for k in range(parts)
        ]
    )
    mixer_grad = sum_pair(scatter_width(mixer_slots) + contract(beta_slots, beta_weights, 0, 0))
    weighted_one = mixer_grad * gain_one
    norm_one_grad = jnp.sum(mixer_grad * rows * first_scale, 0)
    inner_one = row_total(jnp.sum(weighted_one * rows, -1, keepdims=True))
    grad_input = ring.order(
        middle_grad + first_scale * weighted_one - rows * (first_scale**3 * inner_one / D)
    ).reshape(block_input.shape)

    head_total = lax.psum(jnp.sum(head_grad, (0, 1)), ("dp", "mp", "dmod"))
    head_out = lax.dynamic_slice_in_dim(head_total, place * head_norm.size, head_norm.size, 0)
    small = jnp.concatenate(
        [
            jnp.sum(conv_grad, 0),
            ring.order(jnp.stack([norm_one_grad, norm_two_grad]))
            .reshape(2, data_size, -1)
            .transpose(1, 0, 2)
            .reshape(data_size, -1)
            .reshape(-1)
            .reshape(-1, span),
            ring.order(beta_weight_grad)
            .reshape(-1, data_size, strip)
            .transpose(1, 0, 2)
            .reshape(-1, span),
        ],
        0,
    )
    conv_part = (
        small[:lines].reshape(lines, data_size, -1).transpose(1, 0, 2).reshape(data_size, -1)
    )
    norm_part = small[lines : lines + 2 * width // span].reshape(data_size, -1)
    beta_part = small[lines + 2 * width // span :].reshape(data_size, -1)
    small_own = lax.psum_scatter(
        jnp.concatenate([conv_part, norm_part, beta_part], 1), "dp", scatter_dimension=0
    )
    conv_out = small_own[: conv_kernel.size].reshape(conv_kernel.shape)
    norm_one_out = small_own[conv_kernel.size : conv_kernel.size + strip]
    norm_two_out = small_own[conv_kernel.size + strip : conv_kernel.size + 2 * strip]
    beta_out = small_own[conv_kernel.size + 2 * strip :].reshape(-1, strip).T

    def placed(blocks):
        return exclusive_order(trade([values.astype(LOW) for values in blocks]))

    ffn_out = jnp.stack(
        [
            jnp.concatenate([values.astype(WIDE) for values in placed(list(grad))], 1)
            for grad in ffn_grads
        ],
        1,
    )
    down_out = jnp.concatenate(
        [
            values.astype(WIDE).T
            for values in placed(list(down_grads[0]) + list(down_grads[1]))
        ],
        0,
    )
    out_out = jnp.concatenate(
        exclusive_order(jnp.split(jnp.concatenate([grad[0] for grad in out_grads], 1).T, 4, axis=0)),
        0,
    )
    mix_blocks = sum((jnp.split(grad[0], 2, axis=1) for grad in mix_grads), [])
    mix_out = jnp.concatenate(
        [values.reshape(strip, 4, span) for values in exclusive_order(mix_blocks)], 2
    )
    return (
        out,
        grad_input,
        norm_one_out,
        mix_out,
        beta_out,
        conv_out,
        head_out,
        out_out,
        norm_two_out,
        ffn_out,
        down_out,
    )


def solution(mesh):
    wide = P(("dmod", "dp"))
    tokens = P(None, "dp", None, "dmod")
    weights = (
        wide,
        P(("dmod", "dp"), None, "mp"),
        P(("dmod", "dp"), "mp"),
        P(None, None, ("mp", "dmod", "dp")),
        P("dp"),
        P("mp", ("dmod", "dp")),
        wide,
        P(("dmod", "dp"), None, "mp"),
        P("mp", ("dmod", "dp")),
    )
    ids = P(None, "dp", None)
    return jax.shard_map(
        body,
        mesh=mesh,
        in_specs=(tokens, ids, ids, P()) + weights + (tokens,),
        out_specs=(tokens, tokens) + weights,
        check_vma=False,
    )
```

time: 1680 us -> 724 us (0.43)
  waiting for transfers between devices: 712 us -> 214 us
  other arithmetic: 287 us -> 32.8 us
  matrix products: 260 us -> 64 us
  local copies, waits for them, and re-layouts: 240 us -> 133 us
  blocking collectives: 138 us -> 187 us
  starting transfers between devices: 1.5 us -> 37.5 us
  Pallas kernels: 0 us -> 27.3 us
    reduce_scatter x10 -> x4, waiting for transfers between devices: 376 us -> 26.1 us  [scatter(): lax.psum_scatter(make(0).astype(LOW), 'dp', scatter_dimension=1, tiled=True)]
    another operation x77 -> x9, other arithmetic: 192 us -> 5.74 us  [the longest x2 2.7 us: body(): mix_own = jnp.stack(trade(exclusive_order(jnp.split(w_mix, 4, axis=2))))]
    dot_general x186 -> x7, matrix products: 181 us -> 17.3 us  [the longest x2 6.07 us: body(): jnp.dot(mixer_parts[k], mix_parts[half][k], preferred_element_type=WIDE)]
    ppermute x0 -> x52, waiting for transfers between devices: none -> 114 us  [the longest x18 39.6 us: trade(): lax.ppermute(blocks[m], 'dmod', [(i, i ^ m) for i in range(4)])]
    psum x3 -> x0, waiting for transfers between devices: 104 us -> none  [the longest x2 73.3 us: sum_widths(): return lax.psum(values, 'mp')]
    unnamed x31 -> x18, waiting for transfers between devices: 83.7 us -> 0.24 us
    all_gather x10 -> x6, waiting for transfers between devices: 149 us -> 73.6 us  [gather(): return [lax.all_gather(values, 'dp', axis=1, tiled=True)]]
    psum x2, blocking collectives: 14 us -> 65.7 us  [the longest x1 57.4 us: body(): head_total = lax.psum(jnp.sum(head_grad, (0, 1)), ('dp', 'mp', 'dmod'))]
  transfers between devices with their start and end apart: 27 -> 66, of which waited for: 22 -> 25; matrix products, arithmetic and copies ran while one was open for 25% -> 28% of each run, Pallas kernels for 0% -> 4%
where the time goes in v1:
time: 724 us; the launch traced here: 712 us
  waiting for transfers between devices  214 us (30%)
  blocking collectives  187 us (26%)
  local copies, waits for them, and re-layouts  133 us (18%)
  matrix products  64 us (9%)
  starting transfers between devices  37.5 us (5%)
  other arithmetic  32.8 us (5%)
  Pallas kernels  27.3 us (4%)
  between operations  16.3 us (2%)
    unnamed x159, local copies, waits for them, and re-layouts  84.9 us
    all_gather x6, waiting for transfers between devices, gather(): return [lax.all_gather(values, 'dp', axis=1, tiled=True)]  73.6 us
    psum x1, blocking collectives, body(): head_total = lax.psum(jnp.sum(head_grad, (0, 1)), ('dp', 'mp', 'dmod'))  57.4 us
    dot_general x18, matrix products, contract(): lax.dot_general(left, right, (((left_dim,), (right_dim,)), ((), ())), pre...  46.7 us
    all_gather x2, blocking collectives, gather(): return [lax.all_gather(values, 'dp', axis=1, tiled=True)]  46.1 us
    psum x5, blocking collectives, row_total(): return lax.psum(values, 'dmod')  40.3 us
    ppermute x18, waiting for transfers between devices, trade(): lax.ppermute(blocks[m], 'dmod', [(i, i ^ m) for i in range(4)])  39.6 us
    ppermute x4, waiting for transfers between devices, scatter_width(): lax.ppermute((blocks[2] + cross.astype(WIDE)).astype(LOW), 'dmod', ACROSS)  35.7 us
  transfers between devices with their start and end apart: 66, of which 25 were waited for; matrix products, arithmetic and copies ran while one was open for 28% of the time, Pallas kernels for 4%

profile of v1, /device:TPU:16, one launch (start us, length us, event | category | flops | bytes accessed | tf_op | source)
XLA Modules:
  0.0 711.7 jit_solution(1145547077483887251)
XLA Ops:
  10.9 7.3 %collective-permute-done.4 = bf16[128,4,256]{2,1,0:T(4,128)(2,1)S(1)} collective-permute-done((bf16[128,4,256]{2,1,0:T(4,128)(2,1)S(1)}, bf16[128,4,256]{2,1,0:T(4,128)(2,1)S(1)}, u32[]{:S(2)}, u32[]{:S(2)}) %collective-permute-start.4) | collective-permute-done | bytes 262176 | tf_op jit(solution)/shard_map/ppermute | solution.py:327
  33.7 9.7 %collective-permute-done.14 = bf16[128,2,704]{0,2,1:T(8,128)(2,1)S(1)} collective-permute-done((bf16[128,2,704]{0,2,1:T(8,128)(2,1)S(1)}, bf16[128,2,704]{0,2,1:T(8,128)(2,1)S(1)}, u32[]{:S(2)}, u32[]{:S(2)}) %collective-permute-start.14) | collective-permute-done | bytes 360480 | tf_op jit(solution)/shard_map/ppermute | solution.py:327
  43.4 6.3 collective-permute-done.15
  51.2 20.4 %all-gather.12.cloned.1.call-done = bf16[4,512,512]{2,1,0:T(8,128)(2,1)} async-done(((bf16[4,128,512]{2,1,0:T(8,128)(2,1)}), bf16[4,512,512]{2,1,0:T(8,128)(2,1)}) %all-gather.12.cloned.1.call-update) | async-done | bytes 2097168 | tf_op jit(solution)/shard_map/all_gather | solution.py:377
  73.8 16.7 %all-reduce = bf16[8320]{0:T(1024)(128)(2,1)S(1)} all-reduce(bf16[8320]{0:T(1024)(128)(2,1)S(1)} %dynamic-update-slice), channel_id=2, replica_groups=mesh['dp'=4,'mp'=2,'dmod'=4] {'dp'}, use_global_device_ids=true, to_apply=%add | all-reduce | flops 8320 | bytes 33280
  97.9 20.9 %all-gather.10.cloned.1.call-done = bf16[4,512,512]{2,1,0:T(8,128)(2,1)} async-done(((bf16[4,128,512]{2,1,0:T(8,128)(2,1)}), bf16[4,512,512]{2,1,0:T(8,128)(2,1)}) %all-gather.10.cloned.1.call-update) | async-done | bytes 2097168 | tf_op jit(solution)/shard_map/all_gather | solution.py:377
  124.6 9.4 %collective-permute-done.1 = bf16[512,512]{1,0:T(8,128)(2,1)} collective-permute-done((bf16[512,512]{1,0:T(8,128)(2,1)S(1)}, bf16[512,512]{1,0:T(8,128)(2,1)}, u32[]{:S(2)}, u32[]{:S(2)}) %collective-permute-start.1) | collective-permute-done | bytes 524320 | tf_op jit(solution)/shard_map/ppermute | solution.py:332
  134.6 16.5 %psum.50 = f32[8,512]{0,1:T(8,128)S(1)} all-reduce(f32[8,512]{0,1:T(8,128)S(1)} %fusion.56), channel_id=1, replica_groups=mesh['dp'=4,'mp'=2,'dmod'=4] {'dmod'}, use_global_device_ids=true, to_apply=%region_2.3 | all-reduce | flops 4096 | bytes 32768 | tf_op jit(solution)/shard_map/psum | solution.py:350
  158.0 18.5 %mixer_forward.1 = (bf16[512,256]{1,0:T(8,128)(2,1)S(1)}, f32[2,2,256,256]{3,2,1,0:T(8,128)S(1)}, f32[512,256]{1,0:T(8,128)S(1)}, f32[512,256]{1,0:T(8,128)S(1)}) custom-call(f32[512,512]{1,0:T(8,128)S(1)} %fusion.54.first_ref, f32[512,512]{1,0:T(8,128)S(1)} %fusion.53.second_ref, f32[512,2]{1,0:T(8,128)S(1)} %dynamic-slice_bitcast_fusion.beta_ref, ...), custom_call_target="tpu_custom_call" | custom-call | flops 6710886400 | bytes 8388608 | tf_op jit(solution)/shard_map/mixer_forward/pallas_call | solution.py:248
  179.8 22.0 %all-gather.2 = bf16[512,512]{1,0:T(8,128)(2,1)S(1)} all-gather(bf16[128,512]{1,0:T(8,128)(2,1)S(1)} %get-tuple-element.169), channel_id=4, replica_groups=mesh['dp'=4,'mp'=2,'dmod'=4] {'dp'}, dimensions={0}, use_global_device_ids=true | all-gather | bytes 655360 | tf_op jit(solution)/shard_map/all_gather | solution.py:377
  202.4 24.1 %all-gather.1 = bf16[512,512]{1,0:T(8,128)(2,1)S(1)} all-gather(bf16[128,512]{1,0:T(8,128)(2,1)} %get-tuple-element.170), channel_id=3, replica_groups=mesh['dp'=4,'mp'=2,'dmod'=4] {'dp'}, dimensions={0}, use_global_device_ids=true | all-gather | bytes 655360 | tf_op jit(solution)/shard_map/all_gather | solution.py:377
  226.5 8.3 %psum.52 = f32[8]{0:T(128)S(1)} all-reduce(f32[8]{0:T(128)S(1)} %convert_reduce_fusion), channel_id=1, replica_groups=mesh['dp'=4,'mp'=2,'dmod'=4] {'dp'}, use_global_device_ids=true, to_apply=%region_6.7 | all-reduce | flops 8 | bytes 64 | tf_op jit(solution)/shard_map/psum | solution.py:489
  243.2 7.0 collective-permute-done.9
  262.6 11.4 %collective-permute-done.11 = bf16[512,512]{1,0:T(8,128)(2,1)S(1)} collective-permute-done((bf16[512,512]{1,0:T(8,128)(2,1)S(1)}, bf16[512,512]{1,0:T(8,128)(2,1)S(1)}, u32[]{:S(2)}, u32[]{:S(2)}) %collective-permute-start.11) | collective-permute-done | bytes 524320 | tf_op jit(solution)/shard_map/ppermute | solution.py:332
  288.4 32.3 %all-gather.18.cloned.1.call-done = bf16[2,512,704]{1,2,0:T(8,128)(2,1)} async-done(((bf16[2,128,704]{1,2,0:T(8,128)(2,1)}), bf16[2,512,704]{1,2,0:T(8,128)(2,1)}) %all-gather.18.cloned.1.call-update) | async-done | bytes 1441808 | tf_op jit(solution)/shard_map/all_gather | solution.py:377
  336.8 11.3 %collective-permute-done.28 = bf16[512,512]{1,0:T(8,128)(2,1)S(1)} collective-permute-done((bf16[512,512]{1,0:T(8,128)(2,1)S(1)}, bf16[512,512]{1,0:T(8,128)(2,1)S(1)}, u32[]{:S(2)}, u32[]{:S(2)}) %collective-permute-start.28) | collective-permute-done | bytes 524320 | tf_op jit(solution)/shard_map/ppermute | solution.py:340
  350.0 8.7 %collective-permute-done.21 = bf16[512,512]{1,0:T(8,128)(2,1)S(1)} collective-permute-done((bf16[512,512]{1,0:T(8,128)(2,1)S(1)}, bf16[512,512]{1,0:T(8,128)(2,1)S(1)}, u32[]{:S(2)}, u32[]{:S(2)}) %collective-permute-start.21) | collective-permute-done | bytes 524320 | tf_op jit(solution)/shard_map/ppermute | solution.py:340
  389.9 6.1 copy.161
  408.9 6.1 copy.159
  424.9 7.1 convert_element_type.363
  432.0 7.2 %copy.155 = bf16[4,512,704]{2,0,1:T(4,128)(2,1)} copy(bf16[4,512,704]{1,0,2:T(4,128)(2,1)} %convert_element_type.363) | data formatting | bytes 5767168
  439.2 6.8 reshape.239
  451.0 7.1 convert_element_type.369
  458.1 7.2 %copy.157 = bf16[4,512,704]{2,0,1:T(4,128)(2,1)} copy(bf16[4,512,704]{1,0,2:T(4,128)(2,1)} %convert_element_type.369) | data formatting | bytes 5767168
  465.2 6.8 reshape.241
  477.7 6.8 collective-permute-done.32
  484.6 8.7 %mixer_backward.1 = (bf16[512,1024]{1,0:T(8,128)(2,1)S(1)}, f32[512,2]{1,0:T(8,128)S(1)}, f32[2,12,256]{2,1,0:T(8,128)S(1)}, f32[2,1,128]{2,1,0:T(1,128)S(1)}) custom-call(f32[512,512]{1,0:T(8,128)S(1)} %fusion.54.first_ref, f32[512,512]{1,0:T(8,128)S(1)} %copy-done.2, f32[512,2]{1,0:T(8,128)S(1)} %dynamic-slice_bitcast_fusion.beta_ref, ...), custom_call_target="tpu_custom_call" | custom-call | flops 6710886400 | bytes 8388608 | tf_op jit(solution)/shard_map/mixer_backward/pallas_call | solution.py:277
  510.4 57.4 %psum.55 = f32[128]{0:T(128)S(1)} all-reduce(f32[128]{0:T(128)S(1)} %reduce_sum.99), channel_id=1, replica_groups=mesh['dp'=4,'mp'=2,'dmod'=4] {'dp','mp','dmod'}, use_global_device_ids=true, to_apply=%region_19.20 | all-reduce | flops 128 | bytes 1024 | tf_op jit(solution)/shard_map/psum | solution.py:631
  576.9 8.9 %collective-permute-done.35 = bf16[512,512]{1,0:T(8,128)(2,1)} collective-permute-done((bf16[512,512]{1,0:T(8,128)(2,1)}, bf16[512,512]{1,0:T(8,128)(2,1)}, u32[]{:S(2)}, u32[]{:S(2)}) %collective-permute-start.35) | collective-permute-done | bytes 524320 | tf_op jit(solution)/shard_map/ppermute | solution.py:340
  606.3 18.0 %all-reduce.1 = f32[4,2048]{1,0:T(4,128)S(1)} all-reduce(f32[4,2048]{1,0:T(4,128)S(1)} %pad_maximum_fusion.13), channel_id=5, replica_groups=mesh['dp'=4,'mp'=2,'dmod'=4] {'dp'}, use_global_device_ids=true, to_apply=%region_15.16.clone | all-reduce | flops 8192 | bytes 65536
  627.0 6.2 psum.54
  674.4 26.0 %reduce-scatter.17.cloned.1.call-done = bf16[1,128,2048]{2,1,0:T(8,128)(2,1)} async-done(((bf16[1,512,2048]{2,1,0:T(8,128)(2,1)}), bf16[1,128,2048]{2,1,0:T(8,128)(2,1)}) %reduce-scatter.17.cloned.1.call-update) | async-done | bytes 524304 | tf_op jit(solution)/shard_map/reduce_scatter | solution.py:385
  (420 shorter events, 258.2 us)
Async XLA Ops:
  7.2 64.4 %all-gather.12.cloned.1.call-start = ((), (), s32[]{:S(2)}) async-start(), calls=%async_computation.9 | async-start | bytes 2621440 | tf_op jit(solution)/shard_map/all_gather | solution.py:377
  25.8 93.0 %all-gather.10.cloned.1.call-start = ((), (), s32[]{:S(2)}) async-start(), calls=%async_computation.8 | async-start | bytes 2621440 | tf_op jit(solution)/shard_map/all_gather | solution.py:377
  27.0 152.8 %all-gather.16.cloned.1.call-start = ((), (), s32[]{:S(2)}) async-start(), calls=%async_computation.11 | async-start | bytes 3604480 | tf_op jit(solution)/shard_map/all_gather | solution.py:377
  71.6 186.6 %all-gather.14.cloned.1.call-start = ((), (), s32[]{:S(2)}) async-start(), calls=%async_computation.10 | async-start | bytes 3604480 | tf_op jit(solution)/shard_map/all_gather | solution.py:377
  118.8 166.9 %all-gather.20.cloned.1.call-start = ((), (), s32[]{:S(2)}) async-start(), calls=%async_computation.13 | async-start | bytes 1802240 | tf_op jit(solution)/shard_map/all_gather | solution.py:377
  120.6 31.3 %collective-permute-start = (bf16[512,512]{1,0:T(8,128)(2,1)S(1)}, bf16[512,512]{1,0:T(8,128)(2,1)}, u32[]{:S(2)}, u32[]{:S(2)}) collective-permute-start(bf16[512,512]{1,0:T(8,128)(2,1)S(1)} %fusion.34), channel_id=1, source_target_pairs={{0,1},{1,0},{2,3},{3,2},{4,5},{5,4},{6,7},{7,6},{8,9},{9,8},{10,11... | collective-permute-start | bytes 1572872 | tf_op jit(solution)/shard_map/ppermute | solution.py:333
  121.4 57.6 %collective-permute-start.18 = (bf16[704,128]{1,0:T(8,128)(2,1)S(1)}, bf16[704,128]{1,0:T(8,128)(2,1)S(1)}, u32[]{:S(2)}, u32[]{:S(2)}) collective-permute-start(bf16[704,128]{1,0:T(8,128)(2,1)S(1)} %get-tuple-element.153), channel_id=1, source_target_pairs={{0,2},{1,3},{2,0},{3,1},{4,6},{5,7},{6,4},{7,5},{8,10},{9,11},{10,... | collective-permute-start | bytes 540680 | tf_op jit(solution)/shard_map/ppermute | solution.py:327
  122.0 119.5 %collective-permute-start.16 = (bf16[704,128]{1,0:T(8,128)(2,1)}, bf16[704,128]{1,0:T(8,128)(2,1)}, u32[]{:S(2)}, u32[]{:S(2)}) collective-permute-start(bf16[704,128]{1,0:T(8,128)(2,1)} %get-tuple-element.154), channel_id=1, source_target_pairs={{0,1},{1,0},{2,3},{3,2},{4,5},{5,4},{6,7},{7,6},{8,9},{9,8},{10,11... | collective-permute-start | bytes 540680 | tf_op jit(solution)/shard_map/ppermute | solution.py:327
  122.2 56.8 %collective-permute-start.19 = (bf16[704,128]{1,0:T(8,128)(2,1)S(1)}, bf16[704,128]{1,0:T(8,128)(2,1)S(1)}, u32[]{:S(2)}, u32[]{:S(2)}) collective-permute-start(bf16[704,128]{1,0:T(8,128)(2,1)S(1)} %get-tuple-element.155), channel_id=1, source_target_pairs={{0,3},{1,2},{2,1},{3,0},{4,7},{5,6},{6,5},{7,4},{8,11},{9,10},{10,... | collective-permute-start | bytes 540680 | tf_op jit(solution)/shard_map/ppermute | solution.py:327
  178.4 23.5 %collective-permute-start.7 = (bf16[512,256]{1,0:T(8,128)(2,1)S(1)}, bf16[512,256]{1,0:T(8,128)(2,1)}, u32[]{:S(2)}, u32[]{:S(2)}) collective-permute-start(bf16[512,256]{1,0:T(8,128)(2,1)S(1)} %get-tuple-element.27), channel_id=1, source_target_pairs={{0,2},{1,3},{2,0},{3,1},{4,6},{5,7},{6,4},{7,5},{8,10},{9,11},{10,... | collective-permute-start | bytes 786440 | tf_op jit(solution)/shard_map/ppermute | solution.py:332
  179.8 140.9 %all-gather.18.cloned.1.call-start = ((), (), s32[]{:S(2)}) async-start(), calls=%async_computation.12 | async-start | bytes 1802240 | tf_op jit(solution)/shard_map/all_gather | solution.py:377
  201.9 33.1 %collective-permute-start.6 = (bf16[512,256]{1,0:T(8,128)(2,1)S(1)}, bf16[512,256]{1,0:T(8,128)(2,1)}, u32[]{:S(2)}, u32[]{:S(2)}) collective-permute-start(bf16[512,256]{1,0:T(8,128)(2,1)S(1)} %get-tuple-element.27), channel_id=1, source_target_pairs={{0,1},{1,0},{2,3},{3,2},{4,5},{5,4},{6,7},{7,6},{8,9},{9,8},{10,11... | collective-permute-start | bytes 786440 | tf_op jit(solution)/shard_map/ppermute | solution.py:333
  201.9 33.1 %collective-permute-start.8 = (bf16[512,256]{1,0:T(8,128)(2,1)}, bf16[512,256]{1,0:T(8,128)(2,1)}, u32[]{:S(2)}, u32[]{:S(2)}) collective-permute-start(bf16[512,256]{1,0:T(8,128)(2,1)} %collective-permute-done.7), channel_id=1, source_target_pairs={{0,1},{1,0},{2,3},{3,2},{4,5},{5,4},{6,7},{7,6},{8,9},{9,8},{10,11... | collective-permute-start | bytes 786440 | tf_op jit(solution)/shard_map/ppermute | solution.py:334
  239.9 22.2 %collective-permute-start.24 = (bf16[512,512]{1,0:T(8,128)(2,1)S(1)}, bf16[512,512]{1,0:T(8,128)(2,1)}, u32[]{:S(2)}, u32[]{:S(2)}) collective-permute-start(bf16[512,512]{1,0:T(8,128)(2,1)S(1)} %fusion.28), channel_id=1, source_target_pairs={{0,2},{1,3},{2,0},{3,1},{4,6},{5,7},{6,4},{7,5},{8,10},{9,11},{10,... | collective-permute-start | bytes 1572872 | tf_op jit(solution)/shard_map/ppermute | solution.py:332
  258.3 316.4 %reduce-scatter.23.cloned.1.call-start = ((), (), s32[]{:S(2)}) async-start(), calls=%async_computation.17 | async-start | bytes 655360 | tf_op jit(solution)/shard_map/reduce_scatter | solution.py:385
  274.1 48.2 %collective-permute-start.23 = (bf16[512,512]{1,0:T(8,128)(2,1)S(1)}, bf16[512,512]{1,0:T(8,128)(2,1)}, u32[]{:S(2)}, u32[]{:S(2)}) collective-permute-start(bf16[512,512]{1,0:T(8,128)(2,1)S(1)} %fusion.28), channel_id=1, source_target_pairs={{0,1},{1,0},{2,3},{3,2},{4,5},{5,4},{6,7},{7,6},{8,9},{9,8},{10,11... | collective-permute-start | bytes 1572872 | tf_op jit(solution)/shard_map/ppermute | solution.py:333
  336.2 22.4 %collective-permute-start.21 = (bf16[512,512]{1,0:T(8,128)(2,1)S(1)}, bf16[512,512]{1,0:T(8,128)(2,1)S(1)}, u32[]{:S(2)}, u32[]{:S(2)}) collective-permute-start(bf16[512,512]{1,0:T(8,128)(2,1)S(1)} %fusion.17), channel_id=1, source_target_pairs={{0,2},{1,3},{2,0},{3,1},{4,6},{5,7},{6,4},{7,5},{8,10},{9,11},{10,... | collective-permute-start | bytes 1572872 | tf_op jit(solution)/shard_map/ppermute | solution.py:340
  379.3 195.4 %reduce-scatter.21.cloned.1.call-start = ((), (), s32[]{:S(2)}) async-start(), calls=%async_computation.16 | async-start | bytes 655360 | tf_op jit(solution)/shard_map/reduce_scatter | solution.py:385
  381.7 209.0 %reduce-scatter.31.cloned.1.call-start = ((), (), s32[]{:S(2)}) async-start(), calls=%async_computation.21 | async-start | bytes 1802240
  400.6 193.9 %reduce-scatter.29.cloned.1.call-start = ((), (), s32[]{:S(2)}) async-start(), calls=%async_computation.20 | async-start | bytes 1802240
  419.6 216.2 %reduce-scatter.25.cloned.1.call-start = ((), (), s32[]{:S(2)}) async-start(), calls=%async_computation.18 | async-start | bytes 3604480
  446.0 198.3 %reduce-scatter.27.cloned.1.call-start = ((), (), s32[]{:S(2)}) async-start(), calls=%async_computation.19 | async-start | bytes 3604480
  472.0 201.2 %reduce-scatter.19.cloned.1.call-start = ((), (), s32[]{:S(2)}) async-start(), calls=%async_computation.15 | async-start | bytes 2621440 | tf_op jit(solution)/shard_map/reduce_scatter | solution.py:385
  498.8 201.7 %reduce-scatter.17.cloned.1.call-start = ((), (), s32[]{:S(2)}) async-start(), calls=%async_computation.14 | async-start | bytes 2621440 | tf_op jit(solution)/shard_map/reduce_scatter | solution.py:385
  506.5 61.8 %collective-permute-start.34 = (bf16[512,512]{1,0:T(8,128)(2,1)S(1)}, bf16[512,512]{1,0:T(8,128)(2,1)}, u32[]{:S(2)}, u32[]{:S(2)}) collective-permute-start(bf16[512,512]{1,0:T(8,128)(2,1)S(1)} %get-tuple-element.110), channel_id=1, source_target_pairs={{0,1},{1,0},{2,3},{3,2},{4,5},{5,4},{6,7},{7,6},{8,9},{9,8},{10,11... | collective-permute-start | bytes 1572872 | tf_op jit(solution)/shard_map/ppermute | solution.py:339
  506.7 69.2 %collective-permute-start.40 = (bf16[512,1024]{1,0:T(8,128)(2,1)S(1)}, bf16[512,1024]{1,0:T(8,128)(2,1)}, u32[]{:S(2)}, u32[]{:S(2)}) collective-permute-start(bf16[512,1024]{1,0:T(8,128)(2,1)S(1)} %get-tuple-element.35), channel_id=1, source_target_pairs={{0,2},{1,3},{2,0},{3,1},{4,6},{5,7},{6,4},{7,5},{8,10},{9,11},{10,... | collective-permute-start | bytes 3145736 | tf_op jit(solution)/shard_map/ppermute | solution.py:332
  508.9 59.5 %collective-permute-start.36 = (bf16[2,512]{0,1:T(8,128)(2,1)}, bf16[2,512]{0,1:T(8,128)(2,1)}, u32[]{:S(2)}, u32[]{:S(2)}) collective-permute-start(bf16[2,512]{0,1:T(8,128)(2,1)} %convert_bitcast_fusion.1), channel_id=1, source_target_pairs={{0,2},{1,3},{2,0},{3,1},{4,6},{5,7},{6,4},{7,5},{8,10},{9,11},{10,... | collective-permute-start | bytes 6152 | tf_op jit(solution)/shard_map/ppermute | solution.py:332
  509.6 63.4 %collective-permute-start.38 = (bf16[2,512]{0,1:T(8,128)(2,1)}, bf16[2,512]{0,1:T(8,128)(2,1)}, u32[]{:S(2)}, u32[]{:S(2)}) collective-permute-start(bf16[2,512]{0,1:T(8,128)(2,1)} %convert_bitcast_fusion.1), channel_id=1, source_target_pairs={{0,1},{1,0},{2,3},{3,2},{4,5},{5,4},{6,7},{7,6},{8,9},{9,8},{10,11... | collective-permute-start | bytes 6152 | tf_op jit(solution)/shard_map/ppermute | solution.py:333
  509.9 66.2 %collective-permute-start.33 = (bf16[512,512]{1,0:T(8,128)(2,1)}, bf16[512,512]{1,0:T(8,128)(2,1)S(1)}, u32[]{:S(2)}, u32[]{:S(2)}) collective-permute-start(bf16[512,512]{1,0:T(8,128)(2,1)} %get-tuple-element.109), channel_id=1, source_target_pairs={{0,1},{1,0},{2,3},{3,2},{4,5},{5,4},{6,7},{7,6},{8,9},{9,8},{10,11... | collective-permute-start | bytes 1572872 | tf_op jit(solution)/shard_map/ppermute | solution.py:338
  575.8 26.3 %collective-permute-start.41 = (bf16[512,1024]{1,0:T(8,128)(2,1)}, bf16[512,1024]{1,0:T(8,128)(2,1)}, u32[]{:S(2)}, u32[]{:S(2)}) collective-permute-start(bf16[512,1024]{1,0:T(8,128)(2,1)} %collective-permute-done.40), channel_id=1, source_target_pairs={{0,1},{1,0},{2,3},{3,2},{4,5},{5,4},{6,7},{7,6},{8,9},{9,8},{10,11... | collective-permute-start | bytes 3145736 | tf_op jit(solution)/shard_map/ppermute | solution.py:334
  594.6 56.5 %collective-permute-start.51 = (bf16[128,704]{0,1:T(8,128)(2,1)}, bf16[128,704]{0,1:T(8,128)(2,1)}, u32[]{:S(2)}, u32[]{:S(2)}) collective-permute-start(bf16[128,704]{0,1:T(8,128)(2,1)} %bitcast.84), channel_id=1, source_target_pairs={{0,1},{1,0},{2,3},{3,2},{4,5},{5,4},{6,7},{7,6},{8,9},{9,8},{10,11... | collective-permute-start | bytes 540680 | tf_op jit(solution)/shard_map/ppermute | solution.py:327
  598.1 56.4 %collective-permute-start.50 = (bf16[128,704]{0,1:T(8,128)(2,1)S(1)}, bf16[128,704]{0,1:T(8,128)(2,1)}, u32[]{:S(2)}, u32[]{:S(2)}) collective-permute-start(bf16[128,704]{0,1:T(8,128)(2,1)S(1)} %bitcast.305), channel_id=1, source_target_pairs={{0,2},{1,3},{2,0},{3,1},{4,6},{5,7},{6,4},{7,5},{8,10},{9,11},{10,... | collective-permute-start | bytes 540680 | tf_op jit(solution)/shard_map/ppermute | solution.py:327
  (92 other events, 1163.1 us)
Sparse Core Ops, SparseCore 0:
  25.9 45.6 all-gather.11
  73.7 44.9 all-gather.9
  120.9 57.4 all-gather.15
  180.4 67.7 all-gather.13
  249.7 35.1 all-gather.19
  286.9 33.7 all-gather.17
  379.5 20.0 reduce-scatter.22
  401.8 19.9 reduce-scatter.20
  424.1 32.1 reduce-scatter.30
  459.0 32.1 reduce-scatter.28
  493.5 56.3 reduce-scatter.24
  552.6 56.1 reduce-scatter.26
  611.0 43.4 reduce-scatter.18
  657.3 43.1 reduce-scatter.16

commit v2 on v1

v2 whole, which is shorter than its diff:
```python
import jax
import jax.numpy as jnp
from jax import lax
from jax.experimental import pallas as pl
from jax.experimental.pallas import tpu as pltpu
from jax.sharding import PartitionSpec as P

D = 2048
HEAD = 128
LOW = jnp.bfloat16
WIDE = jnp.float32
LONGEST_RING = 1
CORE = [(i, i ^ 1) for i in range(4)]
ACROSS = [(i, i ^ 2) for i in range(4)]
SWAP = [(0, 1), (1, 0)]


def halves(values):
    high = values.astype(LOW)
    return high, (values - high.astype(WIDE)).astype(LOW)


def product(left, right, left_dim, right_dim):
    def one(a, b):
        return lax.dot_general(
            a, b, (((left_dim,), (right_dim,)), ((), ())), preferred_element_type=WIDE
        )

    return one(left[0], right[0]) + (one(left[0], right[1]) + one(left[1], right[0]))


def sigmoid(values):
    return 1.0 / (1.0 + jnp.exp(-values))


def masks_of(seg_col, seg_row):
    length = seg_col.shape[0]
    rows = lax.broadcasted_iota(jnp.int32, (length, length), 0)
    cols = lax.broadcasted_iota(jnp.int32, (length, length), 1)
    same = seg_col == seg_row
    return rows, cols, same & (cols < rows), same & (cols <= rows)


def kept_of(seg_col, taps):
    length = seg_col.shape[0]
    wide = jnp.broadcast_to(seg_col, (length, HEAD))
    place = lax.broadcasted_iota(jnp.int32, (length, HEAD), 0)
    return [
        ((pltpu.roll(wide, shift, 0) == wide) & (place >= shift)).astype(WIDE)
        for shift in range(1, taps)
    ]


def convolve(signal, kernel, kept):
    taps = kernel.shape[0]
    total = signal * kernel[taps - 1 : taps]
    for shift in range(1, taps):
        moved = pltpu.roll(signal, shift, 0) * kept[shift - 1]
        total = total + moved * kernel[taps - 1 - shift : taps - shift]
    return total


def blocks_of(order_ref, length):
    count = order_ref.shape[0]
    share = length // count
    return [pl.ds(pl.multiple_of(order_ref[j] * share, share), share) for j in range(count)]


def single(left, right):
    return lax.dot_general(
        left.astype(LOW),
        right.astype(LOW),
        (((1,), (0,)), ((), ())),
        preferred_element_type=WIDE,
    )


def invert(lower, rows, cols):
    length = lower.shape[0]
    eye = (rows == cols).astype(WIDE)
    inverse = eye - jnp.where((rows // 2) == (cols // 2), lower, 0.0)
    size = 2
    while size < length:
        cross = ((rows // (2 * size)) == (cols // (2 * size))) & ((rows // size) != (cols // size))
        inverse = inverse - single(single(inverse, jnp.where(cross, lower, 0.0)), inverse)
        size *= 2
    rest = eye - inverse - product(halves(lower), halves(inverse), 1, 0)
    return inverse + single(inverse, rest)


def forward_head(signals, beta_in, conv, kept, masks, gain):
    rows, cols, strict, inclusive = masks
    taps = conv.shape[0] // 3
    convolved = []
    for part in range(3):
        pre = convolve(signals[part], conv[part * taps : (part + 1) * taps], kept)
        convolved.append(pre * sigmoid(pre))
    query = convolved[0] * (
        lax.rsqrt(jnp.sum(convolved[0] * convolved[0], 1, keepdims=True) + 1e-06) * HEAD**-0.5
    )
    key = convolved[1] * lax.rsqrt(
        jnp.sum(convolved[1] * convolved[1], 1, keepdims=True) + 1e-06
    )
    beta = sigmoid(beta_in)
    key_parts = halves(key)
    gram = product(key_parts, key_parts, 1, 1)
    inverse = invert(jnp.where(strict, gram * beta, 0.0), rows, cols)
    update = product(halves(inverse), halves(convolved[2] * beta), 1, 0)
    scores = jnp.where(inclusive, product(halves(query), key_parts, 1, 1), 0.0)
    mixed = product(halves(scores), halves(update), 1, 0)
    scale = lax.rsqrt(jnp.sum(mixed * mixed, 1, keepdims=True) * (1.0 / HEAD) + 1e-05)
    gate = signals[3]
    gated = (mixed * scale * gain * (gate * sigmoid(gate))).astype(LOW)
    return gated, inverse, update, mixed


def backward_head(signals, beta_in, conv, kept, masks, gain, inverse, update, mixed, grad):
    rows, cols, strict, inclusive = masks
    length = grad.shape[0]
    taps = conv.shape[0] // 3
    before, gates, convolved = [], [], []
    for part in range(3):
        pre = convolve(signals[part], conv[part * taps : (part + 1) * taps], kept)
        before.append(pre)
        gates.append(sigmoid(pre))
        convolved.append(pre * gates[part])
    query_unit = lax.rsqrt(jnp.sum(convolved[0] * convolved[0], 1, keepdims=True) + 1e-06)
    key_unit = lax.rsqrt(jnp.sum(convolved[1] * convolved[1], 1, keepdims=True) + 1e-06)
    query = convolved[0] * (query_unit * HEAD**-0.5)
    key = convolved[1] * key_unit
    beta = sigmoid(beta_in)
    gate = signals[3]
    gate_sigma = sigmoid(gate)
    opened = gate * gate_sigma
    scale = lax.rsqrt(jnp.sum(mixed * mixed, 1, keepdims=True) * (1.0 / HEAD) + 1e-05)
    normed = mixed * scale
    head_grad = jnp.sum(grad * opened * normed, 0, keepdims=True)
    inner = grad * opened * gain
    mixed_grad = scale * inner - mixed * (
        scale * scale * scale * (jnp.sum(inner * mixed, 1, keepdims=True) * (1.0 / HEAD))
    )
    gate_grad = grad * normed * gain * gate_sigma * (1.0 + gate * (1.0 - gate_sigma))
    key_parts = halves(key)
    query_parts = halves(query)
    update_parts = halves(update)
    mixed_parts = halves(mixed_grad)
    gram = product(key_parts, key_parts, 1, 1)
    scores = jnp.where(inclusive, product(query_parts, key_parts, 1, 1), 0.0)
    scores_grad = halves(jnp.where(inclusive, product(mixed_parts, update_parts, 1, 1), 0.0))
    update_grad = product(halves(scores), mixed_parts, 0, 0)
    solved = product(halves(inverse), halves(update_grad), 0, 0)
    system_grad = jnp.where(strict, -product(halves(solved), update_parts, 1, 1), 0.0)
    gram_grad = halves(system_grad * beta)
    query_grad = product(scores_grad, key_parts, 1, 0)
    key_grad = (
        product(scores_grad, query_parts, 0, 0)
        + product(gram_grad, key_parts, 1, 0)
        + product(gram_grad, key_parts, 0, 0)
    )
    beta_grad = jnp.sum(system_grad * gram, 1, keepdims=True) + jnp.sum(
        solved * convolved[2], 1, keepdims=True
    )
    beta_grad = beta_grad * beta * (1.0 - beta)
    conv_grads = [
        HEAD**-0.5
        * (
            query_grad * query_unit
            - convolved[0]
            * (
                query_unit
                * query_unit
                * query_unit
                * jnp.sum(convolved[0] * query_grad, 1, keepdims=True)
            )
        ),
        key_grad * key_unit
        - convolved[1]
        * (key_unit * key_unit * key_unit * jnp.sum(convolved[1] * key_grad, 1, keepdims=True)),
        solved * beta,
    ]
    lines = [None] * (3 * taps)
    signal_grads = []
    for part in range(3):
        sigma = gates[part]
        error = conv_grads[part] * sigma * (1.0 + before[part] * (1.0 - sigma))
        kernel = conv[part * taps : (part + 1) * taps]
        total = error * kernel[taps - 1 : taps]
        last = part * taps + taps - 1
        lines[last] = jnp.sum(error * signals[part], 0, keepdims=True)
        for shift in range(1, taps):
            held = error * kept[shift - 1]
            lines[last - shift] = jnp.sum(
                held * pltpu.roll(signals[part], shift, 0), 0, keepdims=True
            )
            total = total + pltpu.roll(held, length - shift, 0) * (
                kernel[taps - 1 - shift : taps - shift]
            )
        signal_grads.append(total.astype(LOW))
    signal_grads.append(gate_grad.astype(LOW))
    return signal_grads, beta_grad, lines, head_grad


def head_lanes(head):
    return slice(head * HEAD, (head + 1) * HEAD)


def mixer_forward_kernel(*refs):
    parts = refs[:2]
    beta_ref, col_ref, row_ref, conv_ref, head_ref = refs[2:7]
    gated_ref, inverse_ref, update_ref, mixed_ref = refs[7:]
    masks = masks_of(col_ref[...], row_ref[0])
    kept = kept_of(col_ref[...], conv_ref.shape[0] // 3)
    for head in range(2):
        own = head_lanes(head)
        gated_ref[:, own], inverse_ref[0, head], update_ref[:, own], mixed_ref[:, own] = (
            forward_head(
                [parts[head][:, head_lanes(part)] for part in range(4)],
                beta_ref[:, head : head + 1],
                conv_ref[:, own],
                kept,
                masks,
                head_ref[...],
            )
        )


def mixer_backward_kernel(*refs):
    parts = refs[:2]
    beta_ref, col_ref, row_ref, conv_ref, head_ref = refs[2:7]
    inverse_ref, update_ref, mixed_ref, grad_ref = refs[7:11]
    out_ref, beta_grad_ref, conv_grad_ref, head_grad_ref = refs[11:]
    masks = masks_of(col_ref[...], row_ref[0])
    kept = kept_of(col_ref[...], conv_ref.shape[0] // 3)
    head_grad = jnp.zeros((1, HEAD), WIDE)
    for head in range(2):
        own = head_lanes(head)
        grads, beta_grad, lines, gain_grad = backward_head(
            [parts[head][:, head_lanes(part)] for part in range(4)],
            beta_ref[:, head : head + 1],
            conv_ref[:, own],
            kept,
            masks,
            head_ref[...],
            inverse_ref[0, head],
            update_ref[:, own],
            mixed_ref[:, own],
            grad_ref[:, own],
        )
        head_grad = head_grad + gain_grad
        beta_grad_ref[:, head : head + 1] = beta_grad
        for line, values in enumerate(lines):
            conv_grad_ref[0, line : line + 1, own] = values
        for part in range(4):
            out_ref[:, head_lanes(4 * head + part)] = grads[part]
    head_grad_ref[0] = head_grad


def mixer_specs(length, lines):
    part = pl.BlockSpec((length, 4 * HEAD), lambda i: (i, 0))
    return [
        part,
        part,
        pl.BlockSpec((length, 2), lambda i: (i, 0)),
        pl.BlockSpec((length, 1), lambda i: (i, 0)),
        pl.BlockSpec((1, 1, length), lambda i: (i, 0, 0)),
        pl.BlockSpec((lines, 2 * HEAD), lambda i: (0, 0)),
        pl.BlockSpec((1, HEAD), lambda i: (0, 0)),
    ]


def saved_specs(length):
    return [
        pl.BlockSpec((1, 2, length, length), lambda i: (i, 0, 0, 0)),
        pl.BlockSpec((length, 2 * HEAD), lambda i: (i, 0)),
        pl.BlockSpec((length, 2 * HEAD), lambda i: (i, 0)),
    ]


def saved_shapes(count, length):
    return [
        jax.ShapeDtypeStruct((count, 2, length, length), WIDE),
        jax.ShapeDtypeStruct((count * length, 2 * HEAD), WIDE),
        jax.ShapeDtypeStruct((count * length, 2 * HEAD), WIDE),
    ]


def grad_specs(length, lines):
    return [
        pl.BlockSpec((length, 8 * HEAD), lambda i: (i, 0)),
        pl.BlockSpec((length, 2), lambda i: (i, 0)),
        pl.BlockSpec((1, lines, 2 * HEAD), lambda i: (i, 0, 0)),
        pl.BlockSpec((1, 1, HEAD), lambda i: (i, 0, 0)),
    ]


def grad_shapes(count, length, lines):
    return [
        jax.ShapeDtypeStruct((count * length, 8 * HEAD), LOW),
        jax.ShapeDtypeStruct((count * length, 2), WIDE),
        jax.ShapeDtypeStruct((count, lines, 2 * HEAD), WIDE),
        jax.ShapeDtypeStruct((count, 1, HEAD), WIDE),
    ]


def mixer_forward(inputs):
    count, _, length = inputs[4].shape
    return pl.pallas_call(
        mixer_forward_kernel,
        grid=(count,),
        in_specs=mixer_specs(length, inputs[5].shape[0]),
        out_specs=[pl.BlockSpec((length, 2 * HEAD), lambda i: (i, 0))] + saved_specs(length),
        out_shape=[jax.ShapeDtypeStruct((count * length, 2 * HEAD), LOW)]
        + saved_shapes(count, length),
        compiler_params=pltpu.CompilerParams(vmem_limit_bytes=32 << 20),
        name="mixer_forward",
    )(*inputs)


def mixer_backward(inputs, saved, grad):
    count, _, length = inputs[4].shape
    lines = inputs[5].shape[0]
    return pl.pallas_call(
        mixer_backward_kernel,
        grid=(count,),
        in_specs=mixer_specs(length, lines)
        + saved_specs(length)
        + [pl.BlockSpec((length, 2 * HEAD), lambda i: (i, 0))],
        out_specs=grad_specs(length, lines),
        out_shape=grad_shapes(count, length, lines),
        compiler_params=pltpu.CompilerParams(vmem_limit_bytes=32 << 20),
        name="mixer_backward",
    )(*inputs, *saved, grad)


def across(refs, rows):
    return jnp.concatenate(
        [ref[z, c, rows] for ref in refs for z in range(ref.shape[0]) for c in range(2)], 1
    )


def down_list(refs):
    return jnp.concatenate([ref[...] for ref in refs], 0)


def turned(left, right):
    return lax.dot_general(
        left, right, (((0,), (0,)), ((), ())), preferred_element_type=WIDE
    )


def straight(left, right):
    return lax.dot_general(
        left, right, (((1,), (0,)), ((), ())), preferred_element_type=WIDE
    )


def crossed(left, right):
    return lax.dot_general(
        left, right, (((1,), (1,)), ((), ())), preferred_element_type=WIDE
    )


def collect(token_refs, hold_ref, place_refs):
    half = len(token_refs) // 2
    for step in range(2):

        @pl.when(pl.program_id(0) == step)
        def _():
            for k in range(half):
                hold_ref[place_refs[k], :] = token_refs[step * half + k][...]


def deal(near_ref, far_ref, values, places, lanes):
    share = values.shape[0] // len(places)
    for step, ref in enumerate((near_ref, far_ref)):

        @pl.when(pl.program_id(0) == step)
        def _():
            for j, place in enumerate(places):
                ref[place, lanes] = values[j * share : (j + 1) * share].astype(LOW)


def whole(values):
    rank = len(values.shape)
    return pl.BlockSpec(values.shape, lambda i: (0,) * rank)


def split_refs(refs, sizes):
    out, start = [], 0
    for size in sizes:
        out.append(refs[start : start + size])
        start += size
    return out


def flat(grid):
    return [item for pair in grid for items in pair for item in items]


def nested(refs, lengths):
    flat_lists = split_refs(refs, [n for pair in lengths for n in pair])
    return [flat_lists[:2], flat_lists[2:]]


def lengths_of(grid):
    return [[len(items) for items in pair] for pair in grid]


def call(kernel, inputs, in_specs, out_specs, out_shape, scratch, name, grid=2, work=20):
    return pl.pallas_call(
        kernel,
        grid=(grid,),
        in_specs=in_specs,
        out_specs=out_specs,
        out_shape=out_shape,
        scratch_shapes=scratch,
        compiler_params=pltpu.CompilerParams(vmem_limit_bytes=48 << 20),
        cost_estimate=pl.CostEstimate(
            flops=work * 10**9, bytes_accessed=8 << 20, transcendentals=0
        ),
        name=name,
    )(*inputs)


def column_forward(tokens, weights, gain, beta_weights, seg_col, seg_row, conv, head_gain, order):
    count, _, length = seg_row.shape
    width = tokens[0].shape[1]
    lengths = lengths_of(weights)
    pieces = flat(weights)

    def kernel(*refs):
        token_refs, weight_refs, rest = split_refs(refs, [len(tokens), len(pieces), 18])
        gain_ref, beta_ref, col_ref, row_ref, conv_ref, head_ref, order_ref = rest[:7]
        gated_ref, inverse_ref, update_ref, mixed_ref = rest[7:11]
        mixer_ref, first_ref, second_ref, beta_in_ref, hold_ref = rest[11:]
        weight_refs = nested(weight_refs, lengths)
        collect(token_refs, hold_ref, blocks_of(order_ref, length))
        values = hold_ref[...].astype(WIDE)
        scale = lax.rsqrt(jnp.sum(values * values, 1, keepdims=True) * (1.0 / D) + 1e-06)
        mixer_ref[...] = (values * scale * gain_ref[...]).astype(LOW)
        masks = masks_of(col_ref[...], row_ref[0])
        kept = kept_of(col_ref[...], conv_ref.shape[0] // 3)
        mixer_in = mixer_ref[...].astype(WIDE)
        half = width // 2
        for head, projected_ref in enumerate((first_ref, second_ref)):
            own = head_lanes(head)
            projected_ref[...] = straight(
                mixer_ref[:, :half], down_list(weight_refs[head][0])
            ) + straight(mixer_ref[:, half:], down_list(weight_refs[head][1]))
            beta_in = jnp.sum(
                mixer_in * beta_ref[head : head + 1, :].astype(WIDE), 1, keepdims=True
            )
            beta_in_ref[:, head : head + 1] = beta_in
            gated_ref[:, own], inverse_ref[0, head], update_ref[:, own], mixed_ref[:, own] = (
                forward_head(
                    [projected_ref[:, head_lanes(part)] for part in range(4)],
                    beta_in,
                    conv_ref[:, own],
                    kept,
                    masks,
                    head_ref[...],
                )
            )

    inputs = list(tokens) + pieces + [
        gain, beta_weights, seg_col, seg_row, conv, head_gain, order
    ]
    in_specs = [whole(item) for item in inputs]
    in_specs[-5] = pl.BlockSpec((length, 1), lambda i: (i, 0))
    in_specs[-4] = pl.BlockSpec((1, 1, length), lambda i: (i, 0, 0))
    in_specs[-1] = pl.BlockSpec(memory_space=pltpu.SMEM)
    step = lambda lanes: pl.BlockSpec((length, lanes), lambda i: (i, 0))
    shape = lambda lanes, kind: jax.ShapeDtypeStruct((count * length, lanes), kind)
    return call(
        kernel,
        inputs,
        in_specs,
        [step(2 * HEAD)]
        + saved_specs(length)
        + [step(width), step(4 * HEAD), step(4 * HEAD), step(2)],
        [shape(2 * HEAD, LOW)]
        + saved_shapes(count, length)
        + [shape(width, LOW), shape(4 * HEAD, WIDE), shape(4 * HEAD, WIDE), shape(2, WIDE)],
        [pltpu.VMEM((length, width), LOW)],
        "column_forward",
    )


def column_branch(gated, weights, order, length):
    lengths = lengths_of(weights)
    pieces = flat(weights)
    width = 2 * sum(item.shape[0] * 2 * item.shape[3] for item in weights[0][0])

    def kernel(*refs):
        gated_ref, weight_refs, rest = refs[0], nested(refs[1 : 1 + len(pieces)], lengths), refs[-3:]
        order_ref, near_ref, far_ref = rest
        places = blocks_of(order_ref, length)
        half = width // 2
        for far in range(2):
            values = straight(
                gated_ref[:, :HEAD], across(weight_refs[0][far], slice(None))
            ) + straight(gated_ref[:, HEAD:], across(weight_refs[1][far], slice(None)))
            deal(near_ref, far_ref, values, places, slice(far * half, (far + 1) * half))

    inputs = [gated] + pieces + [order]
    in_specs = [whole(item) for item in inputs]
    in_specs[0] = pl.BlockSpec((length, 2 * HEAD), lambda i: (i, 0))
    in_specs[-1] = pl.BlockSpec(memory_space=pltpu.SMEM)
    out = jax.ShapeDtypeStruct((length, width), LOW)
    return call(kernel, inputs, in_specs, [whole(out)] * 2, [out] * 2, [], "column_branch", work=2)


def column_ffn(tokens, directions, first, down, hidden):
    share, width = tokens[0].shape
    length = share * len(tokens) // 2
    lengths = [lengths_of(first), lengths_of(down)]
    pieces = [flat(first), flat(down)]
    gate_rows, up_rows = slice(0, hidden), slice(hidden, 2 * hidden)

    def kernel(*refs):
        token_refs, way_refs, first_refs, down_refs, rest = split_refs(
            refs, [len(tokens), len(tokens), len(pieces[0]), len(pieces[1]), 10]
        )
        first_refs, down_refs = nested(first_refs, lengths[0]), nested(down_refs, lengths[1])
        near_ref, far_ref, token_ref, way_ref = rest[:4]
        active_refs, gate_refs, up_refs = rest[4:6], rest[6:8], rest[8:10]
        half = width // 2
        order = [pl.ds(k * share, share) for k in range(len(tokens) // 2)]
        collect(token_refs, token_ref, order)
        collect(way_refs, way_ref, order)
        lanes = [slice(0, half), slice(half, width)]
        for i in range(2):
            gate, upward = (
                sum(
                    crossed(token_ref[:, lanes[far]], across(first_refs[i][far], rows))
                    for far in range(2)
                )
                for rows in (gate_rows, up_rows)
            )
            sigma = sigmoid(gate)
            opened = gate * sigma
            active_refs[i][...] = (opened * upward).astype(LOW)
            grad = sum(
                crossed(way_ref[:, lanes[far]], across(down_refs[i][far], slice(None)))
                for far in range(2)
            )
            gate_refs[i][...] = (grad * upward * sigma * (1.0 + gate * (1.0 - sigma))).astype(LOW)
            up_refs[i][...] = (grad * opened).astype(LOW)
        for far in range(2):
            values = sum(
                straight(gate_refs[i][...], across(first_refs[i][far], gate_rows))
                + straight(up_refs[i][...], across(first_refs[i][far], up_rows))
                for i in range(2)
            )
            deal(near_ref, far_ref, values, order, lanes[far])

    inputs = list(tokens) + list(directions) + pieces[0] + pieces[1]
    out = jax.ShapeDtypeStruct((length, width), LOW)
    step = lambda lanes: pl.BlockSpec((length, lanes), lambda i: (i, 0))
    shape = lambda lanes: jax.ShapeDtypeStruct((2 * length, lanes), LOW)
    near, far, all_tokens, all_ways, *rest = call(
        kernel,
        inputs,
        [whole(item) for item in inputs],
        [whole(out)] * 2 + [step(width)] * 2 + [step(hidden)] * 6,
        [out] * 2 + [shape(width)] * 2 + [shape(hidden)] * 6,
        [],
        "column_ffn",
    )
    return near, far, all_tokens, all_ways, rest[:2], rest[2:4], rest[4:6]


def write_across(ref, rows, values):
    size, _, _, strip = ref.shape
    for z in range(size):
        for c in range(2):
            start = (2 * z + c) * strip
            ref[z, c, rows] = values[:, start : start + strip].astype(LOW)


def column_down(actives, ways, down, size, strip):
    hidden = actives[0].shape[1]
    tokens, width = ways.shape
    length = tokens // 2
    lengths = lengths_of(down)
    pieces = flat(down)

    def kernel(*refs):
        active_refs, way_ref = refs[:2], refs[2]
        down_refs = nested(refs[3 : 3 + len(pieces)], lengths)
        near_ref, far_ref = refs[3 + len(pieces) : 5 + len(pieces)]
        grad_refs = refs[5 + len(pieces) :]
        half = width // 2
        for far in range(2):
            lanes = slice(far * half, (far + 1) * half)
            values = sum(
                straight(active_refs[i][...], across(down_refs[i][far], slice(None)))
                for i in range(2)
            ).astype(LOW)
            near_ref[:, lanes] = values[:length]
            far_ref[:, lanes] = values[length:]
            for i in range(2):
                write_across(
                    grad_refs[2 * i + far],
                    slice(None),
                    turned(active_refs[i][...], way_ref[:, lanes]),
                )

    inputs = list(actives) + [ways] + pieces
    out = jax.ShapeDtypeStruct((length, width), LOW)
    grad = jax.ShapeDtypeStruct((size, 2, hidden, strip), LOW)
    near, far, *grads = call(
        kernel,
        inputs,
        [whole(item) for item in inputs],
        [whole(out)] * 2 + [whole(grad)] * 4,
        [out] * 2 + [grad] * 4,
        [],
        "column_down",
        grid=1,
    )
    return near, far, [grads[:2], grads[2:]]


def column_rows(chunks, rights, size, strip):
    rows = [lefts[0].shape[1] for lefts in chunks]
    width = rights.shape[1]

    def kernel(*refs):
        left_refs = refs[: 2 * len(chunks)]
        right_ref = refs[2 * len(chunks)]
        grad_refs = refs[2 * len(chunks) + 1 :]
        half = width // 2
        for i in range(2):
            for far in range(2):
                for n in range(len(chunks)):
                    start = sum(rows[:n])
                    write_across(
                        grad_refs[2 * i + far],
                        slice(start, start + rows[n]),
                        turned(
                            left_refs[2 * n + i][...], right_ref[:, far * half : (far + 1) * half]
                        ),
                    )

    inputs = [left for lefts in chunks for left in lefts] + [rights]
    grad = jax.ShapeDtypeStruct((size, 2, sum(rows), strip), LOW)
    grads = call(
        kernel,
        inputs,
        [whole(item) for item in inputs],
        [whole(grad)] * 4,
        [grad] * 4,
        [],
        "column_rows",
        grid=1,
    )
    return [grads[:2], grads[2:]]


def column_backward(
    grads, out_weights, mix_weights, beta_weights, seg_col, seg_row, conv, head_gain, order,
    saved, projected, beta_in,
):
    count, _, length = seg_row.shape
    lines = conv.shape[0]
    width = grads[0].shape[1]
    lengths = [lengths_of(out_weights), lengths_of(mix_weights)]
    pieces = [flat(out_weights), flat(mix_weights)]

    def kernel(*refs):
        token_refs, out_refs, mix_refs, rest = split_refs(
            refs, [len(grads), len(pieces[0]), len(pieces[1]), 20]
        )
        out_refs, mix_refs = nested(out_refs, lengths[0]), nested(mix_refs, lengths[1])
        beta_ref, col_ref, row_ref, conv_ref, head_ref, order_ref = rest[:6]
        inverse_ref, update_ref, mixed_ref, first_ref, second_ref, beta_in_ref = rest[6:12]
        signal_ref, beta_grad_ref, conv_grad_ref, head_grad_ref = rest[12:16]
        near_ref, far_ref, hold_ref = rest[16:]
        places = blocks_of(order_ref, length)
        collect(token_refs, hold_ref, places)
        half = width // 2
        lanes = [slice(0, half), slice(half, width)]
        masks = masks_of(col_ref[...], row_ref[0])
        kept = kept_of(col_ref[...], conv_ref.shape[0] // 3)
        head_grad = jnp.zeros((1, HEAD), WIDE)
        beta_grads = []
        for head, projected_ref in enumerate((first_ref, second_ref)):
            own = head_lanes(head)
            grad = sum(
                crossed(hold_ref[:, lanes[far]], across(out_refs[head][far], slice(None)))
                for far in range(2)
            )
            signal_grads, beta_grad, conv_lines, gain_grad = backward_head(
                [projected_ref[:, head_lanes(part)] for part in range(4)],
                beta_in_ref[:, head : head + 1],
                conv_ref[:, own],
                kept,
                masks,
                head_ref[...],
                inverse_ref[0, head],
                update_ref[:, own],
                mixed_ref[:, own],
                grad,
            )
            head_grad = head_grad + gain_grad
            beta_grads.append(beta_grad.astype(LOW).astype(WIDE))
            beta_grad_ref[:, head : head + 1] = beta_grad
            for line, values in enumerate(conv_lines):
                conv_grad_ref[0, line : line + 1, own] = values
            for part in range(4):
                signal_ref[:, head_lanes(4 * head + part)] = signal_grads[part]
        head_grad_ref[0] = head_grad
        for far in range(2):
            values = sum(
                crossed(
                    signal_ref[:, 4 * HEAD * head : 4 * HEAD * (head + 1)],
                    down_list(mix_refs[head][far]),
                )
                + beta_grads[head] * beta_ref[head : head + 1, lanes[far]].astype(WIDE)
                for head in range(2)
            )
            deal(near_ref, far_ref, values, places, lanes[far])

    inputs = (
        list(grads)
        + pieces[0]
        + pieces[1]
        + [beta_weights, seg_col, seg_row, conv, head_gain, order]
        + list(saved)
        + list(projected)
        + [beta_in]
    )
    in_specs = [whole(item) for item in inputs]
    step = lambda lanes: pl.BlockSpec((length, lanes), lambda i: (i, 0))
    in_specs[-11] = step(1)
    in_specs[-10] = pl.BlockSpec((1, 1, length), lambda i: (i, 0, 0))
    in_specs[-7] = pl.BlockSpec(memory_space=pltpu.SMEM)
    in_specs[-6:] = saved_specs(length) + [step(4 * HEAD), step(4 * HEAD), step(2)]
    out = jax.ShapeDtypeStruct((length, width), LOW)
    return call(
        kernel,
        inputs,
        in_specs,
        grad_specs(length, lines) + [whole(out)] * 2 + [step(width)],
        grad_shapes(count, length, lines)
        + [out] * 2
        + [jax.ShapeDtypeStruct((count * length, width), LOW)],
        [],
        "column_backward",
    )


def column_mix(mixer_in, signal_grads):
    width = mixer_in.shape[1]

    def kernel(mixer_ref, signal_ref, *grad_refs):
        half = width // 2
        for far in range(2):
            for head in range(2):
                grad_refs[2 * head + far][...] = turned(
                    mixer_ref[:, far * half : (far + 1) * half],
                    signal_ref[:, 4 * HEAD * head : 4 * HEAD * (head + 1)],
                ).astype(LOW)

    inputs = [mixer_in, signal_grads]
    grad = jax.ShapeDtypeStruct((width // 2, 4 * HEAD), LOW)
    grads = call(
        kernel,
        inputs,
        [whole(item) for item in inputs],
        [whole(grad)] * 4,
        [grad] * 4,
        [],
        "column_mix",
        grid=1,
    )
    return [grads[:2], grads[2:]]


def contract(left, right, left_dim, right_dim):
    return lax.dot_general(
        left, right, (((left_dim,), (right_dim,)), ((), ())), preferred_element_type=WIDE
    )


def after(values, earlier):
    return lax.optimization_barrier((values, earlier))[0]


def exclusive_order(blocks):
    place = lax.axis_index("dmod")
    for bit in (1, 2):
        flip = (place & bit) != 0
        blocks = [jnp.where(flip, blocks[i ^ bit], blocks[i]) for i in range(4)]
    return blocks


def trade(blocks):
    return [blocks[0]] + [
        lax.ppermute(blocks[m], "dmod", [(i, i ^ m) for i in range(4)]) for m in (1, 2, 3)
    ]


def gather_width(values):
    far = lax.ppermute(values, "dmod", ACROSS)
    near = lax.ppermute(values, "dmod", CORE)
    return [values, near, far, lax.ppermute(far, "dmod", CORE)]


def scatter_width(blocks):
    near = lax.ppermute(blocks[1].astype(LOW), "dmod", CORE)
    cross = lax.ppermute(blocks[3].astype(LOW), "dmod", CORE)
    far = lax.ppermute((blocks[2] + cross.astype(WIDE)).astype(LOW), "dmod", ACROSS)
    return blocks[0] + near.astype(WIDE) + far.astype(WIDE)


def sum_pair(values):
    low = values.astype(LOW)
    return low.astype(WIDE) + lax.ppermute(low, "mp", SWAP).astype(WIDE)


def row_total(values):
    return lax.psum(values, "dmod")


class Ring:
    def __init__(self):
        self.size = lax.axis_size("dp")
        self.parts = 1

    def order(self, values):
        return values

    def gather(self, values):
        return [lax.all_gather(values, "dp", axis=1, tiled=True)]

    def scatter(self, make):
        return lax.psum_scatter(
            make(0).astype(LOW), "dp", scatter_dimension=1, tiled=True
        ).astype(WIDE)


def plane_body(
    block_input,
    segment_ids,
    group_ids,
    group_weight,
    mixer_norm,
    w_mix,
    w_beta,
    conv_kernel,
    head_norm,
    w_out,
    ffn_norm,
    w_ffn_in,
    w_ffn_down,
    cotangent,
):
    ring = Ring()
    parts = ring.parts
    micro, seqs, length, width = block_input.shape
    tokens = micro * seqs * length
    block = width // parts
    strip = w_mix.shape[0]
    span = w_mix.shape[2] // 4
    hidden = w_ffn_in.shape[2] // 4
    dmod = lax.axis_index("dmod")
    data_size = ring.size
    place = lax.axis_index("dp")

    lines = conv_kernel.shape[0] * conv_kernel.shape[1]
    pack = jnp.concatenate(
        [
            conv_kernel.reshape(-1),
            head_norm,
            mixer_norm,
            ffn_norm,
            w_beta.T.reshape(-1),
        ]
    )
    packs = lax.all_gather(pack, "dp", axis=0)
    sizes = [conv_kernel.size, head_norm.size, strip, strip, w_beta.size]
    cuts = [sum(sizes[:i]) for i in range(6)]
    conv = (
        packs[:, cuts[0] : cuts[1]]
        .reshape(data_size, lines, -1)
        .transpose(1, 0, 2)
        .reshape(lines, span)
        .astype(WIDE)
    )
    head_gain = packs[:, cuts[1] : cuts[2]].reshape(1, -1).astype(WIDE)
    gain_one = ring.order(packs[:, cuts[2] : cuts[3]].reshape(1, -1).astype(WIDE))
    gain_two = ring.order(packs[:, cuts[3] : cuts[4]].reshape(1, -1).astype(WIDE))
    beta_weights = ring.order(
        packs[:, cuts[4] : cuts[5]]
        .reshape(data_size, -1, strip)
        .transpose(1, 0, 2)
        .reshape(-1, width)
    )

    out_rows = jnp.concatenate(exclusive_order(jnp.split(w_out, 4, axis=0)), 0)
    out_halves = jnp.split(out_rows.T, 2, axis=1)
    mix_own = jnp.stack(trade(exclusive_order(jnp.split(w_mix, 4, axis=2))))
    mix_halves = [
        mix_own[:, :, :, head * HEAD : (head + 1) * HEAD].reshape(4, strip, 4 * HEAD)
        for head in (0, 1)
    ]
    ffn_own = jnp.stack(trade(exclusive_order(jnp.split(w_ffn_in, 4, axis=2))))
    ffn_halves = [ffn_own[:, :, 0], ffn_own[:, :, 1]]
    down_own = trade(exclusive_order(jnp.split(w_ffn_down, 4, axis=0)))
    down_halves = [
        jnp.stack([down_own[0].T, down_own[1].T]),
        jnp.stack([down_own[2].T, down_own[3].T]),
    ]

    def chain(half):
        first = ring.gather(out_halves[half][None])
        second = ring.gather(after(mix_halves[half], first[-1]))
        third = ring.gather(after(ffn_halves[half], second[-1]))
        fourth = ring.gather(after(down_halves[half], third[-1]))
        return first, second, third, fourth

    chains = [chain(0), chain(1)]
    out_weights = jnp.concatenate(
        [
            jnp.concatenate([part[0] for part in chains[0][0]], 0),
            jnp.concatenate([part[0] for part in chains[1][0]], 0),
        ],
        1,
    )
    mix_parts = [[part.reshape(4 * block, -1) for part in each[1]] for each in chains]
    ffn_parts = [[part.reshape(4 * block, -1) for part in each[2]] for each in chains]
    down_parts = [[part.reshape(2 * block, -1) for part in each[3]] for each in chains]

    marks = (group_ids.reshape(tokens, 1) == jnp.arange(group_weight.shape[0])[None]).astype(WIDE)
    counts = lax.psum(jnp.sum(marks, 0), "dp")
    table = group_weight * (tokens * data_size / group_weight.shape[0]) / counts
    scales = jnp.sum(marks * table, -1, keepdims=True)
    direction = ring.order(cotangent.reshape(tokens, width).astype(WIDE)) * scales
    direction_low = direction.astype(LOW)

    def by_part(slots):
        return [
            jnp.concatenate([slot[:, k * block : (k + 1) * block] for slot in slots], 1)
            for k in range(parts)
        ]

    def by_slot(pieces):
        return [
            jnp.concatenate([piece[:, m * block : (m + 1) * block] for piece in pieces], 1)
            for m in range(pieces[0].shape[1] // block)
        ]

    direction_parts = by_part(gather_width(direction_low))

    rows = ring.order(block_input.reshape(tokens, width).astype(WIDE))
    first_scale = lax.rsqrt(row_total(jnp.sum(rows * rows, -1, keepdims=True)) / D + 1e-06)
    mixer_in = (rows * first_scale * gain_one).astype(LOW)
    mixer_parts = by_part(gather_width(mixer_in))
    projected = [
        sum(jnp.dot(mixer_parts[k], mix_parts[half][k], preferred_element_type=WIDE) for k in range(parts))
        for half in (0, 1)
    ]
    beta_all = row_total(contract(beta_weights, mixer_in, 1, 1))
    heads = span // HEAD
    beta_in = lax.dynamic_slice_in_dim(beta_all, dmod * heads, heads, 0).T
    seg_col = segment_ids.reshape(tokens, 1)
    seg_row = segment_ids.reshape(micro * seqs, 1, length)
    mixer_args = list(projected) + [
        beta_in, seg_col, seg_row, conv, head_gain
    ]
    gated, *saved = mixer_forward(mixer_args)
    gated_all = jnp.concatenate(gather_width(gated), 1)
    middle = rows + sum_pair(contract(gated_all, out_weights, 1, 1))

    second_scale = lax.rsqrt(row_total(jnp.sum(middle * middle, -1, keepdims=True)) / D + 1e-06)
    ffn_in = (middle * second_scale * gain_two).astype(LOW)
    ffn_in_parts = by_part(gather_width(ffn_in))
    gate, upward = (
        sum(jnp.dot(ffn_in_parts[k], ffn_parts[half][k], preferred_element_type=WIDE) for k in range(parts))
        for half in (0, 1)
    )
    sigma = sigmoid(gate)
    active = (gate * sigma * upward).astype(LOW)
    down_slots = sum(
        (
            by_slot([contract(active, down_parts[half][k], 1, 1) for k in range(parts)])
            for half in (0, 1)
        ),
        [],
    )
    result = middle + sum_pair(scatter_width(down_slots))
    out = ring.order(result).astype(LOW).reshape(block_input.shape)

    down_grads = [
        ring.scatter(
            lambda k: contract(
                direction_parts[k][:, 2 * half * block : 2 * (half + 1) * block], active, 0, 0
            ).reshape(2, block, hidden)
        )
        for half in (0, 1)
    ]
    active_grad = sum(
        jnp.dot(
            direction_parts[k][:, 2 * half * block : 2 * (half + 1) * block],
            down_parts[half][k],
            preferred_element_type=WIDE,
        )
        for k in range(parts)
        for half in (0, 1)
    )
    gate_grad = (active_grad * upward * sigma * (1.0 + gate * (1.0 - sigma))).astype(LOW)
    upward_grad = (active_grad * gate * sigma).astype(LOW)
    ffn_slots = by_slot(
        [
            contract(gate_grad, ffn_parts[0][k], 1, 1) + contract(upward_grad, ffn_parts[1][k], 1, 1)
            for k in range(parts)
        ]
    )
    ffn_grads = [
        ring.scatter(lambda k: contract(ffn_in_parts[k], grad, 0, 0).reshape(4, block, hidden))
        for grad in (gate_grad, upward_grad)
    ]
    ffn_in_grad = sum_pair(scatter_width(ffn_slots))
    weighted_two = ffn_in_grad * gain_two
    norm_two_grad = jnp.sum(ffn_in_grad * middle * second_scale, 0)
    inner_two = row_total(jnp.sum(weighted_two * middle, -1, keepdims=True))
    middle_grad = (
        direction + second_scale * weighted_two - middle * (second_scale**3 * inner_two / D)
    )

    branch_low = middle_grad.astype(LOW)
    out_grads = [
        ring.scatter(
            lambda k: contract(
                branch_low[:, k * block : (k + 1) * block],
                gated_all[:, 2 * half * span : 2 * (half + 1) * span],
                0,
                0,
            )[None]
        )
        for half in (0, 1)
    ]
    gated_slots = jnp.split(jnp.dot(branch_low, out_weights, preferred_element_type=WIDE), 4, axis=1)
    gated_grad = scatter_width(gated_slots)
    projected_grad, beta_grad, conv_grad, head_grad = mixer_backward(
        mixer_args, saved, gated_grad
    )
    projected_slots = gather_width(projected_grad)
    mix_grads = [
        ring.scatter(
            lambda k: contract(
                mixer_in[:, k * block : (k + 1) * block],
                jnp.concatenate(projected_slots[2 * half : 2 * half + 2], 1),
                0,
                0,
            )[None]
        )
        for half in (0, 1)
    ]
    beta_slots = jnp.concatenate(
        exclusive_order(gather_width(beta_grad.T.astype(LOW))), 0
    )
    beta_weight_grad = contract(beta_slots, mixer_in, 1, 0)
    mixer_slots = by_slot(
        [
            contract(projected_grad[:, : 2 * span], mix_parts[0][k], 1, 1)
            + contract(projected_grad[:, 2 * span :], mix_parts[1][k], 1, 1)
            for k in range(parts)
        ]
    )
    mixer_grad = sum_pair(scatter_width(mixer_slots) + contract(beta_slots, beta_weights, 0, 0))
    weighted_one = mixer_grad * gain_one
    norm_one_grad = jnp.sum(mixer_grad * rows * first_scale, 0)
    inner_one = row_total(jnp.sum(weighted_one * rows, -1, keepdims=True))
    grad_input = ring.order(
        middle_grad + first_scale * weighted_one - rows * (first_scale**3 * inner_one / D)
    ).reshape(block_input.shape)

    head_total = lax.psum(jnp.sum(head_grad, (0, 1)), ("dp", "mp", "dmod"))
    head_out = lax.dynamic_slice_in_dim(head_total, place * head_norm.size, head_norm.size, 0)
    small = jnp.concatenate(
        [
            jnp.sum(conv_grad, 0),
            ring.order(jnp.stack([norm_one_grad, norm_two_grad]))
            .reshape(2, data_size, -1)
            .transpose(1, 0, 2)
            .reshape(data_size, -1)
            .reshape(-1)
            .reshape(-1, span),
            ring.order(beta_weight_grad)
            .reshape(-1, data_size, strip)
            .transpose(1, 0, 2)
            .reshape(-1, span),
        ],
        0,
    )
    conv_part = (
        small[:lines].reshape(lines, data_size, -1).transpose(1, 0, 2).reshape(data_size, -1)
    )
    norm_part = small[lines : lines + 2 * width // span].reshape(data_size, -1)
    beta_part = small[lines + 2 * width // span :].reshape(data_size, -1)
    small_own = lax.psum_scatter(
        jnp.concatenate([conv_part, norm_part, beta_part], 1), "dp", scatter_dimension=0
    )
    conv_out = small_own[: conv_kernel.size].reshape(conv_kernel.shape)
    norm_one_out = small_own[conv_kernel.size : conv_kernel.size + strip]
    norm_two_out = small_own[conv_kernel.size + strip : conv_kernel.size + 2 * strip]
    beta_out = small_own[conv_kernel.size + 2 * strip :].reshape(-1, strip).T

    def placed(blocks):
        return exclusive_order(trade([values.astype(LOW) for values in blocks]))

    ffn_out = jnp.stack(
        [
            jnp.concatenate([values.astype(WIDE) for values in placed(list(grad))], 1)
            for grad in ffn_grads
        ],
        1,
    )
    down_out = jnp.concatenate(
        [
            values.astype(WIDE).T
            for values in placed(list(down_grads[0]) + list(down_grads[1]))
        ],
        0,
    )
    out_out = jnp.concatenate(
        exclusive_order(jnp.split(jnp.concatenate([grad[0] for grad in out_grads], 1).T, 4, axis=0)),
        0,
    )
    mix_blocks = sum((jnp.split(grad[0], 2, axis=1) for grad in mix_grads), [])
    mix_out = jnp.concatenate(
        [
            values.reshape(strip, 2, 4, HEAD).transpose(0, 2, 1, 3).reshape(strip, 4, span)
            for values in exclusive_order(mix_blocks)
        ],
        2,
    )
    return (
        out,
        grad_input,
        norm_one_out,
        mix_out,
        beta_out,
        conv_out,
        head_out,
        out_out,
        norm_two_out,
        ffn_out,
        down_out,
    )


def exchange(values, axis):
    return lax.all_to_all(values, axis, 0, 0, tiled=True)


def swap_mp(values):
    return lax.ppermute(values, "mp", SWAP)


def swap_core(values):
    return lax.ppermute(values, "dmod", CORE)


def swap_across(values):
    return lax.ppermute(values, "dmod", ACROSS)


def swap_dp(values, k):
    return lax.ppermute(values, "dp", [(i, i ^ k) for i in range(lax.axis_size("dp"))])


def trade_blocks(blocks, axis, place):
    size = len(blocks)
    blocks = by_difference(blocks, place)
    moved = [blocks[0]] + [
        lax.ppermute(blocks[k], axis, [(i, i ^ k) for i in range(size)]) for k in range(1, size)
    ]
    return by_difference(moved, place)


def by_difference(blocks, place):
    bit = 1
    while bit < len(blocks):
        flip = (place & bit) != 0
        blocks = [jnp.where(flip, blocks[i ^ bit], blocks[i]) for i in range(len(blocks))]
        bit *= 2
    return blocks


def everyone(values, place):
    size = lax.axis_size("dp")
    values = values[None]
    bit = 1
    while bit < size:
        values = jnp.concatenate(turn((place & bit) != 0, (values, swap_dp(values, bit))), 0)
        bit *= 2
    return values


def turn(flag, pair):
    return jnp.where(flag, pair[1], pair[0]), jnp.where(flag, pair[0], pair[1])


def chip_blocks(core, pair):
    keep, send = turn(core, pair)
    return jnp.stack(turn(core, (keep, swap_core(send))), 1)


def along_column(core, pair, earlier=None):
    both = chip_blocks(core, pair)
    if earlier is not None:
        both = after(both, earlier)
    return exchange(both, "dp")


def gather_columns(values, earlier=None, later=None):
    if earlier is not None:
        values = after(values, earlier)
    half = values.shape[0] // 2
    over = swap_mp(values)
    far = swap_across(values)
    corner = (over[:half], far[half:])
    if later is not None:
        corner = after(corner, later)
    both = [swap_across(corner[0]), swap_mp(corner[1])]
    return [[[values], [far]], [[over], both]]


def wide(values):
    return values.astype(WIDE)


def scatter_columns(grid):
    half = grid[0][0].shape[0] // 2
    sent = swap_mp(jnp.concatenate([grid[1][0][:half], grid[1][1][:half]], 0))
    top = wide(grid[0][1][:half]) + wide(sent[half:])
    top = wide(grid[0][0][:half]) + wide(sent[:half]) + wide(swap_across(top.astype(LOW)))
    rest = grid[0][0].shape[0] - half
    sent = swap_across(jnp.concatenate([grid[0][1][half:], grid[1][1][half:]], 0))
    low = wide(grid[1][0][half:]) + wide(sent[rest:])
    low = wide(grid[0][0][half:]) + wide(sent[:rest]) + wide(swap_mp(low.astype(LOW)))
    return jnp.concatenate([top, low], 0).astype(LOW)


def column_blocks(values):
    mine = [values] + [swap_dp(values, k) for k in range(1, lax.axis_size("dp"))]
    return mine + [swap_core(block) for block in mine]


def column_total(near, far):
    size = lax.axis_size("dp")
    share = near.shape[0] // size
    chip = wide(near) + wide(swap_core(far))
    total = chip[:share]
    low = [chip[k * share : (k + 1) * share].astype(LOW) for k in range(1, size)]
    for k in range(1, size):
        total = total + wide(swap_dp(low[k - 1], k))
    return total, low[0]


def column_body(
    block_input,
    segment_ids,
    group_ids,
    group_weight,
    mixer_norm,
    w_mix,
    w_beta,
    conv_kernel,
    head_norm,
    w_out,
    ffn_norm,
    w_ffn_in,
    w_ffn_down,
    cotangent,
):
    place = lax.axis_index("dp")
    size = lax.axis_size("dp")
    side = lax.axis_index("mp")
    dmod = lax.axis_index("dmod")
    row, core = dmod // 2, dmod % 2
    at_far_side, at_far_row, at_core = side == 1, row == 1, core == 1
    micro, _, length, width = block_input.shape
    share = length // size
    strip = w_mix.shape[0]
    groups = group_weight.shape[0]
    group_heads = w_beta.shape[1]
    hidden = w_ffn_down.shape[0] // (2 * size)
    span = 2 * width

    def to_column(values):
        lead = values.shape[:-1]
        values = values.reshape(lead + (2, 2, size, strip))
        values = jnp.swapaxes(values, -2, -3).reshape(lead + (2, span))
        return jnp.concatenate(turn(at_far_row, (values[..., 0, :], values[..., 1, :])), -1)

    def from_column(values):
        lead = values.shape[:-1]
        halves_of = turn(at_far_row, (values[..., :span], values[..., span:]))
        values = jnp.stack(halves_of, -2).reshape(lead + (2, size, 2, strip))
        return jnp.swapaxes(values, -2, -3).reshape(lead + (2 * span,))

    def tokens_in(values):
        values = values.reshape(micro, size, share, width)
        moved = trade_blocks([values[:, z] for z in range(size)], "dp", place)
        moved = jnp.where(at_far_side, jnp.stack(moved[2:]), jnp.stack(moved[:2]))
        moved = moved.reshape(4, share, width)
        moved = trade_blocks([moved[j] for j in range(4)], "dmod", dmod)
        return to_column(jnp.concatenate(moved, 1))

    def tokens_out(values):
        blocks = jnp.split(from_column(values), 4, axis=1)
        moved = jnp.stack(trade_blocks(blocks, "dmod", dmod)).reshape(2, micro, share, width)
        moved = jnp.concatenate(turn(at_far_side, (moved, swap_mp(moved))), 0)
        moved = trade_blocks([moved[z] for z in range(size)], "dp", place)
        return jnp.stack(moved, 1).reshape(block_input.shape)

    blocks = w_mix.reshape(strip, 4, 2, size, HEAD).transpose(2, 3, 0, 1, 4)
    blocks = blocks.reshape(2, size, strip, 4 * HEAD)
    mix_blocks = chip_blocks(at_core, (blocks[0], blocks[1]))
    block_input, w_out, w_ffn_in, w_ffn_down, conv_kernel = after(
        (block_input, w_out, w_ffn_in, w_ffn_down, conv_kernel), mix_blocks
    )
    mix_pieces = exchange(mix_blocks, "dp")
    tokens_low = tokens_in(block_input)
    rows = wide(tokens_low)
    mix_weights = gather_columns(mix_pieces)
    mix_weights = [
        [[item.reshape(-1, 4 * HEAD) for item in items] for items in pair] for pair in mix_weights
    ]
    token_blocks = column_blocks(tokens_low)
    out_pieces = along_column(
        at_core, tuple(w_out.reshape(2, size, HEAD, strip)), (mix_pieces, token_blocks[3])
    )
    ffn_rows = w_ffn_in.transpose(1, 2, 0).reshape(2, 2, size, hidden, strip)
    blocks = jnp.concatenate([ffn_rows[0], ffn_rows[1]], 2)
    first_pieces = along_column(at_core, (blocks[0], blocks[1]), out_pieces)
    out_weights = gather_columns(out_pieces, mix_weights[1][1])

    small = [
        conv_kernel.reshape(-1),
        head_norm,
        mixer_norm,
        ffn_norm,
        w_beta.T.reshape(-1),
        segment_ids.reshape(-1).astype(LOW),
        group_ids.reshape(-1).astype(LOW),
    ]
    count = sum(item.size for item in small)
    pack = jnp.concatenate(small + [jnp.zeros((-count % HEAD,), LOW)]).reshape(-1, HEAD)
    packs = everyone(pack, place)
    packs = jnp.stack(turn(at_far_side, (packs, swap_mp(packs))))
    packs = jnp.stack(turn(at_core, (packs, swap_core(packs))))
    packs = jnp.stack(turn(at_far_row, (packs, swap_across(packs))))
    packs = packs.reshape(2, 2, 2, size, -1)
    fields = []
    start = 0
    for item in small:
        fields.append(packs[..., start : start + item.size])
        start += item.size
    lines = conv_kernel.shape[0] * conv_kernel.shape[1]
    heads = 2 * group_heads
    local_head = size * core + place
    own_heads = [group_heads * side + local_head, group_heads * (1 - side) + local_head]
    conv_all = (
        fields[0]
        .reshape(2, 2, 2, size, lines, -1)
        .transpose(4, 2, 0, 1, 3, 5)
        .reshape(lines, heads * HEAD)
    )
    conv = wide(
        jnp.concatenate(
            [lax.dynamic_slice_in_dim(conv_all, head * HEAD, HEAD, 1) for head in own_heads], 1
        )
    )
    head_gain = wide(fields[1][0, 0, 0].reshape(1, HEAD))
    gain_one = to_column(wide(fields[2][:, :, 0].reshape(1, -1)))
    gain_two = to_column(wide(fields[3][:, :, 0].reshape(1, -1)))
    beta_rows = (
        fields[4]
        .reshape(2, 2, 2, size, group_heads, strip)
        .transpose(2, 4, 0, 1, 3, 5)
        .reshape(heads, -1)
    )
    beta_weights = to_column(
        jnp.concatenate([lax.dynamic_slice_in_dim(beta_rows, head, 1, 0) for head in own_heads], 0)
    )
    sequence = 2 * side + row
    segments = lax.dynamic_index_in_dim(fields[5][0, 0, 0], sequence, 0, keepdims=False)
    segments = segments.reshape(micro, length).astype(jnp.int32)
    segments = jnp.concatenate(turn(at_core, (segments[:1], segments[1:])), 0)
    seg_col = segments.reshape(-1, 1)
    seg_row = segments.reshape(micro, 1, length)
    all_groups = fields[6][0, 0, 0].reshape(-1).astype(jnp.int32)
    names = jnp.arange(groups, dtype=jnp.int32)
    counts = jnp.sum((all_groups[:, None] == names[None]).astype(WIDE), 0)
    table = group_weight * (all_groups.shape[0] / groups) / counts
    own_groups = lax.dynamic_slice_in_dim(
        all_groups, (sequence * micro + core) * length + place * share, share, 0
    )
    scales = jnp.sum((own_groups[:, None] == names[None]).astype(WIDE) * table, -1, keepdims=True)

    order = jnp.arange(size, dtype=jnp.int32) ^ place
    constants = [beta_weights, seg_col, seg_row, conv, head_gain, order]
    gated, inverse, update, mixed, mixer_in, *projected, beta_in = column_forward(
        token_blocks, mix_weights, gain_one, *constants
    )
    branch, mark = column_total(*column_branch(gated, out_weights, order, length))
    first_weights = gather_columns(first_pieces, mix_weights[1][1], gated)
    middle = rows + branch

    second_scale = lax.rsqrt(jnp.mean(middle * middle, -1, keepdims=True) + 1e-06)
    ffn_low = (middle * second_scale * gain_two).astype(LOW)
    ffn_blocks = column_blocks(ffn_low)
    down_pieces = along_column(
        at_core, tuple(w_ffn_down.reshape(2, size, hidden, strip)), (first_pieces, ffn_low)
    )
    down_weights = gather_columns(down_pieces, first_weights[1][1])
    direction = wide(tokens_in(after(cotangent, token_blocks[3]))) * scales
    direction_blocks = column_blocks(after(direction.astype(LOW), ffn_blocks[3]))
    near, far, ffn_in, directions, actives, gate_grads, up_grads = column_ffn(
        ffn_blocks, direction_blocks, first_weights, down_weights, hidden
    )
    ffn_in_grad, mark = column_total(near, far)
    near, far, down_grads = column_down(
        after(actives, mark), directions, down_weights, size, strip
    )
    ffn_grads = column_rows([after(gate_grads, mark), up_grads], ffn_in, size, strip)

    def placed(grid, earlier=None):
        total = scatter_columns(grid)
        return along_column(at_core, (total[:, 0], total[:, 1]), earlier)

    def stacked(pieces):
        return pieces.transpose(1, 0, 2, 3).reshape(2 * size, -1, strip)

    weighted_two = ffn_in_grad * gain_two
    norm_two_grad = jnp.sum(ffn_in_grad * middle * second_scale, 0, keepdims=True)
    inner_two = jnp.mean(weighted_two * middle, -1, keepdims=True)
    middle_grad = (
        direction + second_scale * weighted_two - middle * (second_scale**3 * inner_two)
    )
    branch_low = middle_grad.astype(LOW)
    branch_blocks = column_blocks(branch_low)
    down_pieces = placed(down_grads, branch_blocks[3])
    ffn_pieces = placed(ffn_grads, down_pieces)
    down_out = wide(stacked(down_pieces).reshape(-1, strip))
    ffn_out = stacked(ffn_pieces).reshape(2 * size, 2, hidden, strip)
    ffn_out = wide(ffn_out.transpose(1, 0, 2, 3).reshape(2, -1, strip).transpose(2, 0, 1))
    down_sum, _ = column_total(near, after(far, branch_blocks[3]))
    out = tokens_out((middle + down_sum).astype(LOW))

    signal_grads, beta_grad, conv_grad, head_grad, near, far, branch_all = column_backward(
        branch_blocks,
        out_weights,
        mix_weights,
        *constants,
        (inverse, update, mixed),
        projected,
        beta_in,
    )
    mix_grads = column_mix(mixer_in, signal_grads)
    mixer_grad, _ = column_total(near, far)
    gated_heads = [gated[:, :HEAD], gated[:, HEAD:]]
    out_grads = column_rows(
        [after(gated_heads, mix_grads[1][1])], branch_all, size, strip
    )
    out_pieces = placed(out_grads, ffn_pieces)
    out_out = wide(stacked(out_pieces).reshape(-1, strip))
    mix_total = scatter_columns(mix_grads).reshape(size, 2, strip, 4 * HEAD)
    mix_pieces = along_column(
        at_core, (mix_total[:, 0], mix_total[:, 1]), out_pieces
    )
    mix_out = wide(
        mix_pieces.reshape(size, 2, strip, 4, HEAD).transpose(2, 3, 1, 0, 4).reshape(strip, 4, -1)
    )
    beta_weight_grad = contract(beta_grad.astype(LOW), mixer_in, 0, 0)
    weighted_one = mixer_grad * gain_one
    first_scale = lax.rsqrt(jnp.mean(rows * rows, -1, keepdims=True) + 1e-06)
    norm_one_grad = jnp.sum(mixer_grad * rows * first_scale, 0, keepdims=True)
    inner_one = jnp.mean(weighted_one * rows, -1, keepdims=True)
    grad_input = wide(
        tokens_out(
            (
                middle_grad + first_scale * weighted_one - rows * (first_scale**3 * inner_one)
            ).astype(LOW)
        )
    )

    def over_columns(values):
        values = values + swap_mp(values)
        return values + swap_across(values)

    conv_sides = jnp.stack(turn(at_far_side, jnp.split(jnp.sum(conv_grad, 0), 2, axis=1)))
    beta_sides = from_column(
        jnp.concatenate(turn(at_far_side, (beta_weight_grad[:1], beta_weight_grad[1:])), 0)
    )
    vector = jnp.concatenate(
        [
            conv_sides.reshape(-1, HEAD),
            beta_sides.reshape(-1, HEAD),
            from_column(norm_two_grad).reshape(-1, HEAD),
            jnp.sum(head_grad, 0),
        ]
    )
    vector = over_columns(vector)
    vectors = jnp.stack(turn(at_core, (vector, swap_core(vector))))
    vectors = everyone(vectors, place)
    ends = [2 * lines, 2 * lines + 4 * span // HEAD]
    ends.append(ends[1] + 2 * span // HEAD)
    own_width = dmod * width + place * strip
    taps_own = conv_kernel.shape[2]
    at = (dmod * size + place) * taps_own
    conv_head = at // HEAD
    conv_out = lax.dynamic_slice(
        vectors,
        (conv_head % size, conv_head // size, side * lines, at % HEAD),
        (1, 1, lines, taps_own),
    ).reshape(conv_kernel.shape)
    beta_out = (
        lax.dynamic_slice(
            vectors[:, :, ends[0] : ends[1]].reshape(size, 2, 2, 2 * span),
            (0, 0, side, own_width),
            (size, 2, 1, strip),
        )
        .reshape(size, 2, strip)
        .transpose(2, 1, 0)
        .reshape(strip, group_heads)
    )
    sums = jnp.sum(vectors[:, :, ends[1] :], (0, 1))
    norm_two_out = lax.dynamic_slice_in_dim(sums[:-1].reshape(-1), own_width, strip, 0)
    head_out = lax.dynamic_slice_in_dim(sums[-1], place * head_norm.size, head_norm.size, 0)
    last = over_columns(from_column(norm_one_grad).reshape(-1, HEAD))
    last = last + swap_core(last)
    bit = 1
    while bit < size:
        last = last + swap_dp(last, bit)
        bit *= 2
    last = last.reshape(-1)
    norm_one_out = lax.dynamic_slice_in_dim(last, own_width, strip, 0)
    return (
        out,
        grad_input,
        norm_one_out,
        mix_out,
        beta_out,
        conv_out,
        head_out,
        out_out,
        norm_two_out,
        ffn_out,
        down_out,
    )


def solution(mesh):
    sizes = dict(mesh.shape)
    columns = sizes["mp"] * sizes["dmod"] // 2
    body = column_body if columns == sizes["dp"] else plane_body
    wide = P(("dmod", "dp"))
    tokens = P(None, "dp", None, "dmod")
    weights = (
        wide,
        P(("dmod", "dp"), None, "mp"),
        P(("dmod", "dp"), "mp"),
        P(None, None, ("mp", "dmod", "dp")),
        P("dp"),
        P("mp", ("dmod", "dp")),
        wide,
        P(("dmod", "dp"), None, "mp"),
        P("mp", ("dmod", "dp")),
    )
    ids = P(None, "dp", None)
    return jax.shard_map(
        body,
        mesh=mesh,
        in_specs=(tokens, ids, ids, P()) + weights + (tokens,),
        out_specs=(tokens, tokens) + weights,
        check_vma=False,
    )
```

time: 724 us -> 650 us (0.90)
  blocking collectives: 187 us -> 0 us
  starting transfers between devices: 37.5 us -> 152 us
  local copies, waits for them, and re-layouts: 133 us -> 59 us
  waiting for transfers between devices: 214 us -> 280 us
  matrix products: 64 us -> 0.42 us
  Pallas kernels: 27.3 us -> 74.8 us
  other arithmetic: 32.8 us -> 70.6 us
  between operations: 16.3 us -> 3.89 us
    ppermute x52 -> x125, waiting for transfers between devices: 114 us -> 229 us  [the longest x30 133 us: swap_dp(): lax.ppermute(values, 'dp', [(i, i ^ k) for i in range(lax.axis_size('dp'))])]
    psum x7 -> x0, blocking collectives: 106 us -> none  [the longest x1 57.4 us: body(): head_total = lax.psum(jnp.sum(head_grad, (0, 1)), ('dp', 'mp', 'dmod'))]
    all_gather x6 -> x0, waiting for transfers between devices: 73.6 us -> none  [gather(): return [lax.all_gather(values, 'dp', axis=1, tiled=True)]]
    unnamed x159 -> x281, local copies, waits for them, and re-layouts: 84.9 us -> 16 us
    ppermute x52 -> x125, starting transfers between devices: 36.1 us -> 104 us  [the longest x30 41.1 us: swap_dp(): lax.ppermute(values, 'dp', [(i, i ^ k) for i in range(lax.axis_size('dp'))])]
    all_to_all x0 -> x8, waiting for transfers between devices: none -> 51.5 us  [exchange(): return lax.all_to_all(values, axis, 0, 0, tiled=True)]
    pallas_call x2 -> x8, Pallas kernels: 27.3 us -> 74.8 us  [call(): pl.pallas_call(kernel, grid=(grid,), in_specs=in_specs, out_specs=out_spe...]
    all_to_all x0 -> x8, starting transfers between devices: none -> 47.5 us  [exchange(): return lax.all_to_all(values, axis, 0, 0, tiled=True)]
  transfers between devices with their start and end apart: 66 -> 133, of which waited for: 25 -> 56; matrix products, arithmetic and copies ran while one was open for 28% -> 16% of each run, Pallas kernels for 4% -> 9%
where the time goes in v2:
time: 650 us; the launch traced here: 641 us
  waiting for transfers between devices  280 us (43%)
  starting transfers between devices  152 us (23%)
  Pallas kernels  74.8 us (12%)
  other arithmetic  70.6 us (11%)
  local copies, waits for them, and re-layouts  59 us (9%)
    ppermute x30, waiting for transfers between devices, swap_dp(): lax.ppermute(values, 'dp', [(i, i ^ k) for i in range(lax.axis_size('dp'))])  133 us
    pallas_call x8, Pallas kernels, call(): pl.pallas_call(kernel, grid=(grid,), in_specs=in_specs, out_specs=out_spe...  74.8 us
    all_to_all x8, waiting for transfers between devices, exchange(): return lax.all_to_all(values, axis, 0, 0, tiled=True)  51.5 us
    all_to_all x8, starting transfers between devices, exchange(): return lax.all_to_all(values, axis, 0, 0, tiled=True)  47.5 us
    ppermute x30, starting transfers between devices, swap_dp(): lax.ppermute(values, 'dp', [(i, i ^ k) for i in range(lax.axis_size('dp'))])  41.1 us
    ppermute x21, waiting for transfers between devices, swap_mp(): return lax.ppermute(values, 'mp', SWAP)  40.4 us
    ppermute x24, waiting for transfers between devices, trade_blocks(): lax.ppermute(blocks[k], axis, [(i, i ^ k) for i in range(size)])  25.7 us
    ppermute x24, starting transfers between devices, trade_blocks(): lax.ppermute(blocks[k], axis, [(i, i ^ k) for i in range(size)])  22.9 us
  transfers between devices with their start and end apart: 133, of which 56 were waited for; matrix products, arithmetic and copies ran while one was open for 16% of the time, Pallas kernels for 9%

profile of v2, /device:TPU:16, one launch (start us, length us, event | category | flops | bytes accessed | tf_op | source)
XLA Modules:
  0.0 640.6 jit_solution(1736080037968927268)
XLA Ops:
  6.3 5.3 all-to-all-start
  23.1 7.8 %collective-permute-done.18 = bf16[1,25,128]{2,1,0:T(8,128)(2,1)S(1)} collective-permute-done((bf16[1,25,128]{2,1,0:T(8,128)(2,1)S(1)}, bf16[1,25,128]{2,1,0:T(8,128)(2,1)S(1)}, u32[]{:S(2)}, u32[]{:S(2)}) %collective-permute-start.18) | collective-permute-done | bytes 6432 | tf_op jit(solution)/shard_map/ppermute | solution.py:1173
  64.8 23.3 %collective-permute-done.15 = bf16[4,2,128,512]{3,2,1,0:T(8,128)(2,1)S(1)} collective-permute-done((bf16[4,2,128,512]{3,2,1,0:T(8,128)(2,1)}, bf16[4,2,128,512]{3,2,1,0:T(8,128)(2,1)S(1)}, u32[]{:S(2)}, u32[]{:S(2)}) %collective-permute-start.15) | collective-permute-done | bytes 1048608 | tf_op jit(solution)/shard_map/ppermute | solution.py:1161
  95.2 5.4 all-to-all-start.1
  102.6 8.0 %all-to-all-done.1.refs_1_.refs_8_ = bf16[4,2,128,128]{3,2,1,0:T(8,128)(2,1)S(1)} async-done(((bf16[4,2,128,128]{3,2,1,0:T(8,128)(2,1)}), bf16[4,2,128,128]{3,2,1,0:T(8,128)(2,1)S(1)}, u32[]{:S(2)}, u32[]{:S(2)}) %all-to-all-start.1) | async-done | bytes 262176 | tf_op jit(solution)/shard_map/all_to_all | solution.py:1157
  121.7 7.1 %all-to-all-start.2 = ((bf16[4,2,704,128]{3,2,1,0:T(8,128)(2,1)}), bf16[4,2,704,128]{3,2,1,0:T(8,128)(2,1)}, u32[]{:S(2)}, u32[]{:S(2)}) async-start(bf16[4,2,704,128]{3,2,1,0:T(8,128)(2,1)} %copy.466), calls=%async_computation.2 | async-start | bytes 2883584 | tf_op jit(solution)/shard_map/all_to_all | solution.py:1157
  133.1 20.0 %column_forward.1 = (bf16[512,256]{1,0:T(8,128)(2,1)S(1)}, f32[2,2,256,256]{3,2,1,0:T(8,128)S(1)}, f32[512,256]{1,0:T(8,128)S(1)}, f32[512,256]{1,0:T(8,128)S(1)...) custom-call(bf16[64,2048]{1,0:T(8,128)(2,1)S(1)} %pad_maximum_fusion.18.refs_0_, ...), custom_call_target="tpu_custom_call" | custom-call | flops 20000000000 | bytes 8388608 | tf_op jit(solution)/shard_map/column_forward/pallas_call | solution.py:410
  176.2 13.0 %collective-permute-done.30 = bf16[64,2048]{1,0:T(8,128)(2,1)S(1)} collective-permute-done((bf16[64,2048]{1,0:T(8,128)(2,1)S(1)}, bf16[64,2048]{1,0:T(8,128)(2,1)S(1)}, u32[]{:S(2)}, u32[]{:S(2)}) %collective-permute-start.30) | collective-permute-done | bytes 262176 | tf_op jit(solution)/shard_map/ppermute | solution.py:1173
  189.2 7.0 %collective-permute-done.31 = bf16[64,2048]{1,0:T(8,128)(2,1)S(1)} collective-permute-done((bf16[64,2048]{1,0:T(8,128)(2,1)S(1)}, bf16[64,2048]{1,0:T(8,128)(2,1)S(1)}, u32[]{:S(2)}, u32[]{:S(2)}) %collective-permute-start.31) | collective-permute-done | bytes 262176 | tf_op jit(solution)/shard_map/ppermute | solution.py:1173
  198.2 4.6 all-to-all-start.3
  214.9 9.4 %all-to-all-done.3.refs_21_.refs_3_ = bf16[4,2,352,128]{3,2,1,0:T(8,128)(2,1)S(1)} async-done(((bf16[4,2,352,128]{3,2,1,0:T(8,128)(2,1)}), bf16[4,2,352,128]{3,2,1,0:T(8,128)(2,1)S(1)}, u32[]{:S(2)}, u32[]{:S(2)}) %all-to-all-start.3) | async-done | bytes 720928 | tf_op jit(solution)/shard_map/all_to_all | solution.py:1157
  228.9 8.5 %collective-permute-done.34.refs_3_ = bf16[64,2048]{1,0:T(8,128)(2,1)} collective-permute-done((bf16[64,2048]{1,0:T(8,128)(2,1)S(1)}, bf16[64,2048]{1,0:T(8,128)(2,1)}, u32[]{:S(2)}, u32[]{:S(2)}) %collective-permute-start.34) | collective-permute-done | bytes 262176 | tf_op jit(solution)/shard_map/ppermute | solution.py:1173
  248.7 12.8 %collective-permute-done.46.refs_10_ = bf16[64,2048]{1,0:T(8,128)(2,1)S(1)} collective-permute-done((bf16[64,2048]{1,0:T(8,128)(2,1)S(1)}, bf16[64,2048]{1,0:T(8,128)(2,1)S(1)}, u32[]{:S(2)}, u32[]{:S(2)}) %collective-permute-start.46) | collective-permute-done | bytes 262176 | tf_op jit(solution)/shard_map/ppermute | solution.py:1173
  268.4 5.0 collective-permute-done.60.refs_24_.refs_6_
  273.7 18.1 %column_ffn.1 = (bf16[256,2048]{1,0:T(8,128)(2,1)}, bf16[256,2048]{1,0:T(8,128)(2,1)}, bf16[512,2048]{1,0:T(8,128)(2,1)}, bf16[512,2048]{1,0:T(8,128)(2,1)}, bf1...) custom-call(bf16[64,2048]{1,0:T(8,128)(2,1)S(1)} %multiply_convert_f, ...), custom_call_target="tpu_custom_call" | custom-call | flops 20000000000 | bytes 8388608 | tf_op jit(solution)/shard_map/column_ffn/pallas_call | solution.py:410
  303.6 6.1 column_down.1
  313.6 5.9 column_rows.3
  321.8 4.7 collective-permute-done.65
  334.6 19.4 %collective-permute-done.66.refs_3_ = bf16[64,2048]{1,0:T(8,128)(2,1)S(1)} collective-permute-done((bf16[64,2048]{1,0:T(8,128)(2,1)S(1)}, bf16[64,2048]{1,0:T(8,128)(2,1)S(1)}, u32[]{:S(2)}, u32[]{:S(2)}) %collective-permute-start.66) | collective-permute-done | bytes 262176 | tf_op jit(solution)/shard_map/ppermute | solution.py:1173
  360.4 17.3 %column_backward.1 = (bf16[512,1024]{1,0:T(8,128)(2,1)}, f32[512,2]{1,0:T(8,128)S(1)}, f32[2,12,256]{2,1,0:T(8,128)S(1)}, f32[2,1,128]{2,1,0:T(1,128)S(1)}, bf16...) custom-call(bf16[64,2048]{1,0:T(8,128)(2,1)S(1)} %get-tuple-element.236.refs_0_, ...), custom_call_target="tpu_custom_call" | custom-call | flops 20000000000 | bytes 8388608 | tf_op jit(solution)/shard_map/column_backward/pallas_call | solution.py:410
  398.8 6.4 %collective-permute-done.105 = bf16[4,2,128,128]{3,2,1,0:T(8,128)(2,1)S(1)} collective-permute-done((bf16[4,2,128,128]{3,2,1,0:T(8,128)(2,1)}, bf16[4,2,128,128]{3,2,1,0:T(8,128)(2,1)S(1)}, u32[]{:S(2)}, u32[]{:S(2)}) %collective-permute-start.105) | collective-permute-done | bytes 262176 | tf_op jit(solution)/shard_map/ppermute | solution.py:1161
  419.5 4.9 all-to-all-start.4
  436.5 6.2 collective-permute-done.102
  447.0 11.0 %collective-permute-done.69 = bf16[64,2048]{1,0:T(8,128)(2,1)S(1)} collective-permute-done((bf16[64,2048]{1,0:T(8,128)(2,1)S(1)}, bf16[64,2048]{1,0:T(8,128)(2,1)S(1)}, u32[]{:S(2)}, u32[]{:S(2)}) %collective-permute-start.69) | collective-permute-done | bytes 262176 | tf_op jit(solution)/shard_map/ppermute | solution.py:1173
  470.9 11.8 %collective-permute-done.86 = bf16[64,2048]{1,0:T(8,128)(2,1)S(1)} collective-permute-done((bf16[64,2048]{1,0:T(8,128)(2,1)S(1)}, bf16[64,2048]{1,0:T(8,128)(2,1)S(1)}, u32[]{:S(2)}, u32[]{:S(2)}) %collective-permute-start.86) | collective-permute-done | bytes 262176 | tf_op jit(solution)/shard_map/ppermute | solution.py:1173
  482.7 5.2 collective-permute-done.87
  535.9 5.3 all-to-all-start.5
  554.0 26.3 %all-to-all-done.5 = bf16[4,2,704,128]{3,2,1,0:T(8,128)(2,1)S(1)} async-done(((bf16[4,2,704,128]{3,2,1,0:T(8,128)(2,1)}), bf16[4,2,704,128]{3,2,1,0:T(8,128)(2,1)S(1)}, u32[]{:S(2)}, u32[]{:S(2)}) %all-to-all-start.5) | async-done | bytes 1441824 | tf_op jit(solution)/shard_map/all_to_all | solution.py:1157
  581.1 7.6 %all-to-all-start.6 = ((bf16[4,2,128,128]{3,2,1,0:T(8,128)(2,1)}), bf16[4,2,128,128]{3,2,1,0:T(8,128)(2,1)S(1)}, u32[]{:S(2)}, u32[]{:S(2)}) async-start(bf16[4,2,128,128]{3,2,1,0:T(8,128)(2,1)} %copy.497), calls=%async_computation.6 | async-start | bytes 524288 | tf_op jit(solution)/shard_map/all_to_all | solution.py:1157
  590.0 7.8 %all-to-all-done.6 = bf16[4,2,128,128]{3,2,1,0:T(8,128)(2,1)S(1)} async-done(((bf16[4,2,128,128]{3,2,1,0:T(8,128)(2,1)}), bf16[4,2,128,128]{3,2,1,0:T(8,128)(2,1)S(1)}, u32[]{:S(2)}, u32[]{:S(2)}) %all-to-all-start.6) | async-done | bytes 262176 | tf_op jit(solution)/shard_map/all_to_all | solution.py:1157
  598.8 7.3 %all-to-all-start.7 = ((bf16[4,2,128,512]{3,2,1,0:T(8,128)(2,1)}), bf16[4,2,128,512]{3,2,1,0:T(8,128)(2,1)}, u32[]{:S(2)}, u32[]{:S(2)}) async-start(bf16[4,2,128,512]{3,2,1,0:T(8,128)(2,1)} %copy.498), calls=%async_computation.7 | async-start | bytes 2097152 | tf_op jit(solution)/shard_map/all_to_all | solution.py:1157
  612.2 13.5 %collective-permute-done.77 = bf16[2,64,512]{2,1,0:T(8,128)(2,1)S(1)} collective-permute-done((bf16[2,64,512]{2,1,0:T(8,128)(2,1)S(1)}, bf16[2,64,512]{2,1,0:T(8,128)(2,1)S(1)}, u32[]{:S(2)}, u32[]{:S(2)}) %collective-permute-start.77) | collective-permute-done | bytes 131104 | tf_op jit(solution)/shard_map/ppermute | solution.py:1180
  (777 shorter events, 314.7 us)
Async XLA Ops:
  6.3 57.1 %all-to-all-start = ((bf16[4,2,128,512]{3,2,1,0:T(8,128)(2,1)}), bf16[4,2,128,512]{3,2,1,0:T(8,128)(2,1)}, u32[]{:S(2)}, u32[]{:S(2)}) async-start(bf16[4,2,128,512]{3,2,1,0:T(8,128)(2,1)} %pad_maximum_fusion.4), calls=%async_computation | async-start | bytes 2097152 | tf_op jit(solution)/shard_map/all_to_all | solution.py:1157
  23.1 89.9 %collective-permute-start.52 = (bf16[4,704,128]{2,1,0:T(8,128)(2,1)}, bf16[4,704,128]{2,1,0:T(8,128)(2,1)}, u32[]{:S(2)}, u32[]{:S(2)}) collective-permute-start(bf16[4,704,128]{2,1,0:T(8,128)(2,1)} %select_bitcast_fusion.2), channel_id=1, source_target_pairs={{0,1},{1,0},{2,3},{3,2},{4,5},{5,4},{6,7},{7,6},{8,9},{9,8},{10,11... | collective-permute-start | bytes 2162696 | tf_op jit(solution)/shard_map/ppermute | solution.py:1165
  57.5 36.1 %collective-permute-start.9 = (bf16[64,2048]{1,0:T(8,128)(2,1)S(1)}, bf16[64,2048]{1,0:T(8,128)(2,1)S(1)}, u32[]{:S(2)}, u32[]{:S(2)}) collective-permute-start(bf16[64,2048]{1,0:T(8,128)(2,1)S(1)} %pad_maximum_fusion.18.refs_0_), channel_id=1, source_target_pairs={{0,24},{8,16},{16,8},{24,0},{1,25},{9,17},{17,9},{25,1},{2,26},{10... | collective-permute-start | bytes 786440 | tf_op jit(solution)/shard_map/ppermute | solution.py:1173
  58.1 54.4 %collective-permute-start.7 = (bf16[64,2048]{1,0:T(8,128)(2,1)S(1)}, bf16[64,2048]{1,0:T(8,128)(2,1)S(1)}, u32[]{:S(2)}, u32[]{:S(2)}) collective-permute-start(bf16[64,2048]{1,0:T(8,128)(2,1)S(1)} %pad_maximum_fusion.18.refs_0_), channel_id=1, source_target_pairs={{0,8},{8,0},{16,24},{24,16},{1,9},{9,1},{17,25},{25,17},{2,10},{10... | collective-permute-start | bytes 786440 | tf_op jit(solution)/shard_map/ppermute | solution.py:1173
  63.9 26.8 %collective-permute-start.14 = (bf16[4,2,128,512]{3,2,1,0:T(8,128)(2,1)}, bf16[4,2,128,512]{3,2,1,0:T(8,128)(2,1)}, u32[]{:S(2)}, u32[]{:S(2)}) collective-permute-start(bf16[4,2,128,512]{3,2,1,0:T(8,128)(2,1)} %all-to-all-done), channel_id=1, source_target_pairs={{0,2},{1,3},{2,0},{3,1},{4,6},{5,7},{6,4},{7,5},{8,10},{9,11},{10,... | collective-permute-start | bytes 3145736 | tf_op jit(solution)/shard_map/ppermute | solution.py:1169
  102.6 26.3 %collective-permute-start.10 = (bf16[64,2048]{1,0:T(8,128)(2,1)S(1)}, bf16[64,2048]{1,0:T(8,128)(2,1)}, u32[]{:S(2)}, u32[]{:S(2)}) collective-permute-start(bf16[64,2048]{1,0:T(8,128)(2,1)S(1)} %pad_maximum_fusion.18.refs_0_), channel_id=1, source_target_pairs={{0,1},{1,0},{2,3},{3,2},{4,5},{5,4},{6,7},{7,6},{8,9},{9,8},{10,11... | collective-permute-start | bytes 786440 | tf_op jit(solution)/shard_map/ppermute | solution.py:1165
  121.7 47.5 %all-to-all-start.2 = ((bf16[4,2,704,128]{3,2,1,0:T(8,128)(2,1)}), bf16[4,2,704,128]{3,2,1,0:T(8,128)(2,1)}, u32[]{:S(2)}, u32[]{:S(2)}) async-start(bf16[4,2,704,128]{3,2,1,0:T(8,128)(2,1)} %copy.466), calls=%async_computation.2 | async-start | bytes 2883584 | tf_op jit(solution)/shard_map/all_to_all | solution.py:1157
  128.8 28.2 %collective-permute-start.57 = (bf16[4,352,128]{2,1,0:T(8,128)(2,1)}, bf16[4,352,128]{2,1,0:T(8,128)(2,1)S(1)}, u32[]{:S(2)}, u32[]{:S(2)}) collective-permute-start(bf16[4,352,128]{2,1,0:T(8,128)(2,1)} %bitcast.572), channel_id=1, source_target_pairs={{0,1},{1,0},{2,3},{3,2},{4,5},{5,4},{6,7},{7,6},{8,9},{9,8},{10,11... | collective-permute-start | bytes 1081352 | tf_op jit(solution)/shard_map/ppermute | solution.py:1165
  166.8 29.4 %collective-permute-start.31 = (bf16[64,2048]{1,0:T(8,128)(2,1)S(1)}, bf16[64,2048]{1,0:T(8,128)(2,1)S(1)}, u32[]{:S(2)}, u32[]{:S(2)}) collective-permute-start(bf16[64,2048]{1,0:T(8,128)(2,1)S(1)} %get-tuple-element.289), channel_id=1, source_target_pairs={{0,24},{8,16},{16,8},{24,0},{1,25},{9,17},{17,9},{25,1},{2,26},{10... | collective-permute-start | bytes 786440 | tf_op jit(solution)/shard_map/ppermute | solution.py:1173
  172.1 32.8 %collective-permute-start.54 = (bf16[4,2,704,128]{3,2,1,0:T(8,128)(2,1)}, bf16[4,2,704,128]{3,2,1,0:T(8,128)(2,1)}, u32[]{:S(2)}, u32[]{:S(2)}) collective-permute-start(bf16[4,2,704,128]{3,2,1,0:T(8,128)(2,1)} %all-to-all-done.2.refs_16_), channel_id=1, source_target_pairs={{0,4},{4,0},{1,5},{5,1},{2,6},{6,2},{3,7},{7,3},{8,12},{12,8},{9,1... | collective-permute-start | bytes 4325384 | tf_op jit(solution)/shard_map/ppermute | solution.py:1161
  172.7 33.4 %collective-permute-start.53 = (bf16[4,2,704,128]{3,2,1,0:T(8,128)(2,1)}, bf16[4,2,704,128]{3,2,1,0:T(8,128)(2,1)}, u32[]{:S(2)}, u32[]{:S(2)}) collective-permute-start(bf16[4,2,704,128]{3,2,1,0:T(8,128)(2,1)} %all-to-all-done.2.refs_16_), channel_id=1, source_target_pairs={{0,2},{1,3},{2,0},{3,1},{4,6},{5,7},{6,4},{7,5},{8,10},{9,11},{10,... | collective-permute-start | bytes 4325384 | tf_op jit(solution)/shard_map/ppermute | solution.py:1169
  209.9 27.5 %collective-permute-start.34 = (bf16[64,2048]{1,0:T(8,128)(2,1)S(1)}, bf16[64,2048]{1,0:T(8,128)(2,1)}, u32[]{:S(2)}, u32[]{:S(2)}) collective-permute-start(bf16[64,2048]{1,0:T(8,128)(2,1)S(1)} %multiply_convert_fusion.refs_0_), channel_id=1, source_target_pairs={{0,24},{8,16},{16,8},{24,0},{1,25},{9,17},{17,9},{25,1},{2,26},{10... | collective-permute-start | bytes 786440 | tf_op jit(solution)/shard_map/ppermute | solution.py:1173
  210.5 26.9 %collective-permute-start.32 = (bf16[64,2048]{1,0:T(8,128)(2,1)S(1)}, bf16[64,2048]{1,0:T(8,128)(2,1)}, u32[]{:S(2)}, u32[]{:S(2)}) collective-permute-start(bf16[64,2048]{1,0:T(8,128)(2,1)S(1)} %multiply_convert_fusion.refs_0_), channel_id=1, source_target_pairs={{0,8},{8,0},{16,24},{24,16},{1,9},{9,1},{17,25},{25,17},{2,10},{10... | collective-permute-start | bytes 786440 | tf_op jit(solution)/shard_map/ppermute | solution.py:1173
  226.9 34.5 %collective-permute-start.59 = (bf16[4,2,352,128]{3,2,1,0:T(8,128)(2,1)S(1)}, bf16[4,2,352,128]{3,2,1,0:T(8,128)(2,1)S(1)}, u32[]{:S(2)}, u32[]{:S(2)}) collective-permute-start(bf16[4,2,352,128]{3,2,1,0:T(8,128)(2,1)S(1)} %all-to-all-done.3.refs_21_.refs_3_), channel_id=1, source_target_pairs={{0,4},{4,0},{1,5},{5,1},{2,6},{6,2},{3,7},{7,3},{8,12},{12,8},{9,1... | collective-permute-start | bytes 2162696 | tf_op jit(solution)/shard_map/ppermute | solution.py:1161
  227.5 34.5 %collective-permute-start.58 = (bf16[4,2,352,128]{3,2,1,0:T(8,128)(2,1)S(1)}, bf16[4,2,352,128]{3,2,1,0:T(8,128)(2,1)S(1)}, u32[]{:S(2)}, u32[]{:S(2)}) collective-permute-start(bf16[4,2,352,128]{3,2,1,0:T(8,128)(2,1)S(1)} %all-to-all-done.3.refs_21_.refs_3_), channel_id=1, source_target_pairs={{0,2},{1,3},{2,0},{3,1},{4,6},{5,7},{6,4},{7,5},{8,10},{9,11},{10,... | collective-permute-start | bytes 2162696 | tf_op jit(solution)/shard_map/ppermute | solution.py:1169
  310.6 44.0 %collective-permute-start.117 = (bf16[4,2,352,128]{3,2,0,1:T(8,128)(2,1)S(1)}, bf16[4,2,352,128]{3,2,0,1:T(8,128)(2,1)S(1)}, u32[]{:S(2)}, u32[]{:S(2)}) collective-permute-start(bf16[4,2,352,128]{3,2,0,1:T(8,128)(2,1)S(1)} %pad_maximum_fusion.13), channel_id=1, source_target_pairs={{0,2},{1,3},{2,0},{3,1},{4,6},{5,7},{6,4},{7,5},{8,10},{9,11},{10,... | collective-permute-start | bytes 2162696 | tf_op jit(solution)/shard_map/ppermute | solution.py:1169
  312.4 43.5 %collective-permute-start.115 = (bf16[4,2,352,128]{3,2,0,1:T(8,128)(2,1)S(1)}, bf16[4,2,352,128]{3,2,0,1:T(8,128)(2,1)S(1)}, u32[]{:S(2)}, u32[]{:S(2)}) collective-permute-start(bf16[4,2,352,128]{3,2,0,1:T(8,128)(2,1)S(1)} %pad_maximum_fusion.12), channel_id=1, source_target_pairs={{0,4},{4,0},{1,5},{5,1},{2,6},{6,2},{3,7},{7,3},{8,12},{12,8},{9,1... | collective-permute-start | bytes 2162696 | tf_op jit(solution)/shard_map/ppermute | solution.py:1161
  355.9 68.6 %collective-permute-start.112 = (bf16[4,2,704,128]{3,2,1,0:T(8,128)(2,1)}, bf16[4,2,704,128]{3,2,1,0:T(8,128)(2,1)}, u32[]{:S(2)}, u32[]{:S(2)}) collective-permute-start(bf16[4,2,704,128]{3,2,1,0:T(8,128)(2,1)} %pad_maximum_fusion.2), channel_id=1, source_target_pairs={{0,2},{1,3},{2,0},{3,1},{4,6},{5,7},{6,4},{7,5},{8,10},{9,11},{10,... | collective-permute-start | bytes 4325384 | tf_op jit(solution)/shard_map/ppermute | solution.py:1169
  358.3 70.0 %collective-permute-start.110 = (bf16[4,2,704,128]{3,2,1,0:T(8,128)(2,1)}, bf16[4,2,704,128]{3,2,1,0:T(8,128)(2,1)}, u32[]{:S(2)}, u32[]{:S(2)}) collective-permute-start(bf16[4,2,704,128]{3,2,1,0:T(8,128)(2,1)} %pad_maximum_fusion.1), channel_id=1, source_target_pairs={{0,4},{4,0},{1,5},{5,1},{2,6},{6,2},{3,7},{7,3},{8,12},{12,8},{9,1... | collective-permute-start | bytes 4325384 | tf_op jit(solution)/shard_map/ppermute | solution.py:1161
  358.8 46.4 %collective-permute-start.118 = (bf16[2,2,352,128]{3,2,0,1:T(8,128)(2,1)}, bf16[2,2,352,128]{3,2,0,1:T(8,128)(2,1)}, u32[]{:S(2)}, u32[]{:S(2)}) collective-permute-start(bf16[2,2,352,128]{3,2,0,1:T(8,128)(2,1)} %add_convert_fusion.9), channel_id=1, source_target_pairs={{0,4},{4,0},{1,5},{5,1},{2,6},{6,2},{3,7},{7,3},{8,12},{12,8},{9,1... | collective-permute-start | bytes 1081352 | tf_op jit(solution)/shard_map/ppermute | solution.py:1161
  419.5 115.2 %all-to-all-start.4 = ((bf16[4,2,352,128]{3,2,1,0:T(8,128)(2,1)}), bf16[4,2,352,128]{3,2,1,0:T(8,128)(2,1)}, u32[]{:S(2)}, u32[]{:S(2)}) async-start(bf16[4,2,352,128]{3,2,1,0:T(8,128)(2,1)} %copy.495), calls=%async_computation.4 | async-start | bytes 1441792 | tf_op jit(solution)/shard_map/all_to_all | solution.py:1157
  424.5 40.8 %collective-permute-start.100 = (bf16[1024,512]{1,0:T(8,128)(2,1)}, bf16[1024,512]{1,0:T(8,128)(2,1)S(1)}, u32[]{:S(2)}, u32[]{:S(2)}) collective-permute-start(bf16[1024,512]{1,0:T(8,128)(2,1)} %pad_maximum_fusion.5), channel_id=1, source_target_pairs={{0,4},{4,0},{1,5},{5,1},{2,6},{6,2},{3,7},{7,3},{8,12},{12,8},{9,1... | collective-permute-start | bytes 3145736 | tf_op jit(solution)/shard_map/ppermute | solution.py:1161
  428.3 82.8 %collective-permute-start.113 = (bf16[2,2,704,128]{3,2,1,0:T(8,128)(2,1)}, bf16[2,2,704,128]{3,2,1,0:T(8,128)(2,1)S(1)}, u32[]{:S(2)}, u32[]{:S(2)}) collective-permute-start(bf16[2,2,704,128]{3,2,1,0:T(8,128)(2,1)} %add_convert_fusion.1), channel_id=1, source_target_pairs={{0,4},{4,0},{1,5},{5,1},{2,6},{6,2},{3,7},{7,3},{8,12},{12,8},{9,1... | collective-permute-start | bytes 2162696 | tf_op jit(solution)/shard_map/ppermute | solution.py:1161
  446.6 64.4 %collective-permute-start.111 = (bf16[2,2,704,128]{3,2,1,0:T(8,128)(2,1)S(1)}, bf16[2,2,704,128]{3,2,1,0:T(8,128)(2,1)}, u32[]{:S(2)}, u32[]{:S(2)}) collective-permute-start(bf16[2,2,704,128]{3,2,1,0:T(8,128)(2,1)S(1)} %add_convert_fusion.3), channel_id=1, source_target_pairs={{0,2},{1,3},{2,0},{3,1},{4,6},{5,7},{6,4},{7,5},{8,10},{9,11},{10,... | collective-permute-start | bytes 2162696 | tf_op jit(solution)/shard_map/ppermute | solution.py:1169
  469.3 60.1 %collective-permute-start.103 = (bf16[512,512]{1,0:T(8,128)(2,1)}, bf16[512,512]{1,0:T(8,128)(2,1)}, u32[]{:S(2)}, u32[]{:S(2)}) collective-permute-start(bf16[512,512]{1,0:T(8,128)(2,1)} %add_convert_fusion.5), channel_id=1, source_target_pairs={{0,4},{4,0},{1,5},{5,1},{2,6},{6,2},{3,7},{7,3},{8,12},{12,8},{9,1... | collective-permute-start | bytes 1572872 | tf_op jit(solution)/shard_map/ppermute | solution.py:1161
  535.9 44.5 %all-to-all-start.5 = ((bf16[4,2,704,128]{3,2,1,0:T(8,128)(2,1)}), bf16[4,2,704,128]{3,2,1,0:T(8,128)(2,1)S(1)}, u32[]{:S(2)}, u32[]{:S(2)}) async-start(bf16[4,2,704,128]{3,2,1,0:T(8,128)(2,1)} %copy.496), calls=%async_computation.5 | async-start | bytes 2883584 | tf_op jit(solution)/shard_map/all_to_all | solution.py:1157
  542.1 46.6 %collective-permute-start.104 = (bf16[4,128,512]{2,1,0:T(8,128)(2,1)}, bf16[4,128,512]{2,1,0:T(8,128)(2,1)}, u32[]{:S(2)}, u32[]{:S(2)}) collective-permute-start(bf16[4,128,512]{2,1,0:T(8,128)(2,1)} %select_bitcast_fusion.3), channel_id=1, source_target_pairs={{0,1},{1,0},{2,3},{3,2},{4,5},{5,4},{6,7},{7,6},{8,9},{9,8},{10,11... | collective-permute-start | bytes 1572872 | tf_op jit(solution)/shard_map/ppermute | solution.py:1165
  544.1 64.4 %collective-permute-start.92 = (bf16[2,64,512]{2,1,0:T(8,128)(2,1)}, bf16[2,64,512]{2,1,0:T(8,128)(2,1)}, u32[]{:S(2)}, u32[]{:S(2)}) collective-permute-start(bf16[2,64,512]{2,1,0:T(8,128)(2,1)} %get-tuple-element.320), channel_id=1, source_target_pairs={{0,24},{8,16},{16,8},{24,0},{1,25},{9,17},{17,9},{25,1},{2,26},{10... | collective-permute-start | bytes 393224 | tf_op jit(solution)/shard_map/ppermute | solution.py:1180
  544.7 65.3 %collective-permute-start.93 = (bf16[2,64,512]{2,1,0:T(8,128)(2,1)}, bf16[2,64,512]{2,1,0:T(8,128)(2,1)}, u32[]{:S(2)}, u32[]{:S(2)}) collective-permute-start(bf16[2,64,512]{2,1,0:T(8,128)(2,1)} %get-tuple-element.321), channel_id=1, source_target_pairs={{0,16},{8,24},{16,0},{24,8},{1,17},{9,25},{17,1},{25,9},{2,18},{10... | collective-permute-start | bytes 393224 | tf_op jit(solution)/shard_map/ppermute | solution.py:1180
  548.0 62.0 %collective-permute-start.94 = (bf16[2,64,512]{2,1,0:T(8,128)(2,1)}, bf16[2,64,512]{2,1,0:T(8,128)(2,1)}, u32[]{:S(2)}, u32[]{:S(2)}) collective-permute-start(bf16[2,64,512]{2,1,0:T(8,128)(2,1)} %get-tuple-element.319), channel_id=1, source_target_pairs={{0,8},{8,0},{16,24},{24,16},{1,9},{9,1},{17,25},{25,17},{2,10},{10... | collective-permute-start | bytes 393224 | tf_op jit(solution)/shard_map/ppermute | solution.py:1180
  549.8 62.4 %collective-permute-start.75 = (bf16[2,64,512]{2,1,0:T(8,128)(2,1)}, bf16[2,64,512]{2,1,0:T(8,128)(2,1)}, u32[]{:S(2)}, u32[]{:S(2)}) collective-permute-start(bf16[2,64,512]{2,1,0:T(8,128)(2,1)} %get-tuple-element.327), channel_id=1, source_target_pairs={{0,24},{8,16},{16,8},{24,0},{1,25},{9,17},{17,9},{25,1},{2,26},{10... | collective-permute-start | bytes 393224 | tf_op jit(solution)/shard_map/ppermute | solution.py:1180
  598.8 33.4 %all-to-all-start.7 = ((bf16[4,2,128,512]{3,2,1,0:T(8,128)(2,1)}), bf16[4,2,128,512]{3,2,1,0:T(8,128)(2,1)}, u32[]{:S(2)}, u32[]{:S(2)}) async-start(bf16[4,2,128,512]{3,2,1,0:T(8,128)(2,1)} %copy.498), calls=%async_computation.7 | async-start | bytes 2097152 | tf_op jit(solution)/shard_map/all_to_all | solution.py:1157
  (238 other events, 3456.2 us)

commit v3 on v2

--- a/solution.py
+++ b/solution.py
@@ -60,12 +60,6 @@
     return total
 
 
-def blocks_of(order_ref, length):
-    count = order_ref.shape[0]
-    share = length // count
-    return [pl.ds(pl.multiple_of(order_ref[j] * share, share), share) for j in range(count)]
-
-
 def single(left, right):
     return lax.dot_general(
         left.astype(LOW),
@@ -75,43 +69,61 @@
     )
 
 
-def invert(lower, rows, cols):
-    length = lower.shape[0]
+def invert(lowers, rows, cols):
+    length = lowers[0].shape[0]
     eye = (rows == cols).astype(WIDE)
-    inverse = eye - jnp.where((rows // 2) == (cols // 2), lower, 0.0)
+    pair = (rows // 2) == (cols // 2)
+    inverses = [eye - jnp.where(pair, lower, 0.0) for lower in lowers]
     size = 2
     while size < length:
         cross = ((rows // (2 * size)) == (cols // (2 * size))) & ((rows // size) != (cols // size))
-        inverse = inverse - single(single(inverse, jnp.where(cross, lower, 0.0)), inverse)
+        steps = [
+            single(inverse, jnp.where(cross, lower, 0.0))
+            for inverse, lower in zip(inverses, lowers)
+        ]
+        inverses = [
+            inverse - single(step, inverse) for step, inverse in zip(steps, inverses)
+        ]
         size *= 2
-    rest = eye - inverse - product(halves(lower), halves(inverse), 1, 0)
-    return inverse + single(inverse, rest)
-
-
-def forward_head(signals, beta_in, conv, kept, masks, gain):
+    rests = [
+        eye - inverse - product(halves(lower), halves(inverse), 1, 0)
+        for inverse, lower in zip(inverses, lowers)
+    ]
+    return [inverse + single(inverse, rest) for inverse, rest in zip(inverses, rests)]
+
+
+def forward_heads(signals, beta_in, conv, kept, masks, gain):
     rows, cols, strict, inclusive = masks
-    taps = conv.shape[0] // 3
-    convolved = []
-    for part in range(3):
-        pre = convolve(signals[part], conv[part * taps : (part + 1) * taps], kept)
-        convolved.append(pre * sigmoid(pre))
-    query = convolved[0] * (
-        lax.rsqrt(jnp.sum(convolved[0] * convolved[0], 1, keepdims=True) + 1e-06) * HEAD**-0.5
-    )
-    key = convolved[1] * lax.rsqrt(
-        jnp.sum(convolved[1] * convolved[1], 1, keepdims=True) + 1e-06
-    )
-    beta = sigmoid(beta_in)
-    key_parts = halves(key)
-    gram = product(key_parts, key_parts, 1, 1)
-    inverse = invert(jnp.where(strict, gram * beta, 0.0), rows, cols)
-    update = product(halves(inverse), halves(convolved[2] * beta), 1, 0)
-    scores = jnp.where(inclusive, product(halves(query), key_parts, 1, 1), 0.0)
-    mixed = product(halves(scores), halves(update), 1, 0)
-    scale = lax.rsqrt(jnp.sum(mixed * mixed, 1, keepdims=True) * (1.0 / HEAD) + 1e-05)
-    gate = signals[3]
-    gated = (mixed * scale * gain * (gate * sigmoid(gate))).astype(LOW)
-    return gated, inverse, update, mixed
+    taps = conv[0].shape[0] // 3
+    lowers, held = [], []
+    for head in range(len(signals)):
+        convolved = []
+        for part in range(3):
+            kernel = conv[head][part * taps : (part + 1) * taps]
+            pre = convolve(signals[head][part], kernel, kept)
+            convolved.append(pre * sigmoid(pre))
+        query = convolved[0] * (
+            lax.rsqrt(jnp.sum(convolved[0] * convolved[0], 1, keepdims=True) + 1e-06) * HEAD**-0.5
+        )
+        key = convolved[1] * lax.rsqrt(
+            jnp.sum(convolved[1] * convolved[1], 1, keepdims=True) + 1e-06
+        )
+        beta = sigmoid(beta_in[head])
+        key_parts = halves(key)
+        gram = product(key_parts, key_parts, 1, 1)
+        lowers.append(jnp.where(strict, gram * beta, 0.0))
+        scores = jnp.where(inclusive, product(halves(query), key_parts, 1, 1), 0.0)
+        held.append((halves(scores), halves(convolved[2] * beta)))
+    out = []
+    for head, inverse in enumerate(invert(lowers, rows, cols)):
+        scores, target = held[head]
+        update = product(halves(inverse), target, 1, 0)
+        mixed = product(scores, halves(update), 1, 0)
+        scale = lax.rsqrt(jnp.sum(mixed * mixed, 1, keepdims=True) * (1.0 / HEAD) + 1e-05)
+        gate = signals[head][3]
+        gated = (mixed * scale * gain * (gate * sigmoid(gate))).astype(LOW)
+        out.append((gated, inverse, update, mixed))
+    return out
 
 
 def backward_head(signals, beta_in, conv, kept, masks, gain, inverse, update, mixed, grad):
@@ -210,18 +222,17 @@
     gated_ref, inverse_ref, update_ref, mixed_ref = refs[7:]
     masks = masks_of(col_ref[...], row_ref[0])
     kept = kept_of(col_ref[...], conv_ref.shape[0] // 3)
-    for head in range(2):
+    results = forward_heads(
+        [[parts[head][:, head_lanes(part)] for part in range(4)] for head in range(2)],
+        [beta_ref[:, head : head + 1] for head in range(2)],
+        [conv_ref[:, head_lanes(head)] for head in range(2)],
+        kept,
+        masks,
+        head_ref[...],
+    )
+    for head, result in enumerate(results):
         own = head_lanes(head)
-        gated_ref[:, own], inverse_ref[0, head], update_ref[:, own], mixed_ref[:, own] = (
-            forward_head(
-                [parts[head][:, head_lanes(part)] for part in range(4)],
-                beta_ref[:, head : head + 1],
-                conv_ref[:, own],
-                kept,
-                masks,
-                head_ref[...],
-            )
-        )
+        gated_ref[:, own], inverse_ref[0, head], update_ref[:, own], mixed_ref[:, own] = result
 
 
 def mixer_backward_kernel(*refs):
@@ -332,14 +343,20 @@
     )(*inputs, *saved, grad)
 
 
-def across(refs, rows):
+def beside(refs, rows, lanes=slice(None)):
     return jnp.concatenate(
-        [ref[z, c, rows] for ref in refs for z in range(ref.shape[0]) for c in range(2)], 1
-    )
-
-
-def down_list(refs):
-    return jnp.concatenate([ref[...] for ref in refs], 0)
+        [ref[z, c, rows, lanes] for ref in refs for z in range(ref.shape[0]) for c in range(2)], 1
+    )
+
+
+def atop(refs, lanes):
+    return jnp.concatenate(
+        [ref[z, c, :, lanes] for ref in refs for z in range(ref.shape[0]) for c in range(2)], 0
+    )
+
+
+def both(weight_refs, far, rows, lanes=slice(None)):
+    return jnp.concatenate([beside(weight_refs[i][far], rows, lanes) for i in range(2)], 0)
 
 
 def turned(left, right):
@@ -360,24 +377,20 @@
     )
 
 
-def collect(token_refs, hold_ref, place_refs):
-    half = len(token_refs) // 2
+def collect(token_refs, hold_ref):
     for step in range(2):
 
         @pl.when(pl.program_id(0) == step)
         def _():
-            for k in range(half):
-                hold_ref[place_refs[k], :] = token_refs[step * half + k][...]
-
-
-def deal(near_ref, far_ref, values, places, lanes):
-    share = values.shape[0] // len(places)
-    for step, ref in enumerate((near_ref, far_ref)):
+            hold_ref[...] = token_refs[step][...]
+
+
+def deal(pair_refs, values, lanes):
+    for step in range(2):
 
         @pl.when(pl.program_id(0) == step)
         def _():
-            for j, place in enumerate(places):
-                ref[place, lanes] = values[j * share : (j + 1) * share].astype(LOW)
+            pair_refs[step][:, lanes] = values.astype(LOW)
 
 
 def whole(values):
@@ -397,16 +410,12 @@
     return [item for pair in grid for items in pair for item in items]
 
 
-def nested(refs, lengths):
-    flat_lists = split_refs(refs, [n for pair in lengths for n in pair])
-    return [flat_lists[:2], flat_lists[2:]]
-
-
-def lengths_of(grid):
-    return [[len(items) for items in pair] for pair in grid]
-
-
-def call(kernel, inputs, in_specs, out_specs, out_shape, scratch, name, grid=2, work=20):
+def nested(refs, grid):
+    lists = split_refs(refs, [len(items) for pair in grid for items in pair])
+    return [lists[:2], lists[2:]]
+
+
+def call(kernel, inputs, in_specs, out_specs, out_shape, scratch, name, grid=2):
     return pl.pallas_call(
         kernel,
         grid=(grid,),
@@ -416,199 +425,183 @@
         scratch_shapes=scratch,
         compiler_params=pltpu.CompilerParams(vmem_limit_bytes=48 << 20),
         cost_estimate=pl.CostEstimate(
-            flops=work * 10**9, bytes_accessed=8 << 20, transcendentals=0
+            flops=10 * 10**9, bytes_accessed=8 << 20, transcendentals=0
         ),
         name=name,
     )(*inputs)
 
 
-def column_forward(tokens, weights, gain, beta_weights, seg_col, seg_row, conv, head_gain, order):
+QKVG = slice(0, 4 * HEAD)
+OUT = slice(4 * HEAD, 5 * HEAD)
+
+
+def column_forward(tokens, weights, gain, beta_weights, seg_col, seg_row, conv, head_gain):
     count, _, length = seg_row.shape
     width = tokens[0].shape[1]
-    lengths = lengths_of(weights)
+    half = width // 2
+    span = [slice(0, half), slice(half, width)]
     pieces = flat(weights)
 
     def kernel(*refs):
-        token_refs, weight_refs, rest = split_refs(refs, [len(tokens), len(pieces), 18])
-        gain_ref, beta_ref, col_ref, row_ref, conv_ref, head_ref, order_ref = rest[:7]
-        gated_ref, inverse_ref, update_ref, mixed_ref = rest[7:11]
-        mixer_ref, first_ref, second_ref, beta_in_ref, hold_ref = rest[11:]
-        weight_refs = nested(weight_refs, lengths)
-        collect(token_refs, hold_ref, blocks_of(order_ref, length))
+        token_refs, weight_refs, rest = split_refs(refs, [2, len(pieces), 17])
+        gain_ref, beta_ref, col_ref, row_ref, conv_ref, head_ref = rest[:6]
+        gated_ref, inverse_ref, update_ref, mixed_ref = rest[6:10]
+        mixer_ref, first_ref, second_ref, beta_in_ref = rest[10:14]
+        pair_refs, hold_ref = rest[14:16], rest[16]
+        weight_refs = nested(weight_refs, weights)
+        collect(token_refs, hold_ref)
         values = hold_ref[...].astype(WIDE)
         scale = lax.rsqrt(jnp.sum(values * values, 1, keepdims=True) * (1.0 / D) + 1e-06)
         mixer_ref[...] = (values * scale * gain_ref[...]).astype(LOW)
         masks = masks_of(col_ref[...], row_ref[0])
         kept = kept_of(col_ref[...], conv_ref.shape[0] // 3)
         mixer_in = mixer_ref[...].astype(WIDE)
-        half = width // 2
+        beta_in = []
         for head, projected_ref in enumerate((first_ref, second_ref)):
+            projected_ref[...] = sum(
+                straight(mixer_ref[:, span[far]], atop(weight_refs[head][far], QKVG))
+                for far in range(2)
+            )
+            beta_in.append(
+                jnp.sum(mixer_in * beta_ref[head : head + 1, :].astype(WIDE), 1, keepdims=True)
+            )
+            beta_in_ref[:, head : head + 1] = beta_in[head]
+        results = forward_heads(
+            [
+                [ref[:, head_lanes(part)] for part in range(4)]
+                for ref in (first_ref, second_ref)
+            ],
+            beta_in,
+            [conv_ref[:, head_lanes(head)] for head in range(2)],
+            kept,
+            masks,
+            head_ref[...],
+        )
+        for head, result in enumerate(results):
             own = head_lanes(head)
-            projected_ref[...] = straight(
-                mixer_ref[:, :half], down_list(weight_refs[head][0])
-            ) + straight(mixer_ref[:, half:], down_list(weight_refs[head][1]))
-            beta_in = jnp.sum(
-                mixer_in * beta_ref[head : head + 1, :].astype(WIDE), 1, keepdims=True
-            )
-            beta_in_ref[:, head : head + 1] = beta_in
-            gated_ref[:, own], inverse_ref[0, head], update_ref[:, own], mixed_ref[:, own] = (
-                forward_head(
-                    [projected_ref[:, head_lanes(part)] for part in range(4)],
-                    beta_in,
-                    conv_ref[:, own],
-                    kept,
-                    masks,
-                    head_ref[...],
-                )
-            )
-
-    inputs = list(tokens) + pieces + [
-        gain, beta_weights, seg_col, seg_row, conv, head_gain, order
-    ]
+            gated_ref[:, own], inverse_ref[0, head], update_ref[:, own], mixed_ref[:, own] = result
+        for far in range(2):
+            branch = straight(gated_ref[...], both(weight_refs, far, slice(None), OUT))
+            deal(pair_refs, branch, span[far])
+
+    inputs = list(tokens) + pieces + [gain, beta_weights, seg_col, seg_row, conv, head_gain]
     in_specs = [whole(item) for item in inputs]
-    in_specs[-5] = pl.BlockSpec((length, 1), lambda i: (i, 0))
-    in_specs[-4] = pl.BlockSpec((1, 1, length), lambda i: (i, 0, 0))
-    in_specs[-1] = pl.BlockSpec(memory_space=pltpu.SMEM)
+    in_specs[-4] = pl.BlockSpec((length, 1), lambda i: (i, 0))
+    in_specs[-3] = pl.BlockSpec((1, 1, length), lambda i: (i, 0, 0))
     step = lambda lanes: pl.BlockSpec((length, lanes), lambda i: (i, 0))
     shape = lambda lanes, kind: jax.ShapeDtypeStruct((count * length, lanes), kind)
+    out = jax.ShapeDtypeStruct((length, width), LOW)
     return call(
         kernel,
         inputs,
         in_specs,
         [step(2 * HEAD)]
         + saved_specs(length)
-        + [step(width), step(4 * HEAD), step(4 * HEAD), step(2)],
+        + [step(width), step(4 * HEAD), step(4 * HEAD), step(2)]
+        + [whole(out)] * 2,
         [shape(2 * HEAD, LOW)]
         + saved_shapes(count, length)
-        + [shape(width, LOW), shape(4 * HEAD, WIDE), shape(4 * HEAD, WIDE), shape(2, WIDE)],
+        + [shape(width, LOW), shape(4 * HEAD, WIDE), shape(4 * HEAD, WIDE), shape(2, WIDE)]
+        + [out] * 2,
         [pltpu.VMEM((length, width), LOW)],
         "column_forward",
     )
 
 
-def column_branch(gated, weights, order, length):
-    lengths = lengths_of(weights)
+def ffn_rows_of(hidden):
+    return [slice(n * hidden, (n + 1) * hidden) for n in range(3)]
+
+
+def column_ffn(tokens, ways, scales, weights, hidden):
+    length, width = tokens[0].shape
+    half = width // 2
+    span = [slice(0, half), slice(half, width)]
     pieces = flat(weights)
-    width = 2 * sum(item.shape[0] * 2 * item.shape[3] for item in weights[0][0])
+    gate_rows, up_rows, down_rows = ffn_rows_of(hidden)
 
     def kernel(*refs):
-        gated_ref, weight_refs, rest = refs[0], nested(refs[1 : 1 + len(pieces)], lengths), refs[-3:]
-        order_ref, near_ref, far_ref = rest
-        places = blocks_of(order_ref, length)
-        half = width // 2
+        token_refs, way_refs, (scale_ref,), weight_refs, rest = split_refs(
+            refs, [2, 2, 1, len(pieces), 7]
+        )
+        weight_refs = nested(weight_refs, weights)
+        pair_refs, token_ref, way_ref = rest[:2], rest[2], rest[3]
+        active_ref, gate_ref, up_ref = rest[4:]
+        collect(token_refs, token_ref)
+        collect(way_refs, way_ref)
+        way_ref[...] = (way_ref[...].astype(WIDE) * scale_ref[...]).astype(LOW)
+        gate, upward = (
+            sum(crossed(token_ref[:, span[far]], both(weight_refs, far, rows)) for far in range(2))
+            for rows in (gate_rows, up_rows)
+        )
+        sigma = sigmoid(gate)
+        opened = gate * sigma
+        active_ref[...] = (opened * upward).astype(LOW)
+        grad = sum(
+            crossed(way_ref[:, span[far]], both(weight_refs, far, down_rows)) for far in range(2)
+        )
+        gate_ref[...] = (grad * upward * sigma * (1.0 + gate * (1.0 - sigma))).astype(LOW)
+        up_ref[...] = (grad * opened).astype(LOW)
         for far in range(2):
-            values = straight(
-                gated_ref[:, :HEAD], across(weight_refs[0][far], slice(None))
-            ) + straight(gated_ref[:, HEAD:], across(weight_refs[1][far], slice(None)))
-            deal(near_ref, far_ref, values, places, slice(far * half, (far + 1) * half))
-
-    inputs = [gated] + pieces + [order]
+            values = straight(gate_ref[...], both(weight_refs, far, gate_rows)) + straight(
+                up_ref[...], both(weight_refs, far, up_rows)
+            )
+            deal(pair_refs, values, span[far])
+
+    inputs = list(tokens) + list(ways) + [scales] + pieces
     in_specs = [whole(item) for item in inputs]
-    in_specs[0] = pl.BlockSpec((length, 2 * HEAD), lambda i: (i, 0))
-    in_specs[-1] = pl.BlockSpec(memory_space=pltpu.SMEM)
-    out = jax.ShapeDtypeStruct((length, width), LOW)
-    return call(kernel, inputs, in_specs, [whole(out)] * 2, [out] * 2, [], "column_branch", work=2)
-
-
-def column_ffn(tokens, directions, first, down, hidden):
-    share, width = tokens[0].shape
-    length = share * len(tokens) // 2
-    lengths = [lengths_of(first), lengths_of(down)]
-    pieces = [flat(first), flat(down)]
-    gate_rows, up_rows = slice(0, hidden), slice(hidden, 2 * hidden)
-
-    def kernel(*refs):
-        token_refs, way_refs, first_refs, down_refs, rest = split_refs(
-            refs, [len(tokens), len(tokens), len(pieces[0]), len(pieces[1]), 10]
-        )
-        first_refs, down_refs = nested(first_refs, lengths[0]), nested(down_refs, lengths[1])
-        near_ref, far_ref, token_ref, way_ref = rest[:4]
-        active_refs, gate_refs, up_refs = rest[4:6], rest[6:8], rest[8:10]
-        half = width // 2
-        order = [pl.ds(k * share, share) for k in range(len(tokens) // 2)]
-        collect(token_refs, token_ref, order)
-        collect(way_refs, way_ref, order)
-        lanes = [slice(0, half), slice(half, width)]
-        for i in range(2):
-            gate, upward = (
-                sum(
-                    crossed(token_ref[:, lanes[far]], across(first_refs[i][far], rows))
-                    for far in range(2)
-                )
-                for rows in (gate_rows, up_rows)
-            )
-            sigma = sigmoid(gate)
-            opened = gate * sigma
-            active_refs[i][...] = (opened * upward).astype(LOW)
-            grad = sum(
-                crossed(way_ref[:, lanes[far]], across(down_refs[i][far], slice(None)))
-                for far in range(2)
-            )
-            gate_refs[i][...] = (grad * upward * sigma * (1.0 + gate * (1.0 - sigma))).astype(LOW)
-            up_refs[i][...] = (grad * opened).astype(LOW)
-        for far in range(2):
-            values = sum(
-                straight(gate_refs[i][...], across(first_refs[i][far], gate_rows))
-                + straight(up_refs[i][...], across(first_refs[i][far], up_rows))
-                for i in range(2)
-            )
-            deal(near_ref, far_ref, values, order, lanes[far])
-
-    inputs = list(tokens) + list(directions) + pieces[0] + pieces[1]
+    in_specs[4] = pl.BlockSpec((length, 1), lambda i: (i, 0))
     out = jax.ShapeDtypeStruct((length, width), LOW)
     step = lambda lanes: pl.BlockSpec((length, lanes), lambda i: (i, 0))
     shape = lambda lanes: jax.ShapeDtypeStruct((2 * length, lanes), LOW)
-    near, far, all_tokens, all_ways, *rest = call(
+    return call(
         kernel,
         inputs,
-        [whole(item) for item in inputs],
-        [whole(out)] * 2 + [step(width)] * 2 + [step(hidden)] * 6,
-        [out] * 2 + [shape(width)] * 2 + [shape(hidden)] * 6,
+        in_specs,
+        [whole(out)] * 2 + [step(width)] * 2 + [step(2 * hidden)] * 3,
+        [out] * 2 + [shape(width)] * 2 + [shape(2 * hidden)] * 3,
         [],
         "column_ffn",
     )
-    return near, far, all_tokens, all_ways, rest[:2], rest[2:4], rest[4:6]
-
-
-def write_across(ref, rows, values):
-    size, _, _, strip = ref.shape
+
+
+def write_beside(ref, rows, lanes, values):
+    size = ref.shape[0]
+    strip = values.shape[1] // (2 * size)
     for z in range(size):
         for c in range(2):
             start = (2 * z + c) * strip
-            ref[z, c, rows] = values[:, start : start + strip].astype(LOW)
-
-
-def column_down(actives, ways, down, size, strip):
-    hidden = actives[0].shape[1]
-    tokens, width = ways.shape
-    length = tokens // 2
-    lengths = lengths_of(down)
-    pieces = flat(down)
-
-    def kernel(*refs):
-        active_refs, way_ref = refs[:2], refs[2]
-        down_refs = nested(refs[3 : 3 + len(pieces)], lengths)
-        near_ref, far_ref = refs[3 + len(pieces) : 5 + len(pieces)]
-        grad_refs = refs[5 + len(pieces) :]
-        half = width // 2
+            ref[z, c, rows, lanes] = values[:, start : start + strip].astype(LOW)
+
+
+def column_ffn_grads(active, gate_grad, up_grad, tokens, ways, weights, grad):
+    hidden = active.shape[1] // 2
+    count, width = ways.shape
+    length, half = count // 2, width // 2
+    pieces = flat(weights)
+    rows = ffn_rows_of(hidden)
+
+    def kernel(active_ref, gate_ref, up_ref, token_ref, way_ref, *refs):
+        weight_refs = nested(refs[: len(pieces)], weights)
+        near_ref, far_ref, *out = refs[len(pieces) :]
         for far in range(2):
             lanes = slice(far * half, (far + 1) * half)
-            values = sum(
-                straight(active_refs[i][...], across(down_refs[i][far], slice(None)))
-                for i in range(2)
-            ).astype(LOW)
+            values = straight(active_ref[...], both(weight_refs, far, rows[2])).astype(LOW)
             near_ref[:, lanes] = values[:length]
             far_ref[:, lanes] = values[length:]
-            for i in range(2):
-                write_across(
-                    grad_refs[2 * i + far],
-                    slice(None),
-                    turned(active_refs[i][...], way_ref[:, lanes]),
-                )
-
-    inputs = list(actives) + [ways] + pieces
+            for n, left_ref, right_ref in (
+                (0, gate_ref, token_ref), (1, up_ref, token_ref), (2, active_ref, way_ref)
+            ):
+                values = turned(left_ref[...], right_ref[:, lanes])
+                for i in range(2):
+                    write_beside(
+                        out[2 * i + far],
+                        rows[n],
+                        slice(None),
+                        values[i * hidden : (i + 1) * hidden],
+                    )
+
+    inputs = [active, gate_grad, up_grad, tokens, ways] + pieces
     out = jax.ShapeDtypeStruct((length, width), LOW)
-    grad = jax.ShapeDtypeStruct((size, 2, hidden, strip), LOW)
     near, far, *grads = call(
         kernel,
         inputs,
@@ -616,81 +609,40 @@
         [whole(out)] * 2 + [whole(grad)] * 4,
         [out] * 2 + [grad] * 4,
         [],
-        "column_down",
+        "column_ffn_grads",
         grid=1,
     )
     return near, far, [grads[:2], grads[2:]]
 
 
-def column_rows(chunks, rights, size, strip):
-    rows = [lefts[0].shape[1] for lefts in chunks]
-    width = rights.shape[1]
-
-    def kernel(*refs):
-        left_refs = refs[: 2 * len(chunks)]
-        right_ref = refs[2 * len(chunks)]
-        grad_refs = refs[2 * len(chunks) + 1 :]
-        half = width // 2
-        for i in range(2):
-            for far in range(2):
-                for n in range(len(chunks)):
-                    start = sum(rows[:n])
-                    write_across(
-                        grad_refs[2 * i + far],
-                        slice(start, start + rows[n]),
-                        turned(
-                            left_refs[2 * n + i][...], right_ref[:, far * half : (far + 1) * half]
-                        ),
-                    )
-
-    inputs = [left for lefts in chunks for left in lefts] + [rights]
-    grad = jax.ShapeDtypeStruct((size, 2, sum(rows), strip), LOW)
-    grads = call(
-        kernel,
-        inputs,
-        [whole(item) for item in inputs],
-        [whole(grad)] * 4,
-        [grad] * 4,
-        [],
-        "column_rows",
-        grid=1,
-    )
-    return [grads[:2], grads[2:]]
-
-
 def column_backward(
-    grads, out_weights, mix_weights, beta_weights, seg_col, seg_row, conv, head_gain, order,
-    saved, projected, beta_in,
+    grads, weights, beta_weights, seg_col, seg_row, conv, head_gain, saved, projected, beta_in
 ):
     count, _, length = seg_row.shape
     lines = conv.shape[0]
     width = grads[0].shape[1]
-    lengths = [lengths_of(out_weights), lengths_of(mix_weights)]
-    pieces = [flat(out_weights), flat(mix_weights)]
+    half = width // 2
+    span = [slice(0, half), slice(half, width)]
+    pieces = flat(weights)
 
     def kernel(*refs):
-        token_refs, out_refs, mix_refs, rest = split_refs(
-            refs, [len(grads), len(pieces[0]), len(pieces[1]), 20]
-        )
-        out_refs, mix_refs = nested(out_refs, lengths[0]), nested(mix_refs, lengths[1])
-        beta_ref, col_ref, row_ref, conv_ref, head_ref, order_ref = rest[:6]
-        inverse_ref, update_ref, mixed_ref, first_ref, second_ref, beta_in_ref = rest[6:12]
-        signal_ref, beta_grad_ref, conv_grad_ref, head_grad_ref = rest[12:16]
-        near_ref, far_ref, hold_ref = rest[16:]
-        places = blocks_of(order_ref, length)
-        collect(token_refs, hold_ref, places)
-        half = width // 2
-        lanes = [slice(0, half), slice(half, width)]
+        token_refs, weight_refs, rest = split_refs(refs, [2, len(pieces), 18])
+        weight_refs = nested(weight_refs, weights)
+        beta_ref, col_ref, row_ref, conv_ref, head_ref = rest[:5]
+        inverse_ref, update_ref, mixed_ref, first_ref, second_ref, beta_in_ref = rest[5:11]
+        signal_ref, beta_grad_ref, conv_grad_ref, head_grad_ref = rest[11:15]
+        pair_refs, hold_ref = rest[15:17], rest[17]
+        collect(token_refs, hold_ref)
         masks = masks_of(col_ref[...], row_ref[0])
         kept = kept_of(col_ref[...], conv_ref.shape[0] // 3)
         head_grad = jnp.zeros((1, HEAD), WIDE)
         beta_grads = []
+        grad = sum(
+            crossed(hold_ref[:, span[far]], both(weight_refs, far, slice(None), OUT))
+            for far in range(2)
+        )
         for head, projected_ref in enumerate((first_ref, second_ref)):
             own = head_lanes(head)
-            grad = sum(
-                crossed(hold_ref[:, lanes[far]], across(out_refs[head][far], slice(None)))
-                for far in range(2)
-            )
             signal_grads, beta_grad, conv_lines, gain_grad = backward_head(
                 [projected_ref[:, head_lanes(part)] for part in range(4)],
                 beta_in_ref[:, head : head + 1],
@@ -701,7 +653,7 @@
                 inverse_ref[0, head],
                 update_ref[:, own],
                 mixed_ref[:, own],
-                grad,
+                grad[:, own],
             )
             head_grad = head_grad + gain_grad
             beta_grads.append(beta_grad.astype(LOW).astype(WIDE))
@@ -715,27 +667,25 @@
             values = sum(
                 crossed(
                     signal_ref[:, 4 * HEAD * head : 4 * HEAD * (head + 1)],
-                    down_list(mix_refs[head][far]),
+                    atop(weight_refs[head][far], QKVG),
                 )
-                + beta_grads[head] * beta_ref[head : head + 1, lanes[far]].astype(WIDE)
+                + beta_grads[head] * beta_ref[head : head + 1, span[far]].astype(WIDE)
                 for head in range(2)
             )
-            deal(near_ref, far_ref, values, places, lanes[far])
+            deal(pair_refs, values, span[far])
 
     inputs = (
         list(grads)
-        + pieces[0]
-        + pieces[1]
-        + [beta_weights, seg_col, seg_row, conv, head_gain, order]
+        + pieces
+        + [beta_weights, seg_col, seg_row, conv, head_gain]
         + list(saved)
         + list(projected)
         + [beta_in]
     )
     in_specs = [whole(item) for item in inputs]
     step = lambda lanes: pl.BlockSpec((length, lanes), lambda i: (i, 0))
-    in_specs[-11] = step(1)
-    in_specs[-10] = pl.BlockSpec((1, 1, length), lambda i: (i, 0, 0))
-    in_specs[-7] = pl.BlockSpec(memory_space=pltpu.SMEM)
+    in_specs[-10] = step(1)
+    in_specs[-9] = pl.BlockSpec((1, 1, length), lambda i: (i, 0, 0))
     in_specs[-6:] = saved_specs(length) + [step(4 * HEAD), step(4 * HEAD), step(2)]
     out = jax.ShapeDtypeStruct((length, width), LOW)
     return call(
@@ -751,20 +701,26 @@
     )
 
 
-def column_mix(mixer_in, signal_grads):
-    width = mixer_in.shape[1]
-
-    def kernel(mixer_ref, signal_ref, *grad_refs):
-        half = width // 2
+def column_mixer_grads(mixer_in, signal_grads, gated, ways, grad):
+    half = mixer_in.shape[1] // 2
+    strip = grad.shape[2]
+
+    def kernel(mixer_ref, signal_ref, gated_ref, way_ref, *grad_refs):
         for far in range(2):
+            lanes = slice(far * half, (far + 1) * half)
+            outs = turned(gated_ref[...], way_ref[:, lanes])
             for head in range(2):
-                grad_refs[2 * head + far][...] = turned(
-                    mixer_ref[:, far * half : (far + 1) * half],
-                    signal_ref[:, 4 * HEAD * head : 4 * HEAD * (head + 1)],
+                ref = grad_refs[2 * head + far]
+                values = turned(
+                    mixer_ref[:, lanes], signal_ref[:, 4 * HEAD * head : 4 * HEAD * (head + 1)]
                 ).astype(LOW)
-
-    inputs = [mixer_in, signal_grads]
-    grad = jax.ShapeDtypeStruct((width // 2, 4 * HEAD), LOW)
+                for z in range(ref.shape[0]):
+                    for c in range(2):
+                        start = (2 * z + c) * strip
+                        ref[z, c, :, QKVG] = values[start : start + strip]
+                write_beside(ref, slice(None), OUT, outs[head_lanes(head)])
+
+    inputs = [mixer_in, signal_grads, gated, ways]
     grads = call(
         kernel,
         inputs,
@@ -772,7 +728,7 @@
         [whole(grad)] * 4,
         [grad] * 4,
         [],
-        "column_mix",
+        "column_mixer_grads",
         grid=1,
     )
     return [grads[:2], grads[2:]]
@@ -1234,32 +1190,43 @@
     return values.astype(WIDE)
 
 
-def scatter_columns(grid):
+def scatter_send(grid):
     half = grid[0][0].shape[0] // 2
-    sent = swap_mp(jnp.concatenate([grid[1][0][:half], grid[1][1][:half]], 0))
-    top = wide(grid[0][1][:half]) + wide(sent[half:])
-    top = wide(grid[0][0][:half]) + wide(sent[:half]) + wide(swap_across(top.astype(LOW)))
-    rest = grid[0][0].shape[0] - half
-    sent = swap_across(jnp.concatenate([grid[0][1][half:], grid[1][1][half:]], 0))
-    low = wide(grid[1][0][half:]) + wide(sent[rest:])
-    low = wide(grid[0][0][half:]) + wide(sent[:rest]) + wide(swap_mp(low.astype(LOW)))
+    return (
+        jnp.concatenate([grid[1][0][:half], grid[1][1][:half]], 0),
+        jnp.concatenate([grid[0][1][half:], grid[1][1][half:]], 0),
+    )
+
+
+def scatter_turn(grid, sent):
+    half = grid[0][0].shape[0] // 2
+    top = wide(grid[0][1][:half]) + wide(sent[0][half:])
+    low = wide(grid[1][0][half:]) + wide(sent[1][half:])
+    return top.astype(LOW), low.astype(LOW)
+
+
+def scatter_end(grid, sent, back):
+    half = grid[0][0].shape[0] // 2
+    top = wide(grid[0][0][:half]) + wide(sent[0][:half]) + wide(swap_across(back[0]))
+    low = wide(grid[0][0][half:]) + wide(sent[1][:half]) + wide(swap_mp(back[1]))
     return jnp.concatenate([top, low], 0).astype(LOW)
 
 
-def column_blocks(values):
-    mine = [values] + [swap_dp(values, k) for k in range(1, lax.axis_size("dp"))]
-    return mine + [swap_core(block) for block in mine]
-
-
-def column_total(near, far):
+def column_tokens(values):
     size = lax.axis_size("dp")
-    share = near.shape[0] // size
-    chip = wide(near) + wide(swap_core(far))
-    total = chip[:share]
-    low = [chip[k * share : (k + 1) * share].astype(LOW) for k in range(1, size)]
-    for k in range(1, size):
-        total = total + wide(swap_dp(low[k - 1], k))
-    return total, low[0]
+    moved = [values] + [swap_dp(values, k) for k in range(1, size)]
+    mine = jnp.concatenate(by_difference(moved, lax.axis_index("dp")), 0)
+    return [mine, swap_core(mine)]
+
+
+def column_chip(near, far):
+    return (wide(near) + wide(swap_core(far))).astype(LOW)
+
+
+def column_total(chip):
+    size = lax.axis_size("dp")
+    moved = exchange(chip, "dp").reshape(size, chip.shape[0] // size, -1)
+    return jnp.sum(wide(moved), 0)
 
 
 def column_body(
@@ -1304,11 +1271,13 @@
         values = jnp.stack(halves_of, -2).reshape(lead + (2, size, 2, strip))
         return jnp.swapaxes(values, -2, -3).reshape(lead + (2 * span,))
 
-    def tokens_in(values):
+    def over_dp(values):
         values = values.reshape(micro, size, share, width)
         moved = trade_blocks([values[:, z] for z in range(size)], "dp", place)
         moved = jnp.where(at_far_side, jnp.stack(moved[2:]), jnp.stack(moved[:2]))
-        moved = moved.reshape(4, share, width)
+        return moved.reshape(4, share, width)
+
+    def over_dmod(moved):
         moved = trade_blocks([moved[j] for j in range(4)], "dmod", dmod)
         return to_column(jnp.concatenate(moved, 1))
 
@@ -1321,25 +1290,21 @@
 
     blocks = w_mix.reshape(strip, 4, 2, size, HEAD).transpose(2, 3, 0, 1, 4)
     blocks = blocks.reshape(2, size, strip, 4 * HEAD)
+    blocks = jnp.concatenate([blocks, w_out.reshape(2, size, HEAD, strip)], 3)
     mix_blocks = chip_blocks(at_core, (blocks[0], blocks[1]))
-    block_input, w_out, w_ffn_in, w_ffn_down, conv_kernel = after(
-        (block_input, w_out, w_ffn_in, w_ffn_down, conv_kernel), mix_blocks
-    )
     mix_pieces = exchange(mix_blocks, "dp")
-    tokens_low = tokens_in(block_input)
-    rows = wide(tokens_low)
-    mix_weights = gather_columns(mix_pieces)
-    mix_weights = [
-        [[item.reshape(-1, 4 * HEAD) for item in items] for items in pair] for pair in mix_weights
-    ]
-    token_blocks = column_blocks(tokens_low)
-    out_pieces = along_column(
-        at_core, tuple(w_out.reshape(2, size, HEAD, strip)), (mix_pieces, token_blocks[3])
-    )
-    ffn_rows = w_ffn_in.transpose(1, 2, 0).reshape(2, 2, size, hidden, strip)
-    blocks = jnp.concatenate([ffn_rows[0], ffn_rows[1]], 2)
-    first_pieces = along_column(at_core, (blocks[0], blocks[1]), out_pieces)
-    out_weights = gather_columns(out_pieces, mix_weights[1][1])
+    block_input, cotangent, conv_kernel, w_ffn_in, w_ffn_down = after(
+        (block_input, cotangent, conv_kernel, w_ffn_in, w_ffn_down), mix_blocks
+    )
+    blocks = jnp.concatenate(
+        [
+            w_ffn_in.transpose(1, 2, 0).reshape(2, 2 * size, hidden, strip),
+            w_ffn_down.reshape(1, 2 * size, hidden, strip),
+        ],
+        0,
+    )
+    blocks = blocks.transpose(1, 0, 2, 3).reshape(2, size, 3 * hidden, strip)
+    ffn_blocks = chip_blocks(at_core, (blocks[0], blocks[1]))
 
     small = [
         conv_kernel.reshape(-1),
@@ -1357,6 +1322,15 @@
     packs = jnp.stack(turn(at_core, (packs, swap_core(packs))))
     packs = jnp.stack(turn(at_far_row, (packs, swap_across(packs))))
     packs = packs.reshape(2, 2, 2, size, -1)
+
+    tokens_low, way_moved = over_dp(block_input), over_dp(cotangent)
+    tokens_low = over_dmod(after(tokens_low, (mix_pieces, packs, ffn_blocks)))
+    rows = wide(tokens_low)
+    tokens_pair = column_tokens(tokens_low)
+    mix_weights = gather_columns(mix_pieces)
+    ffn_pieces = exchange(ffn_blocks, "dp")
+    way_low = over_dmod(after(way_moved, tokens_pair[0]))
+
     fields = []
     start = 0
     for item in small:
@@ -1399,44 +1373,40 @@
     names = jnp.arange(groups, dtype=jnp.int32)
     counts = jnp.sum((all_groups[:, None] == names[None]).astype(WIDE), 0)
     table = group_weight * (all_groups.shape[0] / groups) / counts
-    own_groups = lax.dynamic_slice_in_dim(
-        all_groups, (sequence * micro + core) * length + place * share, share, 0
-    )
+    own_groups = lax.dynamic_slice_in_dim(all_groups, sequence * micro * length, micro * length, 0)
     scales = jnp.sum((own_groups[:, None] == names[None]).astype(WIDE) * table, -1, keepdims=True)
-
-    order = jnp.arange(size, dtype=jnp.int32) ^ place
-    constants = [beta_weights, seg_col, seg_row, conv, head_gain, order]
-    gated, inverse, update, mixed, mixer_in, *projected, beta_in = column_forward(
-        token_blocks, mix_weights, gain_one, *constants
-    )
-    branch, mark = column_total(*column_branch(gated, out_weights, order, length))
-    first_weights = gather_columns(first_pieces, mix_weights[1][1], gated)
-    middle = rows + branch
+    scales = jnp.concatenate(turn(at_core, (scales[:length], scales[length:])), 0)
+
+    constants = [beta_weights, seg_col, seg_row, conv, head_gain]
+    gated, inverse, update, mixed, mixer_in, *projected, beta_in, near, far = column_forward(
+        tokens_pair, mix_weights, gain_one, *constants
+    )
+    middle = rows + column_total(after(column_chip(near, far), ffn_pieces))
 
     second_scale = lax.rsqrt(jnp.mean(middle * middle, -1, keepdims=True) + 1e-06)
     ffn_low = (middle * second_scale * gain_two).astype(LOW)
-    ffn_blocks = column_blocks(ffn_low)
-    down_pieces = along_column(
-        at_core, tuple(w_ffn_down.reshape(2, size, hidden, strip)), (first_pieces, ffn_low)
-    )
-    down_weights = gather_columns(down_pieces, first_weights[1][1])
-    direction = wide(tokens_in(after(cotangent, token_blocks[3]))) * scales
-    direction_blocks = column_blocks(after(direction.astype(LOW), ffn_blocks[3]))
-    near, far, ffn_in, directions, actives, gate_grads, up_grads = column_ffn(
-        ffn_blocks, direction_blocks, first_weights, down_weights, hidden
-    )
-    ffn_in_grad, mark = column_total(near, far)
-    near, far, down_grads = column_down(
-        after(actives, mark), directions, down_weights, size, strip
-    )
-    ffn_grads = column_rows([after(gate_grads, mark), up_grads], ffn_in, size, strip)
-
-    def placed(grid, earlier=None):
-        total = scatter_columns(grid)
-        return along_column(at_core, (total[:, 0], total[:, 1]), earlier)
-
-    def stacked(pieces):
-        return pieces.transpose(1, 0, 2, 3).reshape(2 * size, -1, strip)
+    way_pair = column_tokens(after(way_low, middle))
+    direction = wide(way_low) * lax.dynamic_slice_in_dim(scales, place * share, share, 0)
+    ffn_pair = column_tokens(ffn_low)
+    ffn_weights = gather_columns(ffn_pieces, mix_weights[1][1])
+    near, far, ffn_in, directions, active, gate_grad, up_grad = column_ffn(
+        ffn_pair, way_pair, scales, ffn_weights, hidden
+    )
+    chip = column_chip(near, far)
+    ffn_in_grad = column_total(chip)
+    near, far, ffn_grads = column_ffn_grads(
+        after(active, chip),
+        gate_grad,
+        up_grad,
+        ffn_in,
+        directions,
+        ffn_weights,
+        jax.ShapeDtypeStruct((size, 2, 3 * hidden, strip), LOW),
+    )
+    out_chip = column_chip(near, far)
+    ffn_sent = scatter_send(ffn_grads)
+    ffn_in_grad = after(ffn_in_grad, out_chip)
+    ffn_sent = swap_mp(ffn_sent[0]), swap_across(ffn_sent[1])
 
     weighted_two = ffn_in_grad * gain_two
     norm_two_grad = jnp.sum(ffn_in_grad * middle * second_scale, 0, keepdims=True)
@@ -1444,56 +1414,58 @@
     middle_grad = (
         direction + second_scale * weighted_two - middle * (second_scale**3 * inner_two)
     )
-    branch_low = middle_grad.astype(LOW)
-    branch_blocks = column_blocks(branch_low)
-    down_pieces = placed(down_grads, branch_blocks[3])
-    ffn_pieces = placed(ffn_grads, down_pieces)
-    down_out = wide(stacked(down_pieces).reshape(-1, strip))
-    ffn_out = stacked(ffn_pieces).reshape(2 * size, 2, hidden, strip)
-    ffn_out = wide(ffn_out.transpose(1, 0, 2, 3).reshape(2, -1, strip).transpose(2, 0, 1))
-    down_sum, _ = column_total(near, after(far, branch_blocks[3]))
-    out = tokens_out((middle + down_sum).astype(LOW))
+    branch_pair = column_tokens(middle_grad.astype(LOW))
+    down_sum = column_total(after(out_chip, branch_pair[0]))
+    ffn_back = scatter_turn(ffn_grads, ffn_sent)
 
     signal_grads, beta_grad, conv_grad, head_grad, near, far, branch_all = column_backward(
-        branch_blocks,
-        out_weights,
+        branch_pair,
         mix_weights,
         *constants,
         (inverse, update, mixed),
         projected,
         beta_in,
     )
-    mix_grads = column_mix(mixer_in, signal_grads)
-    mixer_grad, _ = column_total(near, far)
-    gated_heads = [gated[:, :HEAD], gated[:, HEAD:]]
-    out_grads = column_rows(
-        [after(gated_heads, mix_grads[1][1])], branch_all, size, strip
-    )
-    out_pieces = placed(out_grads, ffn_pieces)
-    out_out = wide(stacked(out_pieces).reshape(-1, strip))
-    mix_total = scatter_columns(mix_grads).reshape(size, 2, strip, 4 * HEAD)
-    mix_pieces = along_column(
-        at_core, (mix_total[:, 0], mix_total[:, 1]), out_pieces
-    )
-    mix_out = wide(
-        mix_pieces.reshape(size, 2, strip, 4, HEAD).transpose(2, 3, 1, 0, 4).reshape(strip, 4, -1)
-    )
+    mix_grads = column_mixer_grads(
+        mixer_in,
+        signal_grads,
+        gated,
+        branch_all,
+        jax.ShapeDtypeStruct((size, 2, strip, 5 * HEAD), LOW),
+    )
+    chip = column_chip(near, far)
+    mixer_grad = column_total(chip)
+    ffn_total = scatter_end(ffn_grads, ffn_sent, ffn_back)
+    mix_sent = scatter_send(mix_grads)
+    mix_sent = after((swap_mp(mix_sent[0]), swap_across(mix_sent[1])), mixer_grad)
+    mix_total = scatter_end(mix_grads, mix_sent, scatter_turn(mix_grads, mix_sent))
+    out_low = (middle + after(down_sum, mixer_grad)).astype(LOW)
+
+    def placed(total, earlier=None):
+        return along_column(at_core, (total[:, 0], total[:, 1]), earlier).transpose(1, 0, 2, 3)
+
+    ffn_pieces = placed(ffn_total)
+    ffn_out = wide(
+        ffn_pieces[:, :, : 2 * hidden]
+        .reshape(2 * size, 2, hidden, strip)
+        .transpose(1, 0, 2, 3)
+        .reshape(2, -1, strip)
+        .transpose(2, 0, 1)
+    )
+    down_out = wide(ffn_pieces[:, :, 2 * hidden :].reshape(-1, strip))
+    mix_pieces = placed(mix_total, ffn_pieces).reshape(2 * size, strip, 5, HEAD)
+    mix_out = wide(mix_pieces[:, :, :4].transpose(1, 2, 0, 3).reshape(strip, 4, -1))
+    out_out = wide(mix_pieces[:, :, 4].reshape(-1, strip))
     beta_weight_grad = contract(beta_grad.astype(LOW), mixer_in, 0, 0)
     weighted_one = mixer_grad * gain_one
     first_scale = lax.rsqrt(jnp.mean(rows * rows, -1, keepdims=True) + 1e-06)
     norm_one_grad = jnp.sum(mixer_grad * rows * first_scale, 0, keepdims=True)
     inner_one = jnp.mean(weighted_one * rows, -1, keepdims=True)
-    grad_input = wide(
-        tokens_out(
-            (
-                middle_grad + first_scale * weighted_one - rows * (first_scale**3 * inner_one)
-            ).astype(LOW)
-        )
-    )
-
-    def over_columns(values):
-        values = values + swap_mp(values)
-        return values + swap_across(values)
+    grad_low = (
+        middle_grad + first_scale * weighted_one - rows * (first_scale**3 * inner_one)
+    ).astype(LOW)
+    out = tokens_out(out_low)
+    grad_input = wide(tokens_out(grad_low))
 
     conv_sides = jnp.stack(turn(at_far_side, jnp.split(jnp.sum(conv_grad, 0), 2, axis=1)))
     beta_sides = from_column(
@@ -1503,15 +1475,16 @@
         [
             conv_sides.reshape(-1, HEAD),
             beta_sides.reshape(-1, HEAD),
+            from_column(norm_one_grad).reshape(-1, HEAD),
             from_column(norm_two_grad).reshape(-1, HEAD),
             jnp.sum(head_grad, 0),
         ]
     )
-    vector = over_columns(vector)
+    vector = vector + swap_mp(vector)
+    vector = vector + swap_across(vector)
     vectors = jnp.stack(turn(at_core, (vector, swap_core(vector))))
     vectors = everyone(vectors, place)
     ends = [2 * lines, 2 * lines + 4 * span // HEAD]
-    ends.append(ends[1] + 2 * span // HEAD)
     own_width = dmod * width + place * strip
     taps_own = conv_kernel.shape[2]
     at = (dmod * size + place) * taps_own
@@ -1532,16 +1505,11 @@
         .reshape(strip, group_heads)
     )
     sums = jnp.sum(vectors[:, :, ends[1] :], (0, 1))
-    norm_two_out = lax.dynamic_slice_in_dim(sums[:-1].reshape(-1), own_width, strip, 0)
+    norms = sums[:-1].reshape(2, -1)
+    norm_one_out, norm_two_out = (
+        lax.dynamic_slice_in_dim(norms[i], own_width, strip, 0) for i in (0, 1)
+    )
     head_out = lax.dynamic_slice_in_dim(sums[-1], place * head_norm.size, head_norm.size, 0)
-    last = over_columns(from_column(norm_one_grad).reshape(-1, HEAD))
-    last = last + swap_core(last)
-    bit = 1
-    while bit < size:
-        last = last + swap_dp(last, bit)
-        bit *= 2
-    last = last.reshape(-1)
-    norm_one_out = lax.dynamic_slice_in_dim(last, own_width, strip, 0)
     return (
         out,
         grad_input,

time: 650 us -> 554 us (0.85)
  waiting for transfers between devices: 280 us -> 210 us
  starting transfers between devices: 152 us -> 130 us
  local copies, waits for them, and re-layouts: 59 us -> 71.9 us
  other arithmetic: 70.6 us -> 59 us
    ppermute x30 -> x16, waiting for transfers between devices: 133 us -> 63.8 us  [swap_dp(): lax.ppermute(values, 'dp', [(i, i ^ k) for i in range(lax.axis_size('dp'))])]
    ppermute x30 -> x16, starting transfers between devices: 41.1 us -> 24 us  [swap_dp(): lax.ppermute(values, 'dp', [(i, i ^ k) for i in range(lax.axis_size('dp'))])]
    all_to_all x8, waiting for transfers between devices: 51.5 us -> 37.1 us  [exchange(): return lax.all_to_all(values, axis, 0, 0, tiled=True)]
    unnamed x281 -> x144, local copies, waits for them, and re-layouts: 16 us -> 27.7 us
    slice x20 -> x8, local copies, waits for them, and re-layouts: 12.7 us -> 2.37 us  [the longest x2 0.97 us: scatter_send(): grid[0][1][half:]]
    all_to_all x8, starting transfers between devices: 47.5 us -> 57.5 us  [exchange(): return lax.all_to_all(values, axis, 0, 0, tiled=True)]
    ppermute x21 -> x12, waiting for transfers between devices: 40.4 us -> 48.5 us  [swap_mp(): return lax.ppermute(values, 'mp', SWAP)]
    ppermute x19 -> x10, waiting for transfers between devices: 22.2 us -> 30 us  [swap_across(): return lax.ppermute(values, 'dmod', ACROSS)]
  transfers between devices with their start and end apart: 133 -> 84, of which waited for: 56 -> 33; matrix products, arithmetic and copies ran while one was open for 16% -> 19% of each run, Pallas kernels for 9% -> 10%
where the time goes in v3:
time: 554 us; the launch traced here: 547 us
  waiting for transfers between devices  210 us (38%)
  starting transfers between devices  130 us (23%)
  local copies, waits for them, and re-layouts  71.9 us (13%)
  Pallas kernels  71.5 us (13%)
  other arithmetic  59 us (11%)
    pallas_call x5, Pallas kernels, call(): pl.pallas_call(kernel, grid=(grid,), in_specs=in_specs, out_specs=out_spe...  71.5 us
    ppermute x16, waiting for transfers between devices, swap_dp(): lax.ppermute(values, 'dp', [(i, i ^ k) for i in range(lax.axis_size('dp'))])  63.8 us
    all_to_all x8, starting transfers between devices, exchange(): return lax.all_to_all(values, axis, 0, 0, tiled=True)  57.5 us
    ppermute x12, waiting for transfers between devices, swap_mp(): return lax.ppermute(values, 'mp', SWAP)  48.5 us
    all_to_all x8, waiting for transfers between devices, exchange(): return lax.all_to_all(values, axis, 0, 0, tiled=True)  37.1 us
    ppermute x10, waiting for transfers between devices, swap_across(): return lax.ppermute(values, 'dmod', ACROSS)  30 us
    unnamed x144, local copies, waits for them, and re-layouts  27.7 us
    ppermute x16, starting transfers between devices, swap_dp(): lax.ppermute(values, 'dp', [(i, i ^ k) for i in range(lax.axis_size('dp'))])  24 us
  transfers between devices with their start and end apart: 84, of which 33 were waited for; matrix products, arithmetic and copies ran while one was open for 19% of the time, Pallas kernels for 10%

profile of v3, /device:TPU:16, one launch (start us, length us, event | category | flops | bytes accessed | tf_op | source)
XLA Modules:
  0.0 546.5 jit_solution(719073874690966808)
XLA Ops:
  17.3 7.1 %all-to-all-start = ((bf16[4,2,128,640]{3,2,1,0:T(8,128)(2,1)}), bf16[4,2,128,640]{3,2,1,0:T(8,128)(2,1)}, u32[]{:S(2)}, u32[]{:S(2)}) async-start(bf16[4,2,128,640]{3,2,1,0:T(8,128)(2,1)} %copy.372), calls=%async_computation | async-start | bytes 2621440 | tf_op jit(solution)/shard_map/all_to_all | solution.py:1113
  61.4 4.3 collective-permute-start.14
  67.1 14.4 %collective-permute-done.13 = bf16[64,2048]{1,0:T(8,128)(2,1)S(1)} collective-permute-done((bf16[64,2048]{1,0:T(8,128)(2,1)S(1)}, bf16[64,2048]{1,0:T(8,128)(2,1)S(1)}, u32[]{:S(2)}, u32[]{:S(2)}) %collective-permute-start.13) | collective-permute-done | bytes 262176 | tf_op jit(solution)/shard_map/ppermute | solution.py:1129
  85.2 8.1 %all-to-all-start.1 = ((bf16[4,2,1056,128]{3,2,1,0:T(8,128)(2,1)}), bf16[4,2,1056,128]{3,2,1,0:T(8,128)(2,1)}, u32[]{:S(2)}, u32[]{:S(2)}) async-start(bf16[4,2,1056,128]{3,2,1,0:T(8,128)(2,1)} %pad_maximum_fusion), calls=%async_computation.1 | async-start | bytes 4325376 | tf_op jit(solution)/shard_map/all_to_all | solution.py:1113
  98.2 12.8 %collective-permute-done.19.refs_5_ = bf16[2,2,128,640]{3,2,1,0:T(8,128)(2,1)S(1)} collective-permute-done((bf16[2,2,128,640]{3,2,1,0:T(8,128)(2,1)S(1)}, bf16[2,2,128,640]{3,2,1,0:T(8,128)(2,1)S(1)}, u32[]{:S(2)}, u32[]{:S(2)}) %collective-permute-start.19) | collective-permute-done | bytes 655392 | tf_op jit(solution)/shard_map/ppermute | solution.py:1125
  112.7 17.5 %column_forward.1 = (bf16[512,256]{1,0:T(8,128)(2,1)S(1)}, f32[2,2,256,256]{3,2,1,0:T(8,128)S(1)}, f32[512,256]{1,0:T(8,128)S(1)}, f32[512,256]{1,0:T(8,128)S(1)...) custom-call(bf16[256,2048]{1,0:T(8,128)(2,1)} %copy-done.46, ...), custom_call_target="tpu_custom_call" | custom-call | flops 10000000000 | bytes 8388608 | tf_op jit(solution)/shard_map/column_forward/pallas_call | solution.py:419
  135.1 3.3 collective-permute-start.28
  139.8 6.9 %all-to-all-done.1.refs_5_.refs_0_ = bf16[4,2,1056,128]{3,2,1,0:T(8,128)(2,1)} async-done(((bf16[4,2,1056,128]{3,2,1,0:T(8,128)(2,1)}), bf16[4,2,1056,128]{3,2,1,0:T(8,128)(2,1)}, u32[]{:S(2)}, u32[]{:S(2)}) %all-to-all-start.1) | async-done | bytes 2162720 | tf_op jit(solution)/shard_map/all_to_all | solution.py:1113
  146.7 7.4 %all-to-all-start.2 = ((bf16[4,64,2048]{2,1,0:T(8,128)(2,1)}), bf16[4,64,2048]{2,1,0:T(8,128)(2,1)S(1)}, u32[]{:S(2)}, u32[]{:S(2)}) async-start(bf16[4,64,2048]{2,1,0:T(8,128)(2,1)} %bitcast.53), calls=%async_computation.2 | async-start | bytes 2097152 | tf_op jit(solution)/shard_map/all_to_all | solution.py:1113
  160.0 15.1 %all-to-all-done.2 = bf16[4,64,2048]{2,1,0:T(8,128)(2,1)S(1)} async-done(((bf16[4,64,2048]{2,1,0:T(8,128)(2,1)}), bf16[4,64,2048]{2,1,0:T(8,128)(2,1)S(1)}, u32[]{:S(2)}, u32[]{:S(2)}) %all-to-all-start.2) | async-done | bytes 1048608 | tf_op jit(solution)/shard_map/all_to_all | solution.py:1113
  176.2 4.2 collective-permute-start.23
  181.2 24.8 %collective-permute-done.37.refs_7_.refs_2_ = bf16[4,2,1056,128]{3,2,1,0:T(8,128)(2,1)} collective-permute-done((bf16[4,2,1056,128]{3,2,1,0:T(8,128)(2,1)}, bf16[4,2,1056,128]{3,2,1,0:T(8,128)(2,1)}, u32[]{:S(2)}, u32[]{:S(2)}) %collective-permute-start.37) | collective-permute-done | bytes 2162720 | tf_op jit(solution)/shard_map/ppermute | solution.py:1117
  213.9 3.3 collective-permute-start.33
  217.4 15.6 %collective-permute-done.32 = bf16[64,2048]{1,0:T(8,128)(2,1)S(1)} collective-permute-done((bf16[64,2048]{1,0:T(8,128)(2,1)S(1)}, bf16[64,2048]{1,0:T(8,128)(2,1)S(1)}, u32[]{:S(2)}, u32[]{:S(2)}) %collective-permute-start.32) | collective-permute-done | bytes 262176 | tf_op jit(solution)/shard_map/ppermute | solution.py:1129
  237.8 17.4 %column_ffn.1 = (bf16[256,2048]{1,0:T(8,128)(2,1)S(1)}, bf16[256,2048]{1,0:T(8,128)(2,1)}, bf16[512,2048]{1,0:T(8,128)(2,1)}, bf16[512,2048]{1,0:T(8,128)(2,1)},...) custom-call(bf16[256,2048]{1,0:T(8,128)(2,1)S(1)} %pad_maximum_fusion.10.refs_0_, ...), custom_call_target="tpu_custom_call" | custom-call | flops 10000000000 | bytes 8388608 | tf_op jit(solution)/shard_map/column_ffn/pallas_call | solution.py:419
  262.1 7.9 %all-to-all-start.3 = ((bf16[4,64,2048]{2,1,0:T(8,128)(2,1)}), bf16[4,64,2048]{2,1,0:T(8,128)(2,1)}, u32[]{:S(2)}, u32[]{:S(2)}) async-start(bf16[4,64,2048]{2,1,0:T(8,128)(2,1)} %bitcast.491), calls=%async_computation.3 | async-start | bytes 2097152 | tf_op jit(solution)/shard_map/all_to_all | solution.py:1113
  271.2 13.6 %column_ffn_grads.1 = (bf16[256,2048]{1,0:T(8,128)(2,1)S(1)}, bf16[256,2048]{1,0:T(8,128)(2,1)S(1)}, bf16[4,2,1056,128]{3,2,1,0:T(8,128)(2,1)}, bf16[4,2,1056,12...) custom-call(bf16[512,704]{1,0:T(8,128)(2,1)S(1)} %copy-done.10, ...), custom_call_target="tpu_custom_call" | custom-call | flops 10000000000 | bytes 8388608 | tf_op jit(solution)/shard_map/column_ffn_grads/pallas_call | solution.py:419
  301.2 16.5 %collective-permute-done.42 = bf16[64,2048]{1,0:T(8,128)(2,1)S(1)} collective-permute-done((bf16[64,2048]{1,0:T(8,128)(2,1)S(1)}, bf16[64,2048]{1,0:T(8,128)(2,1)S(1)}, u32[]{:S(2)}, u32[]{:S(2)}) %collective-permute-start.42) | collective-permute-done | bytes 262176 | tf_op jit(solution)/shard_map/ppermute | solution.py:1129
  321.9 7.8 %all-to-all-start.4 = ((bf16[4,64,2048]{2,1,0:T(8,128)(2,1)}), bf16[4,64,2048]{2,1,0:T(8,128)(2,1)}, u32[]{:S(2)}, u32[]{:S(2)}) async-start(bf16[4,64,2048]{2,1,0:T(8,128)(2,1)} %bitcast.490), calls=%async_computation.4 | async-start | bytes 2097152 | tf_op jit(solution)/shard_map/all_to_all | solution.py:1113
  329.7 9.8 %collective-permute-done.71 = bf16[4,2,1056,128]{3,2,0,1:T(8,128)(2,1)} collective-permute-done((bf16[4,2,1056,128]{3,2,0,1:T(8,128)(2,1)}, bf16[4,2,1056,128]{3,2,0,1:T(8,128)(2,1)}, u32[]{:S(2)}, u32[]{:S(2)}) %collective-permute-start.71) | collective-permute-done | bytes 2162720 | tf_op jit(solution)/shard_map/ppermute | solution.py:1117
  346.1 16.8 %column_backward.1 = (bf16[512,1024]{1,0:T(8,128)(2,1)S(1)}, f32[512,2]{1,0:T(8,128)S(1)}, f32[2,12,256]{2,1,0:T(8,128)S(1)}, f32[2,1,128]{2,1,0:T(1,128)S(1)}, ...) custom-call(bf16[256,2048]{1,0:T(8,128)(2,1)} %pad_maximum_fusion.12.refs_0_, ...), custom_call_target="tpu_custom_call" | custom-call | flops 10000000000 | bytes 8388608 | tf_op jit(solution)/shard_map/column_backward/pallas_call | solution.py:419
  368.8 6.2 %column_mixer_grads.1 = (bf16[4,2,128,640]{3,2,1,0:T(8,128)(2,1)S(1)}, bf16[4,2,128,640]{3,2,1,0:T(8,128)(2,1)S(1)}, bf16[4,2,128,640]{3,2,1,0:T(8,128)(2,1)S(1)}, bf16[4,2,128,640]{3,2,1,0:T(8,128)(2,1)}) custom-call(bf16[512,2048]{1,0:T(8,128)(2,1)} %get-tuple-element.97.mixer_ref, bf16[512,1024]{1,0:T(8,128)(2,1)S(1)} %copy-done.8, ...), custom_call_target="tpu_custom_call" | custom-call | flops 10000000000 | bytes 8388608 | tf_op jit(solution)/shard_map/column_mixer_grads/pallas_call | solution.py:419
  388.3 5.3 all-to-all-start.5
  403.1 13.4 %all-to-all-done.5 = bf16[4,64,2048]{2,1,0:T(8,128)(2,1)} async-done(((bf16[4,64,2048]{2,1,0:T(8,128)(2,1)}), bf16[4,64,2048]{2,1,0:T(8,128)(2,1)}, u32[]{:S(2)}, u32[]{:S(2)}) %all-to-all-start.5) | async-done | bytes 1048608 | tf_op jit(solution)/shard_map/all_to_all | solution.py:1113
  416.4 7.8 %all-to-all-start.6 = ((bf16[4,2,1056,128]{3,2,1,0:T(8,128)(2,1)}), bf16[4,2,1056,128]{3,2,1,0:T(8,128)(2,1)}, u32[]{:S(2)}, u32[]{:S(2)}) async-start(bf16[4,2,1056,128]{3,2,1,0:T(8,128)(2,1)} %copy.413), calls=%async_computation.6 | async-start | bytes 4325376 | tf_op jit(solution)/shard_map/all_to_all | solution.py:1113
  443.5 15.1 %collective-permute-done.62 = f32[89,128]{1,0:T(8,128)S(1)} collective-permute-done((f32[89,128]{1,0:T(8,128)S(1)}, f32[89,128]{1,0:T(8,128)S(1)}, u32[]{:S(2)}, u32[]{:S(2)}) %collective-permute-start.62) | collective-permute-done | bytes 45600 | tf_op jit(solution)/shard_map/ppermute | solution.py:1125
  464.2 8.0 %collective-permute-done.64 = f32[1,2,89,128]{3,2,1,0:T(8,128)S(1)} collective-permute-done((f32[1,2,89,128]{3,2,1,0:T(8,128)S(1)}, f32[1,2,89,128]{3,2,1,0:T(8,128)S(1)}, u32[]{:S(2)}, u32[]{:S(2)}) %collective-permute-start.64) | collective-permute-done | bytes 91168 | tf_op jit(solution)/shard_map/ppermute | solution.py:1129
  472.2 3.4 collective-permute-start.65
  475.6 6.2 %collective-permute-done.50 = bf16[2,2,64,512]{3,2,1,0:T(8,128)(2,1)S(1)} collective-permute-done((bf16[2,2,64,512]{3,2,1,0:T(8,128)(2,1)S(1)}, bf16[2,2,64,512]{3,2,1,0:T(8,128)(2,1)S(1)}, u32[]{:S(2)}, u32[]{:S(2)}) %collective-permute-start.50) | collective-permute-done | bytes 262176 | tf_op jit(solution)/shard_map/ppermute | solution.py:1117
  499.3 6.1 %all-to-all-start.7 = ((bf16[4,2,128,640]{3,2,1,0:T(8,128)(2,1)}), bf16[4,2,128,640]{3,2,1,0:T(8,128)(2,1)}, u32[]{:S(2)}, u32[]{:S(2)}) async-start(bf16[4,2,128,640]{3,2,1,0:T(8,128)(2,1)} %copy.415), calls=%async_computation.7 | async-start | bytes 2621440 | tf_op jit(solution)/shard_map/all_to_all | solution.py:1113
  512.7 18.8 %collective-permute-done.60 = bf16[2,64,512]{2,1,0:T(8,128)(2,1)S(1)} collective-permute-done((bf16[2,64,512]{2,1,0:T(8,128)(2,1)S(1)}, bf16[2,64,512]{2,1,0:T(8,128)(2,1)S(1)}, u32[]{:S(2)}, u32[]{:S(2)}) %collective-permute-start.60) | collective-permute-done | bytes 131104 | tf_op jit(solution)/shard_map/ppermute | solution.py:1136
  535.2 3.3 copy.423
  (511 shorter events, 215.5 us)
Async XLA Ops:
  17.3 37.0 %all-to-all-start = ((bf16[4,2,128,640]{3,2,1,0:T(8,128)(2,1)}), bf16[4,2,128,640]{3,2,1,0:T(8,128)(2,1)}, u32[]{:S(2)}, u32[]{:S(2)}) async-start(bf16[4,2,128,640]{3,2,1,0:T(8,128)(2,1)} %copy.372), calls=%async_computation | async-start | bytes 2621440 | tf_op jit(solution)/shard_map/all_to_all | solution.py:1113
  56.3 39.1 %collective-permute-start.17 = (bf16[4,2,128,640]{3,2,1,0:T(8,128)(2,1)}, bf16[4,2,128,640]{3,2,1,0:T(8,128)(2,1)}, u32[]{:S(2)}, u32[]{:S(2)}) collective-permute-start(bf16[4,2,128,640]{3,2,1,0:T(8,128)(2,1)} %all-to-all-done.refs_2_), channel_id=1, source_target_pairs={{0,2},{1,3},{2,0},{3,1},{4,6},{5,7},{6,4},{7,5},{8,10},{9,11},{10,... | collective-permute-start | bytes 3932168 | tf_op jit(solution)/shard_map/ppermute | solution.py:1125
  57.8 35.5 %collective-permute-start.18 = (bf16[4,2,128,640]{3,2,1,0:T(8,128)(2,1)}, bf16[4,2,128,640]{3,2,1,0:T(8,128)(2,1)}, u32[]{:S(2)}, u32[]{:S(2)}) collective-permute-start(bf16[4,2,128,640]{3,2,1,0:T(8,128)(2,1)} %all-to-all-done.refs_2_), channel_id=1, source_target_pairs={{0,4},{4,0},{1,5},{5,1},{2,6},{6,2},{3,7},{7,3},{8,12},{12,8},{9,1... | collective-permute-start | bytes 3932168 | tf_op jit(solution)/shard_map/ppermute | solution.py:1117
  85.2 61.4 %all-to-all-start.1 = ((bf16[4,2,1056,128]{3,2,1,0:T(8,128)(2,1)}), bf16[4,2,1056,128]{3,2,1,0:T(8,128)(2,1)}, u32[]{:S(2)}, u32[]{:S(2)}) async-start(bf16[4,2,1056,128]{3,2,1,0:T(8,128)(2,1)} %pad_maximum_fusion), calls=%async_computation.1 | async-start | bytes 4325376 | tf_op jit(solution)/shard_map/all_to_all | solution.py:1113
  146.7 28.4 %all-to-all-start.2 = ((bf16[4,64,2048]{2,1,0:T(8,128)(2,1)}), bf16[4,64,2048]{2,1,0:T(8,128)(2,1)S(1)}, u32[]{:S(2)}, u32[]{:S(2)}) async-start(bf16[4,64,2048]{2,1,0:T(8,128)(2,1)} %bitcast.53), calls=%async_computation.2 | async-start | bytes 2097152 | tf_op jit(solution)/shard_map/all_to_all | solution.py:1113
  156.2 53.3 %collective-permute-start.36 = (bf16[4,2,1056,128]{3,2,1,0:T(8,128)(2,1)}, bf16[4,2,1056,128]{3,2,1,0:T(8,128)(2,1)}, u32[]{:S(2)}, u32[]{:S(2)}) collective-permute-start(bf16[4,2,1056,128]{3,2,1,0:T(8,128)(2,1)} %all-to-all-done.1.refs_5_.refs_0_), channel_id=1, source_target_pairs={{0,2},{1,3},{2,0},{3,1},{4,6},{5,7},{6,4},{7,5},{8,10},{9,11},{10,... | collective-permute-start | bytes 6488072 | tf_op jit(solution)/shard_map/ppermute | solution.py:1125
  157.0 49.0 %collective-permute-start.37 = (bf16[4,2,1056,128]{3,2,1,0:T(8,128)(2,1)}, bf16[4,2,1056,128]{3,2,1,0:T(8,128)(2,1)}, u32[]{:S(2)}, u32[]{:S(2)}) collective-permute-start(bf16[4,2,1056,128]{3,2,1,0:T(8,128)(2,1)} %all-to-all-done.1.refs_5_.refs_0_), channel_id=1, source_target_pairs={{0,4},{4,0},{1,5},{5,1},{2,6},{6,2},{3,7},{7,3},{8,12},{12,8},{9,1... | collective-permute-start | bytes 6488072 | tf_op jit(solution)/shard_map/ppermute | solution.py:1117
  175.6 37.7 %collective-permute-start.22 = (bf16[64,2048]{1,0:T(8,128)(2,1)S(1)}, bf16[64,2048]{1,0:T(8,128)(2,1)S(1)}, u32[]{:S(2)}, u32[]{:S(2)}) collective-permute-start(bf16[64,2048]{1,0:T(8,128)(2,1)S(1)} %multiply_convert_fusion), channel_id=1, source_target_pairs={{0,24},{8,16},{16,8},{24,0},{1,25},{9,17},{17,9},{25,1},{2,26},{10... | collective-permute-start | bytes 786440 | tf_op jit(solution)/shard_map/ppermute | solution.py:1129
  176.2 37.6 %collective-permute-start.23 = (bf16[64,2048]{1,0:T(8,128)(2,1)S(1)}, bf16[64,2048]{1,0:T(8,128)(2,1)S(1)}, u32[]{:S(2)}, u32[]{:S(2)}) collective-permute-start(bf16[64,2048]{1,0:T(8,128)(2,1)S(1)} %multiply_convert_fusion), channel_id=1, source_target_pairs={{0,16},{8,24},{16,0},{24,8},{1,17},{9,25},{17,1},{25,9},{2,18},{10... | collective-permute-start | bytes 786440 | tf_op jit(solution)/shard_map/ppermute | solution.py:1129
  180.4 36.7 %collective-permute-start.24 = (bf16[64,2048]{1,0:T(8,128)(2,1)S(1)}, bf16[64,2048]{1,0:T(8,128)(2,1)S(1)}, u32[]{:S(2)}, u32[]{:S(2)}) collective-permute-start(bf16[64,2048]{1,0:T(8,128)(2,1)S(1)} %multiply_convert_fusion), channel_id=1, source_target_pairs={{0,8},{8,0},{16,24},{24,16},{1,9},{9,1},{17,25},{25,17},{2,10},{10... | collective-permute-start | bytes 786440 | tf_op jit(solution)/shard_map/ppermute | solution.py:1129
  208.3 27.5 %collective-permute-start.38 = (bf16[2,2,1056,128]{3,2,1,0:T(8,128)(2,1)}, bf16[2,2,1056,128]{3,2,1,0:T(8,128)(2,1)}, u32[]{:S(2)}, u32[]{:S(2)}) collective-permute-start(bf16[2,2,1056,128]{3,2,1,0:T(8,128)(2,1)} %slice.465), channel_id=1, source_target_pairs={{0,2},{1,3},{2,0},{3,1},{4,6},{5,7},{6,4},{7,5},{8,10},{9,11},{10,... | collective-permute-start | bytes 3244040 | tf_op jit(solution)/shard_map/ppermute | solution.py:1125
  211.8 24.6 %collective-permute-start.39 = (bf16[2,2,1056,128]{3,2,1,0:T(8,128)(2,1)}, bf16[2,2,1056,128]{3,2,1,0:T(8,128)(2,1)}, u32[]{:S(2)}, u32[]{:S(2)}) collective-permute-start(bf16[2,2,1056,128]{3,2,1,0:T(8,128)(2,1)} %slice.466), channel_id=1, source_target_pairs={{0,4},{4,0},{1,5},{5,1},{2,6},{6,2},{3,7},{7,3},{8,12},{12,8},{9,1... | collective-permute-start | bytes 3244040 | tf_op jit(solution)/shard_map/ppermute | solution.py:1117
  262.1 32.5 %all-to-all-start.3 = ((bf16[4,64,2048]{2,1,0:T(8,128)(2,1)}), bf16[4,64,2048]{2,1,0:T(8,128)(2,1)}, u32[]{:S(2)}, u32[]{:S(2)}) async-start(bf16[4,64,2048]{2,1,0:T(8,128)(2,1)} %bitcast.491), calls=%async_computation.3 | async-start | bytes 2097152 | tf_op jit(solution)/shard_map/all_to_all | solution.py:1113
  289.8 49.8 %collective-permute-start.71 = (bf16[4,2,1056,128]{3,2,0,1:T(8,128)(2,1)}, bf16[4,2,1056,128]{3,2,0,1:T(8,128)(2,1)}, u32[]{:S(2)}, u32[]{:S(2)}) collective-permute-start(bf16[4,2,1056,128]{3,2,0,1:T(8,128)(2,1)} %pad_maximum_fusion.1), channel_id=1, source_target_pairs={{0,4},{4,0},{1,5},{5,1},{2,6},{6,2},{3,7},{7,3},{8,12},{12,8},{9,1... | collective-permute-start | bytes 6488072 | tf_op jit(solution)/shard_map/ppermute | solution.py:1117
  292.4 50.6 %collective-permute-start.73 = (bf16[4,2,1056,128]{3,2,0,1:T(8,128)(2,1)}, bf16[4,2,1056,128]{3,2,0,1:T(8,128)(2,1)}, u32[]{:S(2)}, u32[]{:S(2)}) collective-permute-start(bf16[4,2,1056,128]{3,2,0,1:T(8,128)(2,1)} %pad_maximum_fusion.2), channel_id=1, source_target_pairs={{0,2},{1,3},{2,0},{3,1},{4,6},{5,7},{6,4},{7,5},{8,10},{9,11},{10,... | collective-permute-start | bytes 6488072 | tf_op jit(solution)/shard_map/ppermute | solution.py:1125
  298.0 22.8 %collective-permute-start.43 = (bf16[64,2048]{1,0:T(8,128)(2,1)S(1)}, bf16[64,2048]{1,0:T(8,128)(2,1)S(1)}, u32[]{:S(2)}, u32[]{:S(2)}) collective-permute-start(bf16[64,2048]{1,0:T(8,128)(2,1)S(1)} %get-tuple-element.195), channel_id=1, source_target_pairs={{0,16},{8,24},{16,0},{24,8},{1,17},{9,25},{17,1},{25,9},{2,18},{10... | collective-permute-start | bytes 786440 | tf_op jit(solution)/shard_map/ppermute | solution.py:1129
  321.9 24.2 %collective-permute-start.45 = (bf16[256,2048]{1,0:T(8,128)(2,1)}, bf16[256,2048]{1,0:T(8,128)(2,1)}, u32[]{:S(2)}, u32[]{:S(2)}) collective-permute-start(bf16[256,2048]{1,0:T(8,128)(2,1)} %pad_maximum_fusion.12.refs_0_), channel_id=1, source_target_pairs={{0,1},{1,0},{2,3},{3,2},{4,5},{5,4},{6,7},{7,6},{8,9},{9,8},{10,11... | collective-permute-start | bytes 3145736 | tf_op jit(solution)/shard_map/ppermute | solution.py:1121
  321.9 66.4 %all-to-all-start.4 = ((bf16[4,64,2048]{2,1,0:T(8,128)(2,1)}), bf16[4,64,2048]{2,1,0:T(8,128)(2,1)}, u32[]{:S(2)}, u32[]{:S(2)}) async-start(bf16[4,64,2048]{2,1,0:T(8,128)(2,1)} %bitcast.490), calls=%async_computation.4 | async-start | bytes 2097152 | tf_op jit(solution)/shard_map/all_to_all | solution.py:1113
  342.2 38.4 %collective-permute-start.72 = (bf16[2,2,1056,128]{3,2,0,1:T(8,128)(2,1)}, bf16[2,2,1056,128]{3,2,0,1:T(8,128)(2,1)}, u32[]{:S(2)}, u32[]{:S(2)}) collective-permute-start(bf16[2,2,1056,128]{3,2,0,1:T(8,128)(2,1)} %add_convert_fusion.3), channel_id=1, source_target_pairs={{0,2},{1,3},{2,0},{3,1},{4,6},{5,7},{6,4},{7,5},{8,10},{9,11},{10,... | collective-permute-start | bytes 3244040 | tf_op jit(solution)/shard_map/ppermute | solution.py:1125
  345.5 35.0 %collective-permute-start.74 = (bf16[2,2,1056,128]{3,2,0,1:T(8,128)(2,1)}, bf16[2,2,1056,128]{3,2,0,1:T(8,128)(2,1)}, u32[]{:S(2)}, u32[]{:S(2)}) collective-permute-start(bf16[2,2,1056,128]{3,2,0,1:T(8,128)(2,1)} %add_convert_fusion.1), channel_id=1, source_target_pairs={{0,4},{4,0},{1,5},{5,1},{2,6},{6,2},{3,7},{7,3},{8,12},{12,8},{9,1... | collective-permute-start | bytes 3244040 | tf_op jit(solution)/shard_map/ppermute | solution.py:1117
  378.2 55.3 %collective-permute-start.66 = (bf16[4,2,128,640]{3,2,1,0:T(8,128)(2,1)}, bf16[4,2,128,640]{3,2,1,0:T(8,128)(2,1)}, u32[]{:S(2)}, u32[]{:S(2)}) collective-permute-start(bf16[4,2,128,640]{3,2,1,0:T(8,128)(2,1)} %pad_maximum_fusion.5), channel_id=1, source_target_pairs={{0,4},{4,0},{1,5},{5,1},{2,6},{6,2},{3,7},{7,3},{8,12},{12,8},{9,1... | collective-permute-start | bytes 3932168 | tf_op jit(solution)/shard_map/ppermute | solution.py:1117
  388.3 28.2 %all-to-all-start.5 = ((bf16[4,64,2048]{2,1,0:T(8,128)(2,1)}), bf16[4,64,2048]{2,1,0:T(8,128)(2,1)}, u32[]{:S(2)}, u32[]{:S(2)}) async-start(bf16[4,64,2048]{2,1,0:T(8,128)(2,1)} %bitcast.492), calls=%async_computation.5 | async-start | bytes 2097152 | tf_op jit(solution)/shard_map/all_to_all | solution.py:1113
  396.1 38.3 %collective-permute-start.67 = (bf16[4,2,128,640]{3,2,1,0:T(8,128)(2,1)}, bf16[4,2,128,640]{3,2,1,0:T(8,128)(2,1)}, u32[]{:S(2)}, u32[]{:S(2)}) collective-permute-start(bf16[4,2,128,640]{3,2,1,0:T(8,128)(2,1)} %pad_maximum_fusion.6), channel_id=1, source_target_pairs={{0,2},{1,3},{2,0},{3,1},{4,6},{5,7},{6,4},{7,5},{8,10},{9,11},{10,... | collective-permute-start | bytes 3932168 | tf_op jit(solution)/shard_map/ppermute | solution.py:1125
  416.4 80.0 %all-to-all-start.6 = ((bf16[4,2,1056,128]{3,2,1,0:T(8,128)(2,1)}), bf16[4,2,1056,128]{3,2,1,0:T(8,128)(2,1)}, u32[]{:S(2)}, u32[]{:S(2)}) async-start(bf16[4,2,1056,128]{3,2,1,0:T(8,128)(2,1)} %copy.413), calls=%async_computation.6 | async-start | bytes 4325376 | tf_op jit(solution)/shard_map/all_to_all | solution.py:1113
  433.5 25.7 %collective-permute-start.54 = (bf16[64,512]{1,0:T(8,128)(2,1)S(1)}, bf16[64,512]{1,0:T(8,128)(2,1)S(1)}, u32[]{:S(2)}, u32[]{:S(2)}) collective-permute-start(bf16[64,512]{1,0:T(8,128)(2,1)S(1)} %get-tuple-element.301), channel_id=1, source_target_pairs={{0,3},{1,2},{2,1},{3,0},{4,7},{5,6},{6,5},{7,4},{8,11},{9,10},{10,... | collective-permute-start | bytes 196616 | tf_op jit(solution)/shard_map/ppermute | solution.py:1136
  440.4 47.1 %collective-permute-start.68 = (bf16[2,2,128,640]{3,2,1,0:T(8,128)(2,1)S(1)}, bf16[2,2,128,640]{3,2,1,0:T(8,128)(2,1)S(1)}, u32[]{:S(2)}, u32[]{:S(2)}) collective-permute-start(bf16[2,2,128,640]{3,2,1,0:T(8,128)(2,1)S(1)} %add_convert_fusion.11), channel_id=1, source_target_pairs={{0,2},{1,3},{2,0},{3,1},{4,6},{5,7},{6,4},{7,5},{8,10},{9,11},{10,... | collective-permute-start | bytes 1966088 | tf_op jit(solution)/shard_map/ppermute | solution.py:1125
  458.6 30.6 %collective-permute-start.69 = (bf16[2,2,128,640]{3,2,1,0:T(8,128)(2,1)S(1)}, bf16[2,2,128,640]{3,2,1,0:T(8,128)(2,1)S(1)}, u32[]{:S(2)}, u32[]{:S(2)}) collective-permute-start(bf16[2,2,128,640]{3,2,1,0:T(8,128)(2,1)S(1)} %add_convert_fusion.9), channel_id=1, source_target_pairs={{0,4},{4,0},{1,5},{5,1},{2,6},{6,2},{3,7},{7,3},{8,12},{12,8},{9,1... | collective-permute-start | bytes 1966088 | tf_op jit(solution)/shard_map/ppermute | solution.py:1117
  482.8 26.4 %collective-permute-start.51 = (bf16[2,64,512]{2,1,0:T(8,128)(2,1)}, bf16[2,64,512]{2,1,0:T(8,128)(2,1)}, u32[]{:S(2)}, u32[]{:S(2)}) collective-permute-start(bf16[2,64,512]{2,1,0:T(8,128)(2,1)} %get-tuple-element.269), channel_id=1, source_target_pairs={{0,24},{8,16},{16,8},{24,0},{1,25},{9,17},{17,9},{25,1},{2,26},{10... | collective-permute-start | bytes 393224 | tf_op jit(solution)/shard_map/ppermute | solution.py:1136
  486.3 24.4 %collective-permute-start.52 = (bf16[2,64,512]{2,1,0:T(8,128)(2,1)}, bf16[2,64,512]{2,1,0:T(8,128)(2,1)}, u32[]{:S(2)}, u32[]{:S(2)}) collective-permute-start(bf16[2,64,512]{2,1,0:T(8,128)(2,1)} %get-tuple-element.189), channel_id=1, source_target_pairs={{0,16},{8,24},{16,0},{24,8},{1,17},{9,25},{17,1},{25,9},{2,18},{10... | collective-permute-start | bytes 393224 | tf_op jit(solution)/shard_map/ppermute | solution.py:1136
  487.5 23.1 %collective-permute-start.53 = (bf16[2,64,512]{2,1,0:T(8,128)(2,1)}, bf16[2,64,512]{2,1,0:T(8,128)(2,1)}, u32[]{:S(2)}, u32[]{:S(2)}) collective-permute-start(bf16[2,64,512]{2,1,0:T(8,128)(2,1)} %get-tuple-element.268), channel_id=1, source_target_pairs={{0,8},{8,0},{16,24},{24,16},{1,9},{9,1},{17,25},{25,17},{2,10},{10... | collective-permute-start | bytes 393224 | tf_op jit(solution)/shard_map/ppermute | solution.py:1136
  489.2 23.4 %collective-permute-start.58 = (bf16[2,64,512]{2,1,0:T(8,128)(2,1)}, bf16[2,64,512]{2,1,0:T(8,128)(2,1)}, u32[]{:S(2)}, u32[]{:S(2)}) collective-permute-start(bf16[2,64,512]{2,1,0:T(8,128)(2,1)} %get-tuple-element.262), channel_id=1, source_target_pairs={{0,24},{8,16},{16,8},{24,0},{1,25},{9,17},{17,9},{25,1},{2,26},{10... | collective-permute-start | bytes 393224 | tf_op jit(solution)/shard_map/ppermute | solution.py:1136
  499.3 41.5 %all-to-all-start.7 = ((bf16[4,2,128,640]{3,2,1,0:T(8,128)(2,1)}), bf16[4,2,128,640]{3,2,1,0:T(8,128)(2,1)}, u32[]{:S(2)}, u32[]{:S(2)}) async-start(bf16[4,2,128,640]{3,2,1,0:T(8,128)(2,1)} %copy.415), calls=%async_computation.7 | async-start | bytes 2621440 | tf_op jit(solution)/shard_map/all_to_all | solution.py:1113
  (118 other events, 1103.9 us)

commit v4 on v3

--- a/solution.py
+++ b/solution.py
@@ -1438,8 +1438,9 @@
     ffn_total = scatter_end(ffn_grads, ffn_sent, ffn_back)
     mix_sent = scatter_send(mix_grads)
     mix_sent = after((swap_mp(mix_sent[0]), swap_across(mix_sent[1])), mixer_grad)
-    mix_total = scatter_end(mix_grads, mix_sent, scatter_turn(mix_grads, mix_sent))
-    out_low = (middle + after(down_sum, mixer_grad)).astype(LOW)
+    mix_back = scatter_turn(mix_grads, mix_sent)
+    mix_total = scatter_end(mix_grads, mix_sent, mix_back)
+    out_low = (middle + after(down_sum, mix_back)).astype(LOW)
 
     def placed(total, earlier=None):
         return along_column(at_core, (total[:, 0], total[:, 1]), earlier).transpose(1, 0, 2, 3)
@@ -1480,6 +1481,7 @@
             jnp.sum(head_grad, 0),
         ]
     )
+    vector = after(vector, mix_back)
     vector = vector + swap_mp(vector)
     vector = vector + swap_across(vector)
     vectors = jnp.stack(turn(at_core, (vector, swap_core(vector))))

time: 554 us -> 548 us (0.989)
  local copies, waits for them, and re-layouts: 71.9 us -> 63.4 us
  waiting for transfers between devices: 210 us -> 216 us
    ppermute x10, waiting for transfers between devices: 30 us -> 17.7 us  [swap_across(): return lax.ppermute(values, 'dmod', ACROSS)]
    ppermute x24, waiting for transfers between devices: 21.4 us -> 30.1 us  [trade_blocks(): lax.ppermute(blocks[k], axis, [(i, i ^ k) for i in range(size)])]
    unnamed x144 -> x138, local copies, waits for them, and re-layouts: 27.7 us -> 19.5 us
  transfers between devices with their start and end apart: 84 -> 84, of which waited for: 33 -> 36; matrix products, arithmetic and copies ran while one was open for 19% -> 19% of each run, Pallas kernels for 10% -> 10%
where the time goes in v4:
time: 548 us; the launch traced here: 540 us
  waiting for transfers between devices  216 us (39%)
  starting transfers between devices  126 us (23%)
  Pallas kernels  71.9 us (13%)
  local copies, waits for them, and re-layouts  63.4 us (12%)
  other arithmetic  58.4 us (11%)
    pallas_call x5, Pallas kernels, call(): pl.pallas_call(kernel, grid=(grid,), in_specs=in_specs, out_specs=out_spe...  71.9 us
    ppermute x16, waiting for transfers between devices, swap_dp(): lax.ppermute(values, 'dp', [(i, i ^ k) for i in range(lax.axis_size('dp'))])  68.2 us
    all_to_all x8, starting transfers between devices, exchange(): return lax.all_to_all(values, axis, 0, 0, tiled=True)  56.2 us
    ppermute x12, waiting for transfers between devices, swap_mp(): return lax.ppermute(values, 'mp', SWAP)  48.7 us
    all_to_all x8, waiting for transfers between devices, exchange(): return lax.all_to_all(values, axis, 0, 0, tiled=True)  42.1 us
    ppermute x24, waiting for transfers between devices, trade_blocks(): lax.ppermute(blocks[k], axis, [(i, i ^ k) for i in range(size)])  30.1 us
    ppermute x24, starting transfers between devices, trade_blocks(): lax.ppermute(blocks[k], axis, [(i, i ^ k) for i in range(size)])  23.4 us
    ppermute x16, starting transfers between devices, swap_dp(): lax.ppermute(values, 'dp', [(i, i ^ k) for i in range(lax.axis_size('dp'))])  20.7 us
  transfers between devices with their start and end apart: 84, of which 36 were waited for; matrix products, arithmetic and copies ran while one was open for 19% of the time, Pallas kernels for 10%

profile of v4, /device:TPU:16, one launch (start us, length us, event | category | flops | bytes accessed | tf_op | source)
XLA Modules:
  0.0 540.2 jit_solution(7540094636219511835)
XLA Ops:
  17.3 7.1 %all-to-all-start = ((bf16[4,2,128,640]{3,2,1,0:T(8,128)(2,1)}), bf16[4,2,128,640]{3,2,1,0:T(8,128)(2,1)}, u32[]{:S(2)}, u32[]{:S(2)}) async-start(bf16[4,2,128,640]{3,2,1,0:T(8,128)(2,1)} %copy.372), calls=%async_computation | async-start | bytes 2621440 | tf_op jit(solution)/shard_map/all_to_all | solution.py:1113
  61.4 4.3 collective-permute-start.14
  67.1 14.4 %collective-permute-done.13 = bf16[64,2048]{1,0:T(8,128)(2,1)S(1)} collective-permute-done((bf16[64,2048]{1,0:T(8,128)(2,1)S(1)}, bf16[64,2048]{1,0:T(8,128)(2,1)S(1)}, u32[]{:S(2)}, u32[]{:S(2)}) %collective-permute-start.13) | collective-permute-done | bytes 262176 | tf_op jit(solution)/shard_map/ppermute | solution.py:1129
  85.3 8.1 %all-to-all-start.1 = ((bf16[4,2,1056,128]{3,2,1,0:T(8,128)(2,1)}), bf16[4,2,1056,128]{3,2,1,0:T(8,128)(2,1)}, u32[]{:S(2)}, u32[]{:S(2)}) async-start(bf16[4,2,1056,128]{3,2,1,0:T(8,128)(2,1)} %pad_maximum_fusion), calls=%async_computation.1 | async-start | bytes 4325376 | tf_op jit(solution)/shard_map/all_to_all | solution.py:1113
  98.2 12.8 %collective-permute-done.19.refs_5_ = bf16[2,2,128,640]{3,2,1,0:T(8,128)(2,1)S(1)} collective-permute-done((bf16[2,2,128,640]{3,2,1,0:T(8,128)(2,1)S(1)}, bf16[2,2,128,640]{3,2,1,0:T(8,128)(2,1)S(1)}, u32[]{:S(2)}, u32[]{:S(2)}) %collective-permute-start.19) | collective-permute-done | bytes 655392 | tf_op jit(solution)/shard_map/ppermute | solution.py:1125
  112.7 17.5 %column_forward.1 = (bf16[512,256]{1,0:T(8,128)(2,1)S(1)}, f32[2,2,256,256]{3,2,1,0:T(8,128)S(1)}, f32[512,256]{1,0:T(8,128)S(1)}, f32[512,256]{1,0:T(8,128)S(1)...) custom-call(bf16[256,2048]{1,0:T(8,128)(2,1)} %copy-done.44, ...), custom_call_target="tpu_custom_call" | custom-call | flops 10000000000 | bytes 8388608 | tf_op jit(solution)/shard_map/column_forward/pallas_call | solution.py:419
  134.3 3.3 collective-permute-start.28
  138.9 7.8 %all-to-all-done.1.refs_5_.refs_0_ = bf16[4,2,1056,128]{3,2,1,0:T(8,128)(2,1)} async-done(((bf16[4,2,1056,128]{3,2,1,0:T(8,128)(2,1)}), bf16[4,2,1056,128]{3,2,1,0:T(8,128)(2,1)}, u32[]{:S(2)}, u32[]{:S(2)}) %all-to-all-start.1) | async-done | bytes 2162720 | tf_op jit(solution)/shard_map/all_to_all | solution.py:1113
  146.7 7.4 %all-to-all-start.2 = ((bf16[4,64,2048]{2,1,0:T(8,128)(2,1)}), bf16[4,64,2048]{2,1,0:T(8,128)(2,1)S(1)}, u32[]{:S(2)}, u32[]{:S(2)}) async-start(bf16[4,64,2048]{2,1,0:T(8,128)(2,1)} %bitcast.53), calls=%async_computation.2 | async-start | bytes 2097152 | tf_op jit(solution)/shard_map/all_to_all | solution.py:1113
  160.0 15.1 %all-to-all-done.2 = bf16[4,64,2048]{2,1,0:T(8,128)(2,1)S(1)} async-done(((bf16[4,64,2048]{2,1,0:T(8,128)(2,1)}), bf16[4,64,2048]{2,1,0:T(8,128)(2,1)S(1)}, u32[]{:S(2)}, u32[]{:S(2)}) %all-to-all-start.2) | async-done | bytes 1048608 | tf_op jit(solution)/shard_map/all_to_all | solution.py:1113
  176.3 4.2 collective-permute-start.23
  181.2 24.8 %collective-permute-done.37.refs_7_.refs_2_ = bf16[4,2,1056,128]{3,2,1,0:T(8,128)(2,1)} collective-permute-done((bf16[4,2,1056,128]{3,2,1,0:T(8,128)(2,1)}, bf16[4,2,1056,128]{3,2,1,0:T(8,128)(2,1)}, u32[]{:S(2)}, u32[]{:S(2)}) %collective-permute-start.37) | collective-permute-done | bytes 2162720 | tf_op jit(solution)/shard_map/ppermute | solution.py:1117
  217.5 15.6 %collective-permute-done.32 = bf16[64,2048]{1,0:T(8,128)(2,1)S(1)} collective-permute-done((bf16[64,2048]{1,0:T(8,128)(2,1)S(1)}, bf16[64,2048]{1,0:T(8,128)(2,1)S(1)}, u32[]{:S(2)}, u32[]{:S(2)}) %collective-permute-start.32) | collective-permute-done | bytes 262176 | tf_op jit(solution)/shard_map/ppermute | solution.py:1129
  237.8 17.4 %column_ffn.1 = (bf16[256,2048]{1,0:T(8,128)(2,1)S(1)}, bf16[256,2048]{1,0:T(8,128)(2,1)}, bf16[512,2048]{1,0:T(8,128)(2,1)}, bf16[512,2048]{1,0:T(8,128)(2,1)},...) custom-call(bf16[256,2048]{1,0:T(8,128)(2,1)S(1)} %pad_maximum_fusion.10.refs_0_, ...), custom_call_target="tpu_custom_call" | custom-call | flops 10000000000 | bytes 8388608 | tf_op jit(solution)/shard_map/column_ffn/pallas_call | solution.py:419
  262.2 7.9 %all-to-all-start.3 = ((bf16[4,64,2048]{2,1,0:T(8,128)(2,1)}), bf16[4,64,2048]{2,1,0:T(8,128)(2,1)}, u32[]{:S(2)}, u32[]{:S(2)}) async-start(bf16[4,64,2048]{2,1,0:T(8,128)(2,1)} %bitcast.491), calls=%async_computation.3 | async-start | bytes 2097152 | tf_op jit(solution)/shard_map/all_to_all | solution.py:1113
  271.2 13.6 %column_ffn_grads.1 = (bf16[256,2048]{1,0:T(8,128)(2,1)S(1)}, bf16[256,2048]{1,0:T(8,128)(2,1)S(1)}, bf16[4,2,1056,128]{3,2,1,0:T(8,128)(2,1)}, bf16[4,2,1056,12...) custom-call(bf16[512,704]{1,0:T(8,128)(2,1)S(1)} %copy-done.11, ...), custom_call_target="tpu_custom_call" | custom-call | flops 10000000000 | bytes 8388608 | tf_op jit(solution)/shard_map/column_ffn_grads/pallas_call | solution.py:419
  298.2 3.3 collective-permute-start.43
  301.4 16.8 %collective-permute-done.42 = bf16[64,2048]{1,0:T(8,128)(2,1)S(1)} collective-permute-done((bf16[64,2048]{1,0:T(8,128)(2,1)}, bf16[64,2048]{1,0:T(8,128)(2,1)S(1)}, u32[]{:S(2)}, u32[]{:S(2)}) %collective-permute-start.42) | collective-permute-done | bytes 262176 | tf_op jit(solution)/shard_map/ppermute | solution.py:1129
  323.4 7.7 %all-to-all-start.4 = ((bf16[4,64,2048]{2,1,0:T(8,128)(2,1)}), bf16[4,64,2048]{2,1,0:T(8,128)(2,1)}, u32[]{:S(2)}, u32[]{:S(2)}) async-start(bf16[4,64,2048]{2,1,0:T(8,128)(2,1)} %bitcast.490), calls=%async_computation.4 | async-start | bytes 2097152 | tf_op jit(solution)/shard_map/all_to_all | solution.py:1113
  331.2 8.4 %collective-permute-done.71 = bf16[4,2,1056,128]{3,2,0,1:T(8,128)(2,1)} collective-permute-done((bf16[4,2,1056,128]{3,2,0,1:T(8,128)(2,1)}, bf16[4,2,1056,128]{3,2,0,1:T(8,128)(2,1)}, u32[]{:S(2)}, u32[]{:S(2)}) %collective-permute-start.71) | collective-permute-done | bytes 2162720 | tf_op jit(solution)/shard_map/ppermute | solution.py:1117
  346.1 16.9 %column_backward.1 = (bf16[512,1024]{1,0:T(8,128)(2,1)S(1)}, f32[512,2]{1,0:T(8,128)S(1)}, f32[2,12,256]{2,1,0:T(8,128)S(1)}, f32[2,1,128]{2,1,0:T(1,128)S(1)}, ...) custom-call(bf16[256,2048]{1,0:T(8,128)(2,1)} %pad_maximum_fusion.12.refs_0_, ...), custom_call_target="tpu_custom_call" | custom-call | flops 10000000000 | bytes 8388608 | tf_op jit(solution)/shard_map/column_backward/pallas_call | solution.py:419
  363.0 6.6 %column_mixer_grads.1 = (bf16[4,2,128,640]{3,2,1,0:T(8,128)(2,1)S(1)}, bf16[4,2,128,640]{3,2,1,0:T(8,128)(2,1)S(1)}, bf16[4,2,128,640]{3,2,1,0:T(8,128)(2,1)S(1)}, bf16[4,2,128,640]{3,2,1,0:T(8,128)(2,1)}) custom-call(bf16[512,2048]{1,0:T(8,128)(2,1)} %get-tuple-element.87.mixer_ref, bf16[512,1024]{1,0:T(8,128)(2,1)S(1)} %get-tuple-element.94.signal_ref, ...), custom_call_target="tpu_custom_call" | custom-call | flops 10000000000 | bytes 8388608 | tf_op jit(solution)/shard_map/column_mixer_grads/pallas_call | solution.py:419
  386.7 5.4 all-to-all-start.5
  397.4 17.5 %all-to-all-done.5 = bf16[4,64,2048]{2,1,0:T(8,128)(2,1)} async-done(((bf16[4,64,2048]{2,1,0:T(8,128)(2,1)}), bf16[4,64,2048]{2,1,0:T(8,128)(2,1)}, u32[]{:S(2)}, u32[]{:S(2)}) %all-to-all-start.5) | async-done | bytes 1048608 | tf_op jit(solution)/shard_map/all_to_all | solution.py:1113
  414.8 7.8 %all-to-all-start.6 = ((bf16[4,2,1056,128]{3,2,1,0:T(8,128)(2,1)}), bf16[4,2,1056,128]{3,2,1,0:T(8,128)(2,1)}, u32[]{:S(2)}, u32[]{:S(2)}) async-start(bf16[4,2,1056,128]{3,2,1,0:T(8,128)(2,1)} %copy.413), calls=%async_computation.6 | async-start | bytes 4325376 | tf_op jit(solution)/shard_map/all_to_all | solution.py:1113
  434.4 3.5 collective-permute-done.63
  438.0 7.6 %collective-permute-done.49 = bf16[64,512]{1,0:T(8,128)(2,1)S(1)} collective-permute-done((bf16[64,512]{1,0:T(8,128)(2,1)}, bf16[64,512]{1,0:T(8,128)(2,1)S(1)}, u32[]{:S(2)}, u32[]{:S(2)}) %collective-permute-start.49) | collective-permute-done | bytes 65568 | tf_op jit(solution)/shard_map/ppermute | solution.py:1136
  457.6 12.2 %collective-permute-done.66 = f32[1,2,89,128]{3,2,1,0:T(8,128)S(1)} collective-permute-done((f32[1,2,89,128]{3,2,1,0:T(8,128)S(1)}, f32[1,2,89,128]{3,2,1,0:T(8,128)S(1)}, u32[]{:S(2)}, u32[]{:S(2)}) %collective-permute-start.66) | collective-permute-done | bytes 91168 | tf_op jit(solution)/shard_map/ppermute | solution.py:1129
  469.9 5.4 %collective-permute-done.52 = bf16[2,2,64,512]{3,2,1,0:T(8,128)(2,1)S(1)} collective-permute-done((bf16[2,2,64,512]{3,2,1,0:T(8,128)(2,1)S(1)}, bf16[2,2,64,512]{3,2,1,0:T(8,128)(2,1)S(1)}, u32[]{:S(2)}, u32[]{:S(2)}) %collective-permute-start.52) | collective-permute-done | bytes 262176 | tf_op jit(solution)/shard_map/ppermute | solution.py:1117
  494.3 4.8 all-to-all-start.7
  508.8 16.3 %collective-permute-done.62 = bf16[2,64,512]{2,1,0:T(8,128)(2,1)S(1)} collective-permute-done((bf16[2,64,512]{2,1,0:T(8,128)(2,1)S(1)}, bf16[2,64,512]{2,1,0:T(8,128)(2,1)S(1)}, u32[]{:S(2)}, u32[]{:S(2)}) %collective-permute-start.62) | collective-permute-done | bytes 131104 | tf_op jit(solution)/shard_map/ppermute | solution.py:1136
  528.9 3.3 copy.423
  (505 shorter events, 212.8 us)
Async XLA Ops:
  17.3 37.0 %all-to-all-start = ((bf16[4,2,128,640]{3,2,1,0:T(8,128)(2,1)}), bf16[4,2,128,640]{3,2,1,0:T(8,128)(2,1)}, u32[]{:S(2)}, u32[]{:S(2)}) async-start(bf16[4,2,128,640]{3,2,1,0:T(8,128)(2,1)} %copy.372), calls=%async_computation | async-start | bytes 2621440 | tf_op jit(solution)/shard_map/all_to_all | solution.py:1113
  56.3 39.1 %collective-permute-start.17 = (bf16[4,2,128,640]{3,2,1,0:T(8,128)(2,1)}, bf16[4,2,128,640]{3,2,1,0:T(8,128)(2,1)}, u32[]{:S(2)}, u32[]{:S(2)}) collective-permute-start(bf16[4,2,128,640]{3,2,1,0:T(8,128)(2,1)} %all-to-all-done.refs_2_), channel_id=1, source_target_pairs={{0,2},{1,3},{2,0},{3,1},{4,6},{5,7},{6,4},{7,5},{8,10},{9,11},{10,... | collective-permute-start | bytes 3932168 | tf_op jit(solution)/shard_map/ppermute | solution.py:1125
  57.8 35.6 %collective-permute-start.18 = (bf16[4,2,128,640]{3,2,1,0:T(8,128)(2,1)}, bf16[4,2,128,640]{3,2,1,0:T(8,128)(2,1)}, u32[]{:S(2)}, u32[]{:S(2)}) collective-permute-start(bf16[4,2,128,640]{3,2,1,0:T(8,128)(2,1)} %all-to-all-done.refs_2_), channel_id=1, source_target_pairs={{0,4},{4,0},{1,5},{5,1},{2,6},{6,2},{3,7},{7,3},{8,12},{12,8},{9,1... | collective-permute-start | bytes 3932168 | tf_op jit(solution)/shard_map/ppermute | solution.py:1117
  85.3 61.4 %all-to-all-start.1 = ((bf16[4,2,1056,128]{3,2,1,0:T(8,128)(2,1)}), bf16[4,2,1056,128]{3,2,1,0:T(8,128)(2,1)}, u32[]{:S(2)}, u32[]{:S(2)}) async-start(bf16[4,2,1056,128]{3,2,1,0:T(8,128)(2,1)} %pad_maximum_fusion), calls=%async_computation.1 | async-start | bytes 4325376 | tf_op jit(solution)/shard_map/all_to_all | solution.py:1113
  146.7 28.4 %all-to-all-start.2 = ((bf16[4,64,2048]{2,1,0:T(8,128)(2,1)}), bf16[4,64,2048]{2,1,0:T(8,128)(2,1)S(1)}, u32[]{:S(2)}, u32[]{:S(2)}) async-start(bf16[4,64,2048]{2,1,0:T(8,128)(2,1)} %bitcast.53), calls=%async_computation.2 | async-start | bytes 2097152 | tf_op jit(solution)/shard_map/all_to_all | solution.py:1113
  156.3 53.3 %collective-permute-start.36 = (bf16[4,2,1056,128]{3,2,1,0:T(8,128)(2,1)}, bf16[4,2,1056,128]{3,2,1,0:T(8,128)(2,1)}, u32[]{:S(2)}, u32[]{:S(2)}) collective-permute-start(bf16[4,2,1056,128]{3,2,1,0:T(8,128)(2,1)} %all-to-all-done.1.refs_5_.refs_0_), channel_id=1, source_target_pairs={{0,2},{1,3},{2,0},{3,1},{4,6},{5,7},{6,4},{7,5},{8,10},{9,11},{10,... | collective-permute-start | bytes 6488072 | tf_op jit(solution)/shard_map/ppermute | solution.py:1125
  157.1 49.0 %collective-permute-start.37 = (bf16[4,2,1056,128]{3,2,1,0:T(8,128)(2,1)}, bf16[4,2,1056,128]{3,2,1,0:T(8,128)(2,1)}, u32[]{:S(2)}, u32[]{:S(2)}) collective-permute-start(bf16[4,2,1056,128]{3,2,1,0:T(8,128)(2,1)} %all-to-all-done.1.refs_5_.refs_0_), channel_id=1, source_target_pairs={{0,4},{4,0},{1,5},{5,1},{2,6},{6,2},{3,7},{7,3},{8,12},{12,8},{9,1... | collective-permute-start | bytes 6488072 | tf_op jit(solution)/shard_map/ppermute | solution.py:1117
  175.7 37.7 %collective-permute-start.22 = (bf16[64,2048]{1,0:T(8,128)(2,1)S(1)}, bf16[64,2048]{1,0:T(8,128)(2,1)S(1)}, u32[]{:S(2)}, u32[]{:S(2)}) collective-permute-start(bf16[64,2048]{1,0:T(8,128)(2,1)S(1)} %multiply_convert_fusion), channel_id=1, source_target_pairs={{0,24},{8,16},{16,8},{24,0},{1,25},{9,17},{17,9},{25,1},{2,26},{10... | collective-permute-start | bytes 786440 | tf_op jit(solution)/shard_map/ppermute | solution.py:1129
  176.3 37.6 %collective-permute-start.23 = (bf16[64,2048]{1,0:T(8,128)(2,1)S(1)}, bf16[64,2048]{1,0:T(8,128)(2,1)S(1)}, u32[]{:S(2)}, u32[]{:S(2)}) collective-permute-start(bf16[64,2048]{1,0:T(8,128)(2,1)S(1)} %multiply_convert_fusion), channel_id=1, source_target_pairs={{0,16},{8,24},{16,0},{24,8},{1,17},{9,25},{17,1},{25,9},{2,18},{10... | collective-permute-start | bytes 786440 | tf_op jit(solution)/shard_map/ppermute | solution.py:1129
  180.5 36.7 %collective-permute-start.24 = (bf16[64,2048]{1,0:T(8,128)(2,1)S(1)}, bf16[64,2048]{1,0:T(8,128)(2,1)S(1)}, u32[]{:S(2)}, u32[]{:S(2)}) collective-permute-start(bf16[64,2048]{1,0:T(8,128)(2,1)S(1)} %multiply_convert_fusion), channel_id=1, source_target_pairs={{0,8},{8,0},{16,24},{24,16},{1,9},{9,1},{17,25},{25,17},{2,10},{10... | collective-permute-start | bytes 786440 | tf_op jit(solution)/shard_map/ppermute | solution.py:1129
  208.3 27.5 %collective-permute-start.38 = (bf16[2,2,1056,128]{3,2,1,0:T(8,128)(2,1)}, bf16[2,2,1056,128]{3,2,1,0:T(8,128)(2,1)}, u32[]{:S(2)}, u32[]{:S(2)}) collective-permute-start(bf16[2,2,1056,128]{3,2,1,0:T(8,128)(2,1)} %slice.465), channel_id=1, source_target_pairs={{0,2},{1,3},{2,0},{3,1},{4,6},{5,7},{6,4},{7,5},{8,10},{9,11},{10,... | collective-permute-start | bytes 3244040 | tf_op jit(solution)/shard_map/ppermute | solution.py:1125
  211.8 24.6 %collective-permute-start.39 = (bf16[2,2,1056,128]{3,2,1,0:T(8,128)(2,1)}, bf16[2,2,1056,128]{3,2,1,0:T(8,128)(2,1)}, u32[]{:S(2)}, u32[]{:S(2)}) collective-permute-start(bf16[2,2,1056,128]{3,2,1,0:T(8,128)(2,1)} %slice.466), channel_id=1, source_target_pairs={{0,4},{4,0},{1,5},{5,1},{2,6},{6,2},{3,7},{7,3},{8,12},{12,8},{9,1... | collective-permute-start | bytes 3244040 | tf_op jit(solution)/shard_map/ppermute | solution.py:1117
  262.2 32.6 %all-to-all-start.3 = ((bf16[4,64,2048]{2,1,0:T(8,128)(2,1)}), bf16[4,64,2048]{2,1,0:T(8,128)(2,1)}, u32[]{:S(2)}, u32[]{:S(2)}) async-start(bf16[4,64,2048]{2,1,0:T(8,128)(2,1)} %bitcast.491), calls=%async_computation.3 | async-start | bytes 2097152 | tf_op jit(solution)/shard_map/all_to_all | solution.py:1113
  289.9 49.8 %collective-permute-start.71 = (bf16[4,2,1056,128]{3,2,0,1:T(8,128)(2,1)}, bf16[4,2,1056,128]{3,2,0,1:T(8,128)(2,1)}, u32[]{:S(2)}, u32[]{:S(2)}) collective-permute-start(bf16[4,2,1056,128]{3,2,0,1:T(8,128)(2,1)} %pad_maximum_fusion.1), channel_id=1, source_target_pairs={{0,4},{4,0},{1,5},{5,1},{2,6},{6,2},{3,7},{7,3},{8,12},{12,8},{9,1... | collective-permute-start | bytes 6488072 | tf_op jit(solution)/shard_map/ppermute | solution.py:1117
  292.6 50.5 %collective-permute-start.73 = (bf16[4,2,1056,128]{3,2,0,1:T(8,128)(2,1)}, bf16[4,2,1056,128]{3,2,0,1:T(8,128)(2,1)}, u32[]{:S(2)}, u32[]{:S(2)}) collective-permute-start(bf16[4,2,1056,128]{3,2,0,1:T(8,128)(2,1)} %pad_maximum_fusion.2), channel_id=1, source_target_pairs={{0,2},{1,3},{2,0},{3,1},{4,6},{5,7},{6,4},{7,5},{8,10},{9,11},{10,... | collective-permute-start | bytes 6488072 | tf_op jit(solution)/shard_map/ppermute | solution.py:1125
  298.2 23.1 %collective-permute-start.43 = (bf16[64,2048]{1,0:T(8,128)(2,1)}, bf16[64,2048]{1,0:T(8,128)(2,1)S(1)}, u32[]{:S(2)}, u32[]{:S(2)}) collective-permute-start(bf16[64,2048]{1,0:T(8,128)(2,1)} %get-tuple-element.197), channel_id=1, source_target_pairs={{0,16},{8,24},{16,0},{24,8},{1,17},{9,25},{17,1},{25,9},{2,18},{10... | collective-permute-start | bytes 786440 | tf_op jit(solution)/shard_map/ppermute | solution.py:1129
  323.4 63.3 %all-to-all-start.4 = ((bf16[4,64,2048]{2,1,0:T(8,128)(2,1)}), bf16[4,64,2048]{2,1,0:T(8,128)(2,1)}, u32[]{:S(2)}, u32[]{:S(2)}) async-start(bf16[4,64,2048]{2,1,0:T(8,128)(2,1)} %bitcast.490), calls=%async_computation.4 | async-start | bytes 2097152 | tf_op jit(solution)/shard_map/all_to_all | solution.py:1113
  342.2 36.8 %collective-permute-start.72 = (bf16[2,2,1056,128]{3,2,0,1:T(8,128)(2,1)}, bf16[2,2,1056,128]{3,2,0,1:T(8,128)(2,1)}, u32[]{:S(2)}, u32[]{:S(2)}) collective-permute-start(bf16[2,2,1056,128]{3,2,0,1:T(8,128)(2,1)} %add_convert_fusion.3), channel_id=1, source_target_pairs={{0,2},{1,3},{2,0},{3,1},{4,6},{5,7},{6,4},{7,5},{8,10},{9,11},{10,... | collective-permute-start | bytes 3244040 | tf_op jit(solution)/shard_map/ppermute | solution.py:1125
  345.6 33.4 %collective-permute-start.74 = (bf16[2,2,1056,128]{3,2,0,1:T(8,128)(2,1)}, bf16[2,2,1056,128]{3,2,0,1:T(8,128)(2,1)}, u32[]{:S(2)}, u32[]{:S(2)}) collective-permute-start(bf16[2,2,1056,128]{3,2,0,1:T(8,128)(2,1)} %add_convert_fusion.1), channel_id=1, source_target_pairs={{0,4},{4,0},{1,5},{5,1},{2,6},{6,2},{3,7},{7,3},{8,12},{12,8},{9,1... | collective-permute-start | bytes 3244040 | tf_op jit(solution)/shard_map/ppermute | solution.py:1117
  372.8 51.7 %collective-permute-start.46 = (bf16[4,2,128,640]{3,2,1,0:T(8,128)(2,1)}, bf16[4,2,128,640]{3,2,1,0:T(8,128)(2,1)}, u32[]{:S(2)}, u32[]{:S(2)}) collective-permute-start(bf16[4,2,128,640]{3,2,1,0:T(8,128)(2,1)} %pad_maximum_fusion.5), channel_id=1, source_target_pairs={{0,4},{4,0},{1,5},{5,1},{2,6},{6,2},{3,7},{7,3},{8,12},{12,8},{9,1... | collective-permute-start | bytes 3932168 | tf_op jit(solution)/shard_map/ppermute | solution.py:1117
  375.5 48.9 %collective-permute-start.47 = (bf16[4,2,128,640]{3,2,1,0:T(8,128)(2,1)}, bf16[4,2,128,640]{3,2,1,0:T(8,128)(2,1)}, u32[]{:S(2)}, u32[]{:S(2)}) collective-permute-start(bf16[4,2,128,640]{3,2,1,0:T(8,128)(2,1)} %pad_maximum_fusion.6), channel_id=1, source_target_pairs={{0,2},{1,3},{2,0},{3,1},{4,6},{5,7},{6,4},{7,5},{8,10},{9,11},{10,... | collective-permute-start | bytes 3932168 | tf_op jit(solution)/shard_map/ppermute | solution.py:1125
  386.7 28.1 %all-to-all-start.5 = ((bf16[4,64,2048]{2,1,0:T(8,128)(2,1)}), bf16[4,64,2048]{2,1,0:T(8,128)(2,1)}, u32[]{:S(2)}, u32[]{:S(2)}) async-start(bf16[4,64,2048]{2,1,0:T(8,128)(2,1)} %bitcast.492), calls=%async_computation.5 | async-start | bytes 2097152 | tf_op jit(solution)/shard_map/all_to_all | solution.py:1113
  414.8 76.5 %all-to-all-start.6 = ((bf16[4,2,1056,128]{3,2,1,0:T(8,128)(2,1)}), bf16[4,2,1056,128]{3,2,1,0:T(8,128)(2,1)}, u32[]{:S(2)}, u32[]{:S(2)}) async-start(bf16[4,2,1056,128]{3,2,1,0:T(8,128)(2,1)} %copy.413), calls=%async_computation.6 | async-start | bytes 4325376 | tf_op jit(solution)/shard_map/all_to_all | solution.py:1113
  428.7 52.3 %collective-permute-start.68 = (bf16[2,2,128,640]{3,2,1,0:T(8,128)(2,1)}, bf16[2,2,128,640]{3,2,1,0:T(8,128)(2,1)S(1)}, u32[]{:S(2)}, u32[]{:S(2)}) collective-permute-start(bf16[2,2,128,640]{3,2,1,0:T(8,128)(2,1)} %add_convert_fusion.11), channel_id=1, source_target_pairs={{0,2},{1,3},{2,0},{3,1},{4,6},{5,7},{6,4},{7,5},{8,10},{9,11},{10,... | collective-permute-start | bytes 1966088 | tf_op jit(solution)/shard_map/ppermute | solution.py:1125
  452.1 30.6 %collective-permute-start.69 = (bf16[2,2,128,640]{3,2,1,0:T(8,128)(2,1)S(1)}, bf16[2,2,128,640]{3,2,1,0:T(8,128)(2,1)S(1)}, u32[]{:S(2)}, u32[]{:S(2)}) collective-permute-start(bf16[2,2,128,640]{3,2,1,0:T(8,128)(2,1)S(1)} %copy-done.47), channel_id=1, source_target_pairs={{0,4},{4,0},{1,5},{5,1},{2,6},{6,2},{3,7},{7,3},{8,12},{12,8},{9,1... | collective-permute-start | bytes 1966088 | tf_op jit(solution)/shard_map/ppermute | solution.py:1117
  452.6 22.7 %collective-permute-start.52 = (bf16[2,2,64,512]{3,2,1,0:T(8,128)(2,1)S(1)}, bf16[2,2,64,512]{3,2,1,0:T(8,128)(2,1)S(1)}, u32[]{:S(2)}, u32[]{:S(2)}) collective-permute-start(bf16[2,2,64,512]{3,2,1,0:T(8,128)(2,1)S(1)} %bitcast.500), channel_id=1, source_target_pairs={{0,4},{4,0},{1,5},{5,1},{2,6},{6,2},{3,7},{7,3},{8,12},{12,8},{9,1... | collective-permute-start | bytes 786440 | tf_op jit(solution)/shard_map/ppermute | solution.py:1117
  457.0 22.7 %collective-permute-start.59 = (bf16[2,2,64,512]{3,2,1,0:T(8,128)(2,1)S(1)}, bf16[2,2,64,512]{3,2,1,0:T(8,128)(2,1)S(1)}, u32[]{:S(2)}, u32[]{:S(2)}) collective-permute-start(bf16[2,2,64,512]{3,2,1,0:T(8,128)(2,1)S(1)} %bitcast.503), channel_id=1, source_target_pairs={{0,4},{4,0},{1,5},{5,1},{2,6},{6,2},{3,7},{7,3},{8,12},{12,8},{9,1... | collective-permute-start | bytes 786440 | tf_op jit(solution)/shard_map/ppermute | solution.py:1117
  476.2 26.6 %collective-permute-start.53 = (bf16[2,64,512]{2,1,0:T(8,128)(2,1)}, bf16[2,64,512]{2,1,0:T(8,128)(2,1)}, u32[]{:S(2)}, u32[]{:S(2)}) collective-permute-start(bf16[2,64,512]{2,1,0:T(8,128)(2,1)} %get-tuple-element.271), channel_id=1, source_target_pairs={{0,24},{8,16},{16,8},{24,0},{1,25},{9,17},{17,9},{25,1},{2,26},{10... | collective-permute-start | bytes 393224 | tf_op jit(solution)/shard_map/ppermute | solution.py:1136
  479.7 24.6 %collective-permute-start.54 = (bf16[2,64,512]{2,1,0:T(8,128)(2,1)}, bf16[2,64,512]{2,1,0:T(8,128)(2,1)}, u32[]{:S(2)}, u32[]{:S(2)}) collective-permute-start(bf16[2,64,512]{2,1,0:T(8,128)(2,1)} %get-tuple-element.191), channel_id=1, source_target_pairs={{0,16},{8,24},{16,0},{24,8},{1,17},{9,25},{17,1},{25,9},{2,18},{10... | collective-permute-start | bytes 393224 | tf_op jit(solution)/shard_map/ppermute | solution.py:1136
  481.0 23.3 %collective-permute-start.55 = (bf16[2,64,512]{2,1,0:T(8,128)(2,1)}, bf16[2,64,512]{2,1,0:T(8,128)(2,1)}, u32[]{:S(2)}, u32[]{:S(2)}) collective-permute-start(bf16[2,64,512]{2,1,0:T(8,128)(2,1)} %get-tuple-element.270), channel_id=1, source_target_pairs={{0,8},{8,0},{16,24},{24,16},{1,9},{9,1},{17,25},{25,17},{2,10},{10... | collective-permute-start | bytes 393224 | tf_op jit(solution)/shard_map/ppermute | solution.py:1136
  482.7 23.6 %collective-permute-start.60 = (bf16[2,64,512]{2,1,0:T(8,128)(2,1)}, bf16[2,64,512]{2,1,0:T(8,128)(2,1)}, u32[]{:S(2)}, u32[]{:S(2)}) collective-permute-start(bf16[2,64,512]{2,1,0:T(8,128)(2,1)} %get-tuple-element.264), channel_id=1, source_target_pairs={{0,24},{8,16},{16,8},{24,0},{1,25},{9,17},{17,9},{25,1},{2,26},{10... | collective-permute-start | bytes 393224 | tf_op jit(solution)/shard_map/ppermute | solution.py:1136
  494.3 40.2 %all-to-all-start.7 = ((bf16[4,2,128,640]{3,2,1,0:T(8,128)(2,1)}), bf16[4,2,128,640]{3,2,1,0:T(8,128)(2,1)}, u32[]{:S(2)}, u32[]{:S(2)}) async-start(bf16[4,2,128,640]{3,2,1,0:T(8,128)(2,1)} %copy.415), calls=%async_computation.7 | async-start | bytes 2621440 | tf_op jit(solution)/shard_map/all_to_all | solution.py:1113
  (115 other events, 1193.5 us)

commit v5 on v4

--- a/solution.py
+++ b/solution.py
@@ -423,9 +423,9 @@
         out_specs=out_specs,
         out_shape=out_shape,
         scratch_shapes=scratch,
-        compiler_params=pltpu.CompilerParams(vmem_limit_bytes=48 << 20),
+        compiler_params=pltpu.CompilerParams(vmem_limit_bytes=44 << 20),
         cost_estimate=pl.CostEstimate(
-            flops=10 * 10**9, bytes_accessed=8 << 20, transcendentals=0
+            flops=6 * 10**9, bytes_accessed=8 << 20, transcendentals=0
         ),
         name=name,
     )(*inputs)
@@ -1229,6 +1229,12 @@
     return jnp.sum(wide(moved), 0)
 
 
+def column_hops(chip):
+    size = lax.axis_size("dp")
+    blocks = by_difference(jnp.split(chip, size), lax.axis_index("dp"))
+    return sum([wide(blocks[0])] + [wide(swap_dp(blocks[k], k)) for k in range(1, size)])
+
+
 def column_body(
     block_input,
     segment_ids,
@@ -1393,7 +1399,7 @@
         ffn_pair, way_pair, scales, ffn_weights, hidden
     )
     chip = column_chip(near, far)
-    ffn_in_grad = column_total(chip)
+    ffn_in_grad = column_hops(chip)
     near, far, ffn_grads = column_ffn_grads(
         after(active, chip),
         gate_grad,

time: 548 us -> 540 us (0.985)
    all_to_all x8 -> x7, waiting for transfers between devices: 42.1 us -> 32 us  [exchange(): return lax.all_to_all(values, axis, 0, 0, tiled=True)]
    all_to_all x8 -> x7, starting transfers between devices: 56.2 us -> 47.3 us  [exchange(): return lax.all_to_all(values, axis, 0, 0, tiled=True)]
    ppermute x16 -> x19, starting transfers between devices: 20.7 us -> 28 us  [swap_dp(): lax.ppermute(values, 'dp', [(i, i ^ k) for i in range(lax.axis_size('dp'))])]
    unnamed x138 -> x166, local copies, waits for them, and re-layouts: 19.5 us -> 24.9 us
    ppermute x16 -> x19, waiting for transfers between devices: 68.2 us -> 72.1 us  [swap_dp(): lax.ppermute(values, 'dp', [(i, i ^ k) for i in range(lax.axis_size('dp'))])]
  transfers between devices with their start and end apart: 84 -> 86, of which waited for: 36 -> 36; matrix products, arithmetic and copies ran while one was open for 19% -> 19% of each run, Pallas kernels for 10% -> 9%
where the time goes in v5:
time: 540 us; the launch traced here: 533 us
  waiting for transfers between devices  211 us (39%)
  starting transfers between devices  127 us (24%)
  Pallas kernels  67.5 us (12%)
  local copies, waits for them, and re-layouts  67.3 us (12%)
  other arithmetic  56.4 us (10%)
    ppermute x19, waiting for transfers between devices, swap_dp(): lax.ppermute(values, 'dp', [(i, i ^ k) for i in range(lax.axis_size('dp'))])  72.1 us
    pallas_call x5, Pallas kernels, call(): pl.pallas_call(kernel, grid=(grid,), in_specs=in_specs, out_specs=out_spe...  67.5 us
    ppermute x12, waiting for transfers between devices, swap_mp(): return lax.ppermute(values, 'mp', SWAP)  50.9 us
    all_to_all x7, starting transfers between devices, exchange(): return lax.all_to_all(values, axis, 0, 0, tiled=True)  47.3 us
    all_to_all x7, waiting for transfers between devices, exchange(): return lax.all_to_all(values, axis, 0, 0, tiled=True)  32 us
    ppermute x24, waiting for transfers between devices, trade_blocks(): lax.ppermute(blocks[k], axis, [(i, i ^ k) for i in range(size)])  29 us
    ppermute x19, starting transfers between devices, swap_dp(): lax.ppermute(values, 'dp', [(i, i ^ k) for i in range(lax.axis_size('dp'))])  28 us
    ppermute x24, starting transfers between devices, trade_blocks(): lax.ppermute(blocks[k], axis, [(i, i ^ k) for i in range(size)])  25.4 us
  transfers between devices with their start and end apart: 86, of which 36 were waited for; matrix products, arithmetic and copies ran while one was open for 19% of the time, Pallas kernels for 9%

profile of v5, /device:TPU:16, one launch (start us, length us, event | category | flops | bytes accessed | tf_op | source)
XLA Modules:
  0.0 532.9 jit_solution(12212853550938919021)
XLA Ops:
  17.3 7.1 %all-to-all-start = ((bf16[4,2,128,640]{3,2,1,0:T(8,128)(2,1)}), bf16[4,2,128,640]{3,2,1,0:T(8,128)(2,1)}, u32[]{:S(2)}, u32[]{:S(2)}) async-start(bf16[4,2,128,640]{3,2,1,0:T(8,128)(2,1)} %copy.372), calls=%async_computation | async-start | bytes 2621440 | tf_op jit(solution)/shard_map/all_to_all | solution.py:1113
  61.4 4.3 collective-permute-start.14
  67.1 7.5 %all-to-all-start.1 = ((bf16[4,2,1056,128]{3,2,1,0:T(8,128)(2,1)}), bf16[4,2,1056,128]{3,2,1,0:T(8,128)(2,1)}, u32[]{:S(2)}, u32[]{:S(2)}) async-start(bf16[4,2,1056,128]{3,2,1,0:T(8,128)(2,1)} %pad_maximum_fusion), calls=%async_computation.1 | async-start | bytes 4325376 | tf_op jit(solution)/shard_map/all_to_all | solution.py:1113
  74.6 6.9 %collective-permute-done.13 = bf16[64,2048]{1,0:T(8,128)(2,1)S(1)} collective-permute-done((bf16[64,2048]{1,0:T(8,128)(2,1)S(1)}, bf16[64,2048]{1,0:T(8,128)(2,1)S(1)}, u32[]{:S(2)}, u32[]{:S(2)}) %collective-permute-start.13) | collective-permute-done | bytes 262176 | tf_op jit(solution)/shard_map/ppermute | solution.py:1129
  81.5 15.1 %collective-permute-done.14 = bf16[64,2048]{1,0:T(8,128)(2,1)S(1)} collective-permute-done((bf16[64,2048]{1,0:T(8,128)(2,1)S(1)}, bf16[64,2048]{1,0:T(8,128)(2,1)S(1)}, u32[]{:S(2)}, u32[]{:S(2)}) %collective-permute-start.14) | collective-permute-done | bytes 262176 | tf_op jit(solution)/shard_map/ppermute | solution.py:1129
  100.9 14.8 %collective-permute-done.19.refs_5_ = bf16[2,2,128,640]{3,2,1,0:T(8,128)(2,1)S(1)} collective-permute-done((bf16[2,2,128,640]{3,2,1,0:T(8,128)(2,1)S(1)}, bf16[2,2,128,640]{3,2,1,0:T(8,128)(2,1)S(1)}, u32[]{:S(2)}, u32[]{:S(2)}) %collective-permute-start.19) | collective-permute-done | bytes 655392 | tf_op jit(solution)/shard_map/ppermute | solution.py:1125
  116.2 16.4 %column_forward.1 = (bf16[512,256]{1,0:T(8,128)(2,1)S(1)}, f32[2,2,256,256]{3,2,1,0:T(8,128)S(1)}, f32[512,256]{1,0:T(8,128)S(1)}, f32[512,256]{1,0:T(8,128)S(1)...) custom-call(bf16[256,2048]{1,0:T(8,128)(2,1)S(1)} %pad_maximum_fusio, ...), custom_call_target="tpu_custom_call" | custom-call | flops 6000000000 | bytes 8388608 | tf_op jit(solution)/shard_map/column_forward/pallas_call | solution.py:419
  143.2 6.6 %all-to-all-start.2 = ((bf16[4,64,2048]{2,1,0:T(8,128)(2,1)}), bf16[4,64,2048]{2,1,0:T(8,128)(2,1)S(1)}, u32[]{:S(2)}, u32[]{:S(2)}) async-start(bf16[4,64,2048]{2,1,0:T(8,128)(2,1)} %bitcast.53), calls=%async_computation.2 | async-start | bytes 2097152 | tf_op jit(solution)/shard_map/all_to_all | solution.py:1113
  158.0 14.4 %all-to-all-done.2 = bf16[4,64,2048]{2,1,0:T(8,128)(2,1)S(1)} async-done(((bf16[4,64,2048]{2,1,0:T(8,128)(2,1)}), bf16[4,64,2048]{2,1,0:T(8,128)(2,1)S(1)}, u32[]{:S(2)}, u32[]{:S(2)}) %all-to-all-start.2) | async-done | bytes 1048608 | tf_op jit(solution)/shard_map/all_to_all | solution.py:1113
  174.1 4.2 collective-permute-start.23
  179.0 24.9 %collective-permute-done.37.refs_7_.refs_2_ = bf16[4,2,1056,128]{3,2,1,0:T(8,128)(2,1)} collective-permute-done((bf16[4,2,1056,128]{3,2,1,0:T(8,128)(2,1)}, bf16[4,2,1056,128]{3,2,1,0:T(8,128)(2,1)}, u32[]{:S(2)}, u32[]{:S(2)}) %collective-permute-start.37) | collective-permute-done | bytes 2162720 | tf_op jit(solution)/shard_map/ppermute | solution.py:1117
  210.7 4.1 collective-permute-start.33
  215.1 15.7 %collective-permute-done.32 = bf16[64,2048]{1,0:T(8,128)(2,1)S(1)} collective-permute-done((bf16[64,2048]{1,0:T(8,128)(2,1)S(1)}, bf16[64,2048]{1,0:T(8,128)(2,1)S(1)}, u32[]{:S(2)}, u32[]{:S(2)}) %collective-permute-start.32) | collective-permute-done | bytes 262176 | tf_op jit(solution)/shard_map/ppermute | solution.py:1129
  236.3 17.2 %column_ffn.1 = (bf16[256,2048]{1,0:T(8,128)(2,1)S(1)}, bf16[256,2048]{1,0:T(8,128)(2,1)}, bf16[512,2048]{1,0:T(8,128)(2,1)}, bf16[512,2048]{1,0:T(8,128)(2,1)},...) custom-call(bf16[256,2048]{1,0:T(8,128)(2,1)S(1)} %pad_maximum_fusion.10.refs_0_, ...), custom_call_target="tpu_custom_call" | custom-call | flops 6000000000 | bytes 8388608 | tf_op jit(solution)/shard_map/column_ffn/pallas_call | solution.py:419
  261.3 4.3 collective-permute-start.43
  265.6 13.0 %column_ffn_grads.1 = (bf16[256,2048]{1,0:T(8,128)(2,1)S(1)}, bf16[256,2048]{1,0:T(8,128)(2,1)S(1)}, bf16[4,2,1056,128]{3,2,1,0:T(8,128)(2,1)}, bf16[4,2,1056,12...) custom-call(bf16[512,704]{1,0:T(8,128)(2,1)S(1)} %copy-done.20, ...), custom_call_target="tpu_custom_call" | custom-call | flops 6000000000 | bytes 8388608 | tf_op jit(solution)/shard_map/column_ffn_grads/pallas_call | solution.py:419
  289.9 3.8 collective-permute-start.46
  293.8 16.0 %collective-permute-done.45 = bf16[64,2048]{1,0:T(8,128)(2,1)S(1)} collective-permute-done((bf16[64,2048]{1,0:T(8,128)(2,1)S(1)}, bf16[64,2048]{1,0:T(8,128)(2,1)S(1)}, u32[]{:S(2)}, u32[]{:S(2)}) %collective-permute-start.45) | collective-permute-done | bytes 262176 | tf_op jit(solution)/shard_map/ppermute | solution.py:1129
  313.0 7.8 %all-to-all-start.3 = ((bf16[4,64,2048]{2,1,0:T(8,128)(2,1)}), bf16[4,64,2048]{2,1,0:T(8,128)(2,1)}, u32[]{:S(2)}, u32[]{:S(2)}) async-start(bf16[4,64,2048]{2,1,0:T(8,128)(2,1)} %bitcast.80), calls=%async_computation.3 | async-start | bytes 2097152 | tf_op jit(solution)/shard_map/all_to_all | solution.py:1113
  320.8 11.6 %collective-permute-done.74 = bf16[4,2,1056,128]{3,2,0,1:T(8,128)(2,1)} collective-permute-done((bf16[4,2,1056,128]{3,2,0,1:T(8,128)(2,1)}, bf16[4,2,1056,128]{3,2,0,1:T(8,128)(2,1)}, u32[]{:S(2)}, u32[]{:S(2)}) %collective-permute-start.74) | collective-permute-done | bytes 2162720 | tf_op jit(solution)/shard_map/ppermute | solution.py:1117
  341.8 16.0 %column_backward.1 = (bf16[512,1024]{1,0:T(8,128)(2,1)S(1)}, f32[512,2]{1,0:T(8,128)S(1)}, f32[2,12,256]{2,1,0:T(8,128)S(1)}, f32[2,1,128]{2,1,0:T(1,128)S(1)}, ...) custom-call(bf16[256,2048]{1,0:T(8,128)(2,1)S(1)} %pad_maximum_fusion.12.refs_0_, ...), custom_call_target="tpu_custom_call" | custom-call | flops 6000000000 | bytes 8388608 | tf_op jit(solution)/shard_map/column_backward/pallas_call | solution.py:419
  357.9 4.9 column_mixer_grads.1
  377.7 6.2 %all-to-all-start.4 = ((bf16[4,64,2048]{2,1,0:T(8,128)(2,1)}), bf16[4,64,2048]{2,1,0:T(8,128)(2,1)}, u32[]{:S(2)}, u32[]{:S(2)}) async-start(bf16[4,64,2048]{2,1,0:T(8,128)(2,1)} %bitcast.489), calls=%async_computation.4 | async-start | bytes 2097152 | tf_op jit(solution)/shard_map/all_to_all | solution.py:1113
  391.0 15.9 %all-to-all-done.4 = bf16[4,64,2048]{2,1,0:T(8,128)(2,1)} async-done(((bf16[4,64,2048]{2,1,0:T(8,128)(2,1)}), bf16[4,64,2048]{2,1,0:T(8,128)(2,1)}, u32[]{:S(2)}, u32[]{:S(2)}) %all-to-all-start.4) | async-done | bytes 1048608 | tf_op jit(solution)/shard_map/all_to_all | solution.py:1113
  406.9 7.8 %all-to-all-start.5 = ((bf16[4,2,1056,128]{3,2,1,0:T(8,128)(2,1)}), bf16[4,2,1056,128]{3,2,1,0:T(8,128)(2,1)}, u32[]{:S(2)}, u32[]{:S(2)}) async-start(bf16[4,2,1056,128]{3,2,1,0:T(8,128)(2,1)} %copy.413), calls=%async_computation.5 | async-start | bytes 4325376 | tf_op jit(solution)/shard_map/all_to_all | solution.py:1113
  429.0 3.7 collective-permute-done.66
  433.6 4.5 collective-permute-done.52
  450.0 12.2 %collective-permute-done.69 = f32[1,2,89,128]{3,2,1,0:T(8,128)S(1)} collective-permute-done((f32[1,2,89,128]{3,2,1,0:T(8,128)S(1)}, f32[1,2,89,128]{3,2,1,0:T(8,128)S(1)}, u32[]{:S(2)}, u32[]{:S(2)}) %collective-permute-start.69) | collective-permute-done | bytes 91168 | tf_op jit(solution)/shard_map/ppermute | solution.py:1129
  462.3 5.4 %collective-permute-done.55 = bf16[2,2,64,512]{3,2,1,0:T(8,128)(2,1)S(1)} collective-permute-done((bf16[2,2,64,512]{3,2,1,0:T(8,128)(2,1)S(1)}, bf16[2,2,64,512]{3,2,1,0:T(8,128)(2,1)S(1)}, u32[]{:S(2)}, u32[]{:S(2)}) %collective-permute-start.55) | collective-permute-done | bytes 262176 | tf_op jit(solution)/shard_map/ppermute | solution.py:1117
  480.4 3.7 collective-permute-start.64
  487.3 4.4 all-to-all-start.6
  501.2 16.8 %collective-permute-done.65 = bf16[2,64,512]{2,1,0:T(8,128)(2,1)S(1)} collective-permute-done((bf16[2,64,512]{2,1,0:T(8,128)(2,1)S(1)}, bf16[2,64,512]{2,1,0:T(8,128)(2,1)S(1)}, u32[]{:S(2)}, u32[]{:S(2)}) %collective-permute-start.65) | collective-permute-done | bytes 131104 | tf_op jit(solution)/shard_map/ppermute | solution.py:1136
  (538 shorter events, 213.1 us)
Async XLA Ops:
  17.3 37.0 %all-to-all-start = ((bf16[4,2,128,640]{3,2,1,0:T(8,128)(2,1)}), bf16[4,2,128,640]{3,2,1,0:T(8,128)(2,1)}, u32[]{:S(2)}, u32[]{:S(2)}) async-start(bf16[4,2,128,640]{3,2,1,0:T(8,128)(2,1)} %copy.372), calls=%async_computation | async-start | bytes 2621440 | tf_op jit(solution)/shard_map/all_to_all | solution.py:1113
  56.3 42.9 %collective-permute-start.17 = (bf16[4,2,128,640]{3,2,1,0:T(8,128)(2,1)}, bf16[4,2,128,640]{3,2,1,0:T(8,128)(2,1)S(1)}, u32[]{:S(2)}, u32[]{:S(2)}) collective-permute-start(bf16[4,2,128,640]{3,2,1,0:T(8,128)(2,1)} %all-to-all-done.refs_2_), channel_id=1, source_target_pairs={{0,2},{1,3},{2,0},{3,1},{4,6},{5,7},{6,4},{7,5},{8,10},{9,11},{10,... | collective-permute-start | bytes 3932168 | tf_op jit(solution)/shard_map/ppermute | solution.py:1125
  57.8 39.6 %collective-permute-start.18 = (bf16[4,2,128,640]{3,2,1,0:T(8,128)(2,1)}, bf16[4,2,128,640]{3,2,1,0:T(8,128)(2,1)}, u32[]{:S(2)}, u32[]{:S(2)}) collective-permute-start(bf16[4,2,128,640]{3,2,1,0:T(8,128)(2,1)} %all-to-all-done.refs_2_), channel_id=1, source_target_pairs={{0,4},{4,0},{1,5},{5,1},{2,6},{6,2},{3,7},{7,3},{8,12},{12,8},{9,1... | collective-permute-start | bytes 3932168 | tf_op jit(solution)/shard_map/ppermute | solution.py:1117
  61.4 35.2 %collective-permute-start.14 = (bf16[64,2048]{1,0:T(8,128)(2,1)S(1)}, bf16[64,2048]{1,0:T(8,128)(2,1)S(1)}, u32[]{:S(2)}, u32[]{:S(2)}) collective-permute-start(bf16[64,2048]{1,0:T(8,128)(2,1)S(1)} %pad_maximum_fusion.17), channel_id=1, source_target_pairs={{0,16},{8,24},{16,0},{24,8},{1,17},{9,25},{17,1},{25,9},{2,18},{10... | collective-permute-start | bytes 786440 | tf_op jit(solution)/shard_map/ppermute | solution.py:1129
  65.7 30.9 %collective-permute-start.15 = (bf16[64,2048]{1,0:T(8,128)(2,1)S(1)}, bf16[64,2048]{1,0:T(8,128)(2,1)S(1)}, u32[]{:S(2)}, u32[]{:S(2)}) collective-permute-start(bf16[64,2048]{1,0:T(8,128)(2,1)S(1)} %pad_maximum_fusion.17), channel_id=1, source_target_pairs={{0,8},{8,0},{16,24},{24,16},{1,9},{9,1},{17,25},{25,17},{2,10},{10... | collective-permute-start | bytes 786440 | tf_op jit(solution)/shard_map/ppermute | solution.py:1129
  67.1 76.1 %all-to-all-start.1 = ((bf16[4,2,1056,128]{3,2,1,0:T(8,128)(2,1)}), bf16[4,2,1056,128]{3,2,1,0:T(8,128)(2,1)}, u32[]{:S(2)}, u32[]{:S(2)}) async-start(bf16[4,2,1056,128]{3,2,1,0:T(8,128)(2,1)} %pad_maximum_fusion), calls=%async_computation.1 | async-start | bytes 4325376 | tf_op jit(solution)/shard_map/all_to_all | solution.py:1113
  143.2 29.2 %all-to-all-start.2 = ((bf16[4,64,2048]{2,1,0:T(8,128)(2,1)}), bf16[4,64,2048]{2,1,0:T(8,128)(2,1)S(1)}, u32[]{:S(2)}, u32[]{:S(2)}) async-start(bf16[4,64,2048]{2,1,0:T(8,128)(2,1)} %bitcast.53), calls=%async_computation.2 | async-start | bytes 2097152 | tf_op jit(solution)/shard_map/all_to_all | solution.py:1113
  153.5 53.4 %collective-permute-start.36 = (bf16[4,2,1056,128]{3,2,1,0:T(8,128)(2,1)}, bf16[4,2,1056,128]{3,2,1,0:T(8,128)(2,1)}, u32[]{:S(2)}, u32[]{:S(2)}) collective-permute-start(bf16[4,2,1056,128]{3,2,1,0:T(8,128)(2,1)} %all-to-all-done.1.refs_5_.refs_0_), channel_id=1, source_target_pairs={{0,2},{1,3},{2,0},{3,1},{4,6},{5,7},{6,4},{7,5},{8,10},{9,11},{10,... | collective-permute-start | bytes 6488072 | tf_op jit(solution)/shard_map/ppermute | solution.py:1125
  154.9 49.0 %collective-permute-start.37 = (bf16[4,2,1056,128]{3,2,1,0:T(8,128)(2,1)}, bf16[4,2,1056,128]{3,2,1,0:T(8,128)(2,1)}, u32[]{:S(2)}, u32[]{:S(2)}) collective-permute-start(bf16[4,2,1056,128]{3,2,1,0:T(8,128)(2,1)} %all-to-all-done.1.refs_5_.refs_0_), channel_id=1, source_target_pairs={{0,4},{4,0},{1,5},{5,1},{2,6},{6,2},{3,7},{7,3},{8,12},{12,8},{9,1... | collective-permute-start | bytes 6488072 | tf_op jit(solution)/shard_map/ppermute | solution.py:1117
  172.9 37.8 %collective-permute-start.22 = (bf16[64,2048]{1,0:T(8,128)(2,1)S(1)}, bf16[64,2048]{1,0:T(8,128)(2,1)S(1)}, u32[]{:S(2)}, u32[]{:S(2)}) collective-permute-start(bf16[64,2048]{1,0:T(8,128)(2,1)S(1)} %multiply_convert_fusion), channel_id=1, source_target_pairs={{0,24},{8,16},{16,8},{24,0},{1,25},{9,17},{17,9},{25,1},{2,26},{10... | collective-permute-start | bytes 786440 | tf_op jit(solution)/shard_map/ppermute | solution.py:1129
  174.1 36.7 %collective-permute-start.23 = (bf16[64,2048]{1,0:T(8,128)(2,1)S(1)}, bf16[64,2048]{1,0:T(8,128)(2,1)S(1)}, u32[]{:S(2)}, u32[]{:S(2)}) collective-permute-start(bf16[64,2048]{1,0:T(8,128)(2,1)S(1)} %multiply_convert_fusion), channel_id=1, source_target_pairs={{0,16},{8,24},{16,0},{24,8},{1,17},{9,25},{17,1},{25,9},{2,18},{10... | collective-permute-start | bytes 786440 | tf_op jit(solution)/shard_map/ppermute | solution.py:1129
  178.2 36.6 %collective-permute-start.24 = (bf16[64,2048]{1,0:T(8,128)(2,1)S(1)}, bf16[64,2048]{1,0:T(8,128)(2,1)S(1)}, u32[]{:S(2)}, u32[]{:S(2)}) collective-permute-start(bf16[64,2048]{1,0:T(8,128)(2,1)S(1)} %multiply_convert_fusion), channel_id=1, source_target_pairs={{0,8},{8,0},{16,24},{24,16},{1,9},{9,1},{17,25},{25,17},{2,10},{10... | collective-permute-start | bytes 786440 | tf_op jit(solution)/shard_map/ppermute | solution.py:1129
  206.2 26.8 %collective-permute-start.38 = (bf16[2,2,1056,128]{3,2,1,0:T(8,128)(2,1)}, bf16[2,2,1056,128]{3,2,1,0:T(8,128)(2,1)}, u32[]{:S(2)}, u32[]{:S(2)}) collective-permute-start(bf16[2,2,1056,128]{3,2,1,0:T(8,128)(2,1)} %slice.465), channel_id=1, source_target_pairs={{0,2},{1,3},{2,0},{3,1},{4,6},{5,7},{6,4},{7,5},{8,10},{9,11},{10,... | collective-permute-start | bytes 3244040 | tf_op jit(solution)/shard_map/ppermute | solution.py:1125
  209.2 24.8 %collective-permute-start.39 = (bf16[2,2,1056,128]{3,2,1,0:T(8,128)(2,1)}, bf16[2,2,1056,128]{3,2,1,0:T(8,128)(2,1)}, u32[]{:S(2)}, u32[]{:S(2)}) collective-permute-start(bf16[2,2,1056,128]{3,2,1,0:T(8,128)(2,1)} %slice.466), channel_id=1, source_target_pairs={{0,4},{4,0},{1,5},{5,1},{2,6},{6,2},{3,7},{7,3},{8,12},{12,8},{9,1... | collective-permute-start | bytes 3244040 | tf_op jit(solution)/shard_map/ppermute | solution.py:1117
  259.6 25.7 %collective-permute-start.44 = (bf16[64,2048]{1,0:T(8,128)(2,1)S(1)}, bf16[64,2048]{1,0:T(8,128)(2,1)S(1)}, u32[]{:S(2)}, u32[]{:S(2)}) collective-permute-start(bf16[64,2048]{1,0:T(8,128)(2,1)S(1)} %get-tuple-element.237), channel_id=1, source_target_pairs={{0,24},{8,16},{16,8},{24,0},{1,25},{9,17},{17,9},{25,1},{2,26},{10... | collective-permute-start | bytes 786440 | tf_op jit(solution)/shard_map/ppermute | solution.py:1129
  261.3 25.2 %collective-permute-start.43 = (bf16[64,2048]{1,0:T(8,128)(2,1)S(1)}, bf16[64,2048]{1,0:T(8,128)(2,1)S(1)}, u32[]{:S(2)}, u32[]{:S(2)}) collective-permute-start(bf16[64,2048]{1,0:T(8,128)(2,1)S(1)} %get-tuple-element.236), channel_id=1, source_target_pairs={{0,16},{8,24},{16,0},{24,8},{1,17},{9,25},{17,1},{25,9},{2,18},{10... | collective-permute-start | bytes 786440 | tf_op jit(solution)/shard_map/ppermute | solution.py:1129
  282.6 49.8 %collective-permute-start.74 = (bf16[4,2,1056,128]{3,2,0,1:T(8,128)(2,1)}, bf16[4,2,1056,128]{3,2,0,1:T(8,128)(2,1)}, u32[]{:S(2)}, u32[]{:S(2)}) collective-permute-start(bf16[4,2,1056,128]{3,2,0,1:T(8,128)(2,1)} %pad_maximum_fusion.1), channel_id=1, source_target_pairs={{0,4},{4,0},{1,5},{5,1},{2,6},{6,2},{3,7},{7,3},{8,12},{12,8},{9,1... | collective-permute-start | bytes 6488072 | tf_op jit(solution)/shard_map/ppermute | solution.py:1117
  285.3 51.2 %collective-permute-start.76 = (bf16[4,2,1056,128]{3,2,0,1:T(8,128)(2,1)}, bf16[4,2,1056,128]{3,2,0,1:T(8,128)(2,1)}, u32[]{:S(2)}, u32[]{:S(2)}) collective-permute-start(bf16[4,2,1056,128]{3,2,0,1:T(8,128)(2,1)} %pad_maximum_fusion.2), channel_id=1, source_target_pairs={{0,2},{1,3},{2,0},{3,1},{4,6},{5,7},{6,4},{7,5},{8,10},{9,11},{10,... | collective-permute-start | bytes 6488072 | tf_op jit(solution)/shard_map/ppermute | solution.py:1125
  312.9 26.6 %collective-permute-start.48 = (bf16[256,2048]{1,0:T(8,128)(2,1)S(1)}, bf16[256,2048]{1,0:T(8,128)(2,1)S(1)}, u32[]{:S(2)}, u32[]{:S(2)}) collective-permute-start(bf16[256,2048]{1,0:T(8,128)(2,1)S(1)} %pad_maximum_fusion.12.refs_0_), channel_id=1, source_target_pairs={{0,1},{1,0},{2,3},{3,2},{4,5},{5,4},{6,7},{7,6},{8,9},{9,8},{10,11... | collective-permute-start | bytes 3145736 | tf_op jit(solution)/shard_map/ppermute | solution.py:1121
  313.0 64.7 %all-to-all-start.3 = ((bf16[4,64,2048]{2,1,0:T(8,128)(2,1)}), bf16[4,64,2048]{2,1,0:T(8,128)(2,1)}, u32[]{:S(2)}, u32[]{:S(2)}) async-start(bf16[4,64,2048]{2,1,0:T(8,128)(2,1)} %bitcast.80), calls=%async_computation.3 | async-start | bytes 2097152 | tf_op jit(solution)/shard_map/all_to_all | solution.py:1113
  335.3 35.1 %collective-permute-start.75 = (bf16[2,2,1056,128]{3,2,0,1:T(8,128)(2,1)}, bf16[2,2,1056,128]{3,2,0,1:T(8,128)(2,1)}, u32[]{:S(2)}, u32[]{:S(2)}) collective-permute-start(bf16[2,2,1056,128]{3,2,0,1:T(8,128)(2,1)} %add_convert_fusion.3), channel_id=1, source_target_pairs={{0,2},{1,3},{2,0},{3,1},{4,6},{5,7},{6,4},{7,5},{8,10},{9,11},{10,... | collective-permute-start | bytes 3244040 | tf_op jit(solution)/shard_map/ppermute | solution.py:1125
  339.0 31.4 %collective-permute-start.77 = (bf16[2,2,1056,128]{3,2,0,1:T(8,128)(2,1)}, bf16[2,2,1056,128]{3,2,0,1:T(8,128)(2,1)}, u32[]{:S(2)}, u32[]{:S(2)}) collective-permute-start(bf16[2,2,1056,128]{3,2,0,1:T(8,128)(2,1)} %add_convert_fusion.1), channel_id=1, source_target_pairs={{0,4},{4,0},{1,5},{5,1},{2,6},{6,2},{3,7},{7,3},{8,12},{12,8},{9,1... | collective-permute-start | bytes 3244040 | tf_op jit(solution)/shard_map/ppermute | solution.py:1117
  365.2 51.9 %collective-permute-start.49 = (bf16[4,2,128,640]{3,2,1,0:T(8,128)(2,1)}, bf16[4,2,128,640]{3,2,1,0:T(8,128)(2,1)}, u32[]{:S(2)}, u32[]{:S(2)}) collective-permute-start(bf16[4,2,128,640]{3,2,1,0:T(8,128)(2,1)} %pad_maximum_fusion.5), channel_id=1, source_target_pairs={{0,4},{4,0},{1,5},{5,1},{2,6},{6,2},{3,7},{7,3},{8,12},{12,8},{9,1... | collective-permute-start | bytes 3932168 | tf_op jit(solution)/shard_map/ppermute | solution.py:1117
  367.9 49.1 %collective-permute-start.50 = (bf16[4,2,128,640]{3,2,1,0:T(8,128)(2,1)}, bf16[4,2,128,640]{3,2,1,0:T(8,128)(2,1)}, u32[]{:S(2)}, u32[]{:S(2)}) collective-permute-start(bf16[4,2,128,640]{3,2,1,0:T(8,128)(2,1)} %pad_maximum_fusion.6), channel_id=1, source_target_pairs={{0,2},{1,3},{2,0},{3,1},{4,6},{5,7},{6,4},{7,5},{8,10},{9,11},{10,... | collective-permute-start | bytes 3932168 | tf_op jit(solution)/shard_map/ppermute | solution.py:1125
  377.7 29.2 %all-to-all-start.4 = ((bf16[4,64,2048]{2,1,0:T(8,128)(2,1)}), bf16[4,64,2048]{2,1,0:T(8,128)(2,1)}, u32[]{:S(2)}, u32[]{:S(2)}) async-start(bf16[4,64,2048]{2,1,0:T(8,128)(2,1)} %bitcast.489), calls=%async_computation.4 | async-start | bytes 2097152 | tf_op jit(solution)/shard_map/all_to_all | solution.py:1113
  406.9 77.5 %all-to-all-start.5 = ((bf16[4,2,1056,128]{3,2,1,0:T(8,128)(2,1)}), bf16[4,2,1056,128]{3,2,1,0:T(8,128)(2,1)}, u32[]{:S(2)}, u32[]{:S(2)}) async-start(bf16[4,2,1056,128]{3,2,1,0:T(8,128)(2,1)} %copy.413), calls=%async_computation.5 | async-start | bytes 4325376 | tf_op jit(solution)/shard_map/all_to_all | solution.py:1113
  420.5 52.9 %collective-permute-start.71 = (bf16[2,2,128,640]{3,2,1,0:T(8,128)(2,1)}, bf16[2,2,128,640]{3,2,1,0:T(8,128)(2,1)S(1)}, u32[]{:S(2)}, u32[]{:S(2)}) collective-permute-start(bf16[2,2,128,640]{3,2,1,0:T(8,128)(2,1)} %add_convert_fusion.11), channel_id=1, source_target_pairs={{0,2},{1,3},{2,0},{3,1},{4,6},{5,7},{6,4},{7,5},{8,10},{9,11},{10,... | collective-permute-start | bytes 1966088 | tf_op jit(solution)/shard_map/ppermute | solution.py:1125
  444.5 30.3 %collective-permute-start.72 = (bf16[2,2,128,640]{3,2,1,0:T(8,128)(2,1)S(1)}, bf16[2,2,128,640]{3,2,1,0:T(8,128)(2,1)S(1)}, u32[]{:S(2)}, u32[]{:S(2)}) collective-permute-start(bf16[2,2,128,640]{3,2,1,0:T(8,128)(2,1)S(1)} %add_convert_fusion.10), channel_id=1, source_target_pairs={{0,4},{4,0},{1,5},{5,1},{2,6},{6,2},{3,7},{7,3},{8,12},{12,8},{9,1... | collective-permute-start | bytes 1966088 | tf_op jit(solution)/shard_map/ppermute | solution.py:1117
  468.6 26.9 %collective-permute-start.56 = (bf16[2,64,512]{2,1,0:T(8,128)(2,1)}, bf16[2,64,512]{2,1,0:T(8,128)(2,1)}, u32[]{:S(2)}, u32[]{:S(2)}) collective-permute-start(bf16[2,64,512]{2,1,0:T(8,128)(2,1)} %get-tuple-element.274), channel_id=1, source_target_pairs={{0,24},{8,16},{16,8},{24,0},{1,25},{9,17},{17,9},{25,1},{2,26},{10... | collective-permute-start | bytes 393224 | tf_op jit(solution)/shard_map/ppermute | solution.py:1136
  471.8 25.1 %collective-permute-start.57 = (bf16[2,64,512]{2,1,0:T(8,128)(2,1)}, bf16[2,64,512]{2,1,0:T(8,128)(2,1)}, u32[]{:S(2)}, u32[]{:S(2)}) collective-permute-start(bf16[2,64,512]{2,1,0:T(8,128)(2,1)} %get-tuple-element.191), channel_id=1, source_target_pairs={{0,16},{8,24},{16,0},{24,8},{1,17},{9,25},{17,1},{25,9},{2,18},{10... | collective-permute-start | bytes 393224 | tf_op jit(solution)/shard_map/ppermute | solution.py:1136
  474.8 24.2 %collective-permute-start.63 = (bf16[2,64,512]{2,1,0:T(8,128)(2,1)}, bf16[2,64,512]{2,1,0:T(8,128)(2,1)}, u32[]{:S(2)}, u32[]{:S(2)}) collective-permute-start(bf16[2,64,512]{2,1,0:T(8,128)(2,1)} %get-tuple-element.267), channel_id=1, source_target_pairs={{0,24},{8,16},{16,8},{24,0},{1,25},{9,17},{17,9},{25,1},{2,26},{10... | collective-permute-start | bytes 393224 | tf_op jit(solution)/shard_map/ppermute | solution.py:1136
  487.3 40.1 %all-to-all-start.6 = ((bf16[4,2,128,640]{3,2,1,0:T(8,128)(2,1)}), bf16[4,2,128,640]{3,2,1,0:T(8,128)(2,1)}, u32[]{:S(2)}, u32[]{:S(2)}) async-start(bf16[4,2,128,640]{3,2,1,0:T(8,128)(2,1)} %copy.415), calls=%async_computation.6 | async-start | bytes 2621440 | tf_op jit(solution)/shard_map/all_to_all | solution.py:1113
  (131 other events, 1437.7 us)

commit v6 on v5

--- a/solution.py
+++ b/solution.py
@@ -415,7 +415,7 @@
     return [lists[:2], lists[2:]]
 
 
-def call(kernel, inputs, in_specs, out_specs, out_shape, scratch, name, grid=2):
+def call(kernel, inputs, in_specs, out_specs, out_shape, scratch, name, grid=2, work=6):
     return pl.pallas_call(
         kernel,
         grid=(grid,),
@@ -425,7 +425,7 @@
         scratch_shapes=scratch,
         compiler_params=pltpu.CompilerParams(vmem_limit_bytes=44 << 20),
         cost_estimate=pl.CostEstimate(
-            flops=6 * 10**9, bytes_accessed=8 << 20, transcendentals=0
+            flops=work * 10**9, bytes_accessed=8 << 20, transcendentals=0
         ),
         name=name,
     )(*inputs)
@@ -611,6 +611,7 @@
         [],
         "column_ffn_grads",
         grid=1,
+        work=10,
     )
     return near, far, [grads[:2], grads[2:]]
 

time: 540 us -> 540 us (level)
  no operation moved by 1% of the time
where the time goes in v6:
time: 540 us; the launch traced here: 533 us
  waiting for transfers between devices  211 us (39%)
  starting transfers between devices  127 us (24%)
  Pallas kernels  67.5 us (12%)
  local copies, waits for them, and re-layouts  67.3 us (12%)
  other arithmetic  56.4 us (10%)
    ppermute x19, waiting for transfers between devices, swap_dp(): lax.ppermute(values, 'dp', [(i, i ^ k) for i in range(lax.axis_size('dp'))])  72.1 us
    pallas_call x5, Pallas kernels, call(): pl.pallas_call(kernel, grid=(grid,), in_specs=in_specs, out_specs=out_spe...  67.5 us
    ppermute x12, waiting for transfers between devices, swap_mp(): return lax.ppermute(values, 'mp', SWAP)  50.9 us
    all_to_all x7, starting transfers between devices, exchange(): return lax.all_to_all(values, axis, 0, 0, tiled=True)  47.3 us
    all_to_all x7, waiting for transfers between devices, exchange(): return lax.all_to_all(values, axis, 0, 0, tiled=True)  32 us
    ppermute x24, waiting for transfers between devices, trade_blocks(): lax.ppermute(blocks[k], axis, [(i, i ^ k) for i in range(size)])  29 us
    ppermute x19, starting transfers between devices, swap_dp(): lax.ppermute(values, 'dp', [(i, i ^ k) for i in range(lax.axis_size('dp'))])  28 us
    ppermute x24, starting transfers between devices, trade_blocks(): lax.ppermute(blocks[k], axis, [(i, i ^ k) for i in range(size)])  25.4 us
  transfers between devices with their start and end apart: 86, of which 36 were waited for; matrix products, arithmetic and copies ran while one was open for 19% of the time, Pallas kernels for 9%

profile of v6, /device:TPU:16, one launch (start us, length us, event | category | flops | bytes accessed | tf_op | source)
XLA Modules:
  0.0 532.9 jit_solution(12212853550938919021)
XLA Ops:
  17.3 7.1 %all-to-all-start = ((bf16[4,2,128,640]{3,2,1,0:T(8,128)(2,1)}), bf16[4,2,128,640]{3,2,1,0:T(8,128)(2,1)}, u32[]{:S(2)}, u32[]{:S(2)}) async-start(bf16[4,2,128,640]{3,2,1,0:T(8,128)(2,1)} %copy.372), calls=%async_computation | async-start | bytes 2621440 | tf_op jit(solution)/shard_map/all_to_all | solution.py:1114
  61.4 4.3 collective-permute-start.14
  67.1 7.5 %all-to-all-start.1 = ((bf16[4,2,1056,128]{3,2,1,0:T(8,128)(2,1)}), bf16[4,2,1056,128]{3,2,1,0:T(8,128)(2,1)}, u32[]{:S(2)}, u32[]{:S(2)}) async-start(bf16[4,2,1056,128]{3,2,1,0:T(8,128)(2,1)} %pad_maximum_fusion), calls=%async_computation.1 | async-start | bytes 4325376 | tf_op jit(solution)/shard_map/all_to_all | solution.py:1114
  74.6 6.9 %collective-permute-done.13 = bf16[64,2048]{1,0:T(8,128)(2,1)S(1)} collective-permute-done((bf16[64,2048]{1,0:T(8,128)(2,1)S(1)}, bf16[64,2048]{1,0:T(8,128)(2,1)S(1)}, u32[]{:S(2)}, u32[]{:S(2)}) %collective-permute-start.13) | collective-permute-done | bytes 262176 | tf_op jit(solution)/shard_map/ppermute | solution.py:1130
  81.5 15.1 %collective-permute-done.14 = bf16[64,2048]{1,0:T(8,128)(2,1)S(1)} collective-permute-done((bf16[64,2048]{1,0:T(8,128)(2,1)S(1)}, bf16[64,2048]{1,0:T(8,128)(2,1)S(1)}, u32[]{:S(2)}, u32[]{:S(2)}) %collective-permute-start.14) | collective-permute-done | bytes 262176 | tf_op jit(solution)/shard_map/ppermute | solution.py:1130
  100.9 14.8 %collective-permute-done.19.refs_5_ = bf16[2,2,128,640]{3,2,1,0:T(8,128)(2,1)S(1)} collective-permute-done((bf16[2,2,128,640]{3,2,1,0:T(8,128)(2,1)S(1)}, bf16[2,2,128,640]{3,2,1,0:T(8,128)(2,1)S(1)}, u32[]{:S(2)}, u32[]{:S(2)}) %collective-permute-start.19) | collective-permute-done | bytes 655392 | tf_op jit(solution)/shard_map/ppermute | solution.py:1126
  116.2 16.4 %column_forward.1 = (bf16[512,256]{1,0:T(8,128)(2,1)S(1)}, f32[2,2,256,256]{3,2,1,0:T(8,128)S(1)}, f32[512,256]{1,0:T(8,128)S(1)}, f32[512,256]{1,0:T(8,128)S(1)...) custom-call(bf16[256,2048]{1,0:T(8,128)(2,1)S(1)} %pad_maximum_fusio, ...), custom_call_target="tpu_custom_call" | custom-call | flops 6000000000 | bytes 8388608 | tf_op jit(solution)/shard_map/column_forward/pallas_call | solution.py:419
  143.2 6.6 %all-to-all-start.2 = ((bf16[4,64,2048]{2,1,0:T(8,128)(2,1)}), bf16[4,64,2048]{2,1,0:T(8,128)(2,1)S(1)}, u32[]{:S(2)}, u32[]{:S(2)}) async-start(bf16[4,64,2048]{2,1,0:T(8,128)(2,1)} %bitcast.53), calls=%async_computation.2 | async-start | bytes 2097152 | tf_op jit(solution)/shard_map/all_to_all | solution.py:1114
  158.0 14.4 %all-to-all-done.2 = bf16[4,64,2048]{2,1,0:T(8,128)(2,1)S(1)} async-done(((bf16[4,64,2048]{2,1,0:T(8,128)(2,1)}), bf16[4,64,2048]{2,1,0:T(8,128)(2,1)S(1)}, u32[]{:S(2)}, u32[]{:S(2)}) %all-to-all-start.2) | async-done | bytes 1048608 | tf_op jit(solution)/shard_map/all_to_all | solution.py:1114
  174.1 4.2 collective-permute-start.23
  179.0 24.9 %collective-permute-done.37.refs_7_.refs_2_ = bf16[4,2,1056,128]{3,2,1,0:T(8,128)(2,1)} collective-permute-done((bf16[4,2,1056,128]{3,2,1,0:T(8,128)(2,1)}, bf16[4,2,1056,128]{3,2,1,0:T(8,128)(2,1)}, u32[]{:S(2)}, u32[]{:S(2)}) %collective-permute-start.37) | collective-permute-done | bytes 2162720 | tf_op jit(solution)/shard_map/ppermute | solution.py:1118
  210.7 4.1 collective-permute-start.33
  215.1 15.7 %collective-permute-done.32 = bf16[64,2048]{1,0:T(8,128)(2,1)S(1)} collective-permute-done((bf16[64,2048]{1,0:T(8,128)(2,1)S(1)}, bf16[64,2048]{1,0:T(8,128)(2,1)S(1)}, u32[]{:S(2)}, u32[]{:S(2)}) %collective-permute-start.32) | collective-permute-done | bytes 262176 | tf_op jit(solution)/shard_map/ppermute | solution.py:1130
  236.3 17.2 %column_ffn.1 = (bf16[256,2048]{1,0:T(8,128)(2,1)S(1)}, bf16[256,2048]{1,0:T(8,128)(2,1)}, bf16[512,2048]{1,0:T(8,128)(2,1)}, bf16[512,2048]{1,0:T(8,128)(2,1)},...) custom-call(bf16[256,2048]{1,0:T(8,128)(2,1)S(1)} %pad_maximum_fusion.10.refs_0_, ...), custom_call_target="tpu_custom_call" | custom-call | flops 6000000000 | bytes 8388608 | tf_op jit(solution)/shard_map/column_ffn/pallas_call | solution.py:419
  261.3 4.3 collective-permute-start.43
  265.6 13.0 %column_ffn_grads.1 = (bf16[256,2048]{1,0:T(8,128)(2,1)S(1)}, bf16[256,2048]{1,0:T(8,128)(2,1)S(1)}, bf16[4,2,1056,128]{3,2,1,0:T(8,128)(2,1)}, bf16[4,2,1056,12...) custom-call(bf16[512,704]{1,0:T(8,128)(2,1)S(1)} %copy-done.24, ...), custom_call_target="tpu_custom_call" | custom-call | flops 10000000000 | bytes 8388608 | tf_op jit(solution)/shard_map/column_ffn_grads/pallas_call | solution.py:419
  289.9 3.8 collective-permute-start.46
  293.8 16.0 %collective-permute-done.45 = bf16[64,2048]{1,0:T(8,128)(2,1)S(1)} collective-permute-done((bf16[64,2048]{1,0:T(8,128)(2,1)S(1)}, bf16[64,2048]{1,0:T(8,128)(2,1)S(1)}, u32[]{:S(2)}, u32[]{:S(2)}) %collective-permute-start.45) | collective-permute-done | bytes 262176 | tf_op jit(solution)/shard_map/ppermute | solution.py:1130
  313.0 7.8 %all-to-all-start.3 = ((bf16[4,64,2048]{2,1,0:T(8,128)(2,1)}), bf16[4,64,2048]{2,1,0:T(8,128)(2,1)}, u32[]{:S(2)}, u32[]{:S(2)}) async-start(bf16[4,64,2048]{2,1,0:T(8,128)(2,1)} %bitcast.80), calls=%async_computation.3 | async-start | bytes 2097152 | tf_op jit(solution)/shard_map/all_to_all | solution.py:1114
  320.8 11.6 %collective-permute-done.74 = bf16[4,2,1056,128]{3,2,0,1:T(8,128)(2,1)} collective-permute-done((bf16[4,2,1056,128]{3,2,0,1:T(8,128)(2,1)}, bf16[4,2,1056,128]{3,2,0,1:T(8,128)(2,1)}, u32[]{:S(2)}, u32[]{:S(2)}) %collective-permute-start.74) | collective-permute-done | bytes 2162720 | tf_op jit(solution)/shard_map/ppermute | solution.py:1118
  341.8 16.0 %column_backward.1 = (bf16[512,1024]{1,0:T(8,128)(2,1)S(1)}, f32[512,2]{1,0:T(8,128)S(1)}, f32[2,12,256]{2,1,0:T(8,128)S(1)}, f32[2,1,128]{2,1,0:T(1,128)S(1)}, ...) custom-call(bf16[256,2048]{1,0:T(8,128)(2,1)S(1)} %pad_maximum_fusion.12.refs_0_, ...), custom_call_target="tpu_custom_call" | custom-call | flops 6000000000 | bytes 8388608 | tf_op jit(solution)/shard_map/column_backward/pallas_call | solution.py:419
  357.9 4.9 column_mixer_grads.1
  377.7 6.2 %all-to-all-start.4 = ((bf16[4,64,2048]{2,1,0:T(8,128)(2,1)}), bf16[4,64,2048]{2,1,0:T(8,128)(2,1)}, u32[]{:S(2)}, u32[]{:S(2)}) async-start(bf16[4,64,2048]{2,1,0:T(8,128)(2,1)} %bitcast.489), calls=%async_computation.4 | async-start | bytes 2097152 | tf_op jit(solution)/shard_map/all_to_all | solution.py:1114
  391.0 15.9 %all-to-all-done.4 = bf16[4,64,2048]{2,1,0:T(8,128)(2,1)} async-done(((bf16[4,64,2048]{2,1,0:T(8,128)(2,1)}), bf16[4,64,2048]{2,1,0:T(8,128)(2,1)}, u32[]{:S(2)}, u32[]{:S(2)}) %all-to-all-start.4) | async-done | bytes 1048608 | tf_op jit(solution)/shard_map/all_to_all | solution.py:1114
  406.9 7.8 %all-to-all-start.5 = ((bf16[4,2,1056,128]{3,2,1,0:T(8,128)(2,1)}), bf16[4,2,1056,128]{3,2,1,0:T(8,128)(2,1)}, u32[]{:S(2)}, u32[]{:S(2)}) async-start(bf16[4,2,1056,128]{3,2,1,0:T(8,128)(2,1)} %copy.413), calls=%async_computation.5 | async-start | bytes 4325376 | tf_op jit(solution)/shard_map/all_to_all | solution.py:1114
  429.0 3.7 collective-permute-done.66
  433.6 4.5 collective-permute-done.52
  450.0 12.2 %collective-permute-done.69 = f32[1,2,89,128]{3,2,1,0:T(8,128)S(1)} collective-permute-done((f32[1,2,89,128]{3,2,1,0:T(8,128)S(1)}, f32[1,2,89,128]{3,2,1,0:T(8,128)S(1)}, u32[]{:S(2)}, u32[]{:S(2)}) %collective-permute-start.69) | collective-permute-done | bytes 91168 | tf_op jit(solution)/shard_map/ppermute | solution.py:1130
  462.3 5.4 %collective-permute-done.55 = bf16[2,2,64,512]{3,2,1,0:T(8,128)(2,1)S(1)} collective-permute-done((bf16[2,2,64,512]{3,2,1,0:T(8,128)(2,1)S(1)}, bf16[2,2,64,512]{3,2,1,0:T(8,128)(2,1)S(1)}, u32[]{:S(2)}, u32[]{:S(2)}) %collective-permute-start.55) | collective-permute-done | bytes 262176 | tf_op jit(solution)/shard_map/ppermute | solution.py:1118
  480.4 3.7 collective-permute-start.64
  487.3 4.4 all-to-all-start.6
  501.2 16.8 %collective-permute-done.65 = bf16[2,64,512]{2,1,0:T(8,128)(2,1)S(1)} collective-permute-done((bf16[2,64,512]{2,1,0:T(8,128)(2,1)S(1)}, bf16[2,64,512]{2,1,0:T(8,128)(2,1)S(1)}, u32[]{:S(2)}, u32[]{:S(2)}) %collective-permute-start.65) | collective-permute-done | bytes 131104 | tf_op jit(solution)/shard_map/ppermute | solution.py:1137
  (538 shorter events, 213.1 us)
Async XLA Ops:
  17.3 37.0 %all-to-all-start = ((bf16[4,2,128,640]{3,2,1,0:T(8,128)(2,1)}), bf16[4,2,128,640]{3,2,1,0:T(8,128)(2,1)}, u32[]{:S(2)}, u32[]{:S(2)}) async-start(bf16[4,2,128,640]{3,2,1,0:T(8,128)(2,1)} %copy.372), calls=%async_computation | async-start | bytes 2621440 | tf_op jit(solution)/shard_map/all_to_all | solution.py:1114
  56.3 42.9 %collective-permute-start.17 = (bf16[4,2,128,640]{3,2,1,0:T(8,128)(2,1)}, bf16[4,2,128,640]{3,2,1,0:T(8,128)(2,1)S(1)}, u32[]{:S(2)}, u32[]{:S(2)}) collective-permute-start(bf16[4,2,128,640]{3,2,1,0:T(8,128)(2,1)} %all-to-all-done.refs_2_), channel_id=1, source_target_pairs={{0,2},{1,3},{2,0},{3,1},{4,6},{5,7},{6,4},{7,5},{8,10},{9,11},{10,... | collective-permute-start | bytes 3932168 | tf_op jit(solution)/shard_map/ppermute | solution.py:1126
  57.8 39.6 %collective-permute-start.18 = (bf16[4,2,128,640]{3,2,1,0:T(8,128)(2,1)}, bf16[4,2,128,640]{3,2,1,0:T(8,128)(2,1)}, u32[]{:S(2)}, u32[]{:S(2)}) collective-permute-start(bf16[4,2,128,640]{3,2,1,0:T(8,128)(2,1)} %all-to-all-done.refs_2_), channel_id=1, source_target_pairs={{0,4},{4,0},{1,5},{5,1},{2,6},{6,2},{3,7},{7,3},{8,12},{12,8},{9,1... | collective-permute-start | bytes 3932168 | tf_op jit(solution)/shard_map/ppermute | solution.py:1118
  61.4 35.2 %collective-permute-start.14 = (bf16[64,2048]{1,0:T(8,128)(2,1)S(1)}, bf16[64,2048]{1,0:T(8,128)(2,1)S(1)}, u32[]{:S(2)}, u32[]{:S(2)}) collective-permute-start(bf16[64,2048]{1,0:T(8,128)(2,1)S(1)} %pad_maximum_fusion.17), channel_id=1, source_target_pairs={{0,16},{8,24},{16,0},{24,8},{1,17},{9,25},{17,1},{25,9},{2,18},{10... | collective-permute-start | bytes 786440 | tf_op jit(solution)/shard_map/ppermute | solution.py:1130
  65.7 30.9 %collective-permute-start.15 = (bf16[64,2048]{1,0:T(8,128)(2,1)S(1)}, bf16[64,2048]{1,0:T(8,128)(2,1)S(1)}, u32[]{:S(2)}, u32[]{:S(2)}) collective-permute-start(bf16[64,2048]{1,0:T(8,128)(2,1)S(1)} %pad_maximum_fusion.17), channel_id=1, source_target_pairs={{0,8},{8,0},{16,24},{24,16},{1,9},{9,1},{17,25},{25,17},{2,10},{10... | collective-permute-start | bytes 786440 | tf_op jit(solution)/shard_map/ppermute | solution.py:1130
  67.1 76.1 %all-to-all-start.1 = ((bf16[4,2,1056,128]{3,2,1,0:T(8,128)(2,1)}), bf16[4,2,1056,128]{3,2,1,0:T(8,128)(2,1)}, u32[]{:S(2)}, u32[]{:S(2)}) async-start(bf16[4,2,1056,128]{3,2,1,0:T(8,128)(2,1)} %pad_maximum_fusion), calls=%async_computation.1 | async-start | bytes 4325376 | tf_op jit(solution)/shard_map/all_to_all | solution.py:1114
  143.2 29.2 %all-to-all-start.2 = ((bf16[4,64,2048]{2,1,0:T(8,128)(2,1)}), bf16[4,64,2048]{2,1,0:T(8,128)(2,1)S(1)}, u32[]{:S(2)}, u32[]{:S(2)}) async-start(bf16[4,64,2048]{2,1,0:T(8,128)(2,1)} %bitcast.53), calls=%async_computation.2 | async-start | bytes 2097152 | tf_op jit(solution)/shard_map/all_to_all | solution.py:1114
  153.5 53.4 %collective-permute-start.36 = (bf16[4,2,1056,128]{3,2,1,0:T(8,128)(2,1)}, bf16[4,2,1056,128]{3,2,1,0:T(8,128)(2,1)}, u32[]{:S(2)}, u32[]{:S(2)}) collective-permute-start(bf16[4,2,1056,128]{3,2,1,0:T(8,128)(2,1)} %all-to-all-done.1.refs_5_.refs_0_), channel_id=1, source_target_pairs={{0,2},{1,3},{2,0},{3,1},{4,6},{5,7},{6,4},{7,5},{8,10},{9,11},{10,... | collective-permute-start | bytes 6488072 | tf_op jit(solution)/shard_map/ppermute | solution.py:1126
  154.9 49.0 %collective-permute-start.37 = (bf16[4,2,1056,128]{3,2,1,0:T(8,128)(2,1)}, bf16[4,2,1056,128]{3,2,1,0:T(8,128)(2,1)}, u32[]{:S(2)}, u32[]{:S(2)}) collective-permute-start(bf16[4,2,1056,128]{3,2,1,0:T(8,128)(2,1)} %all-to-all-done.1.refs_5_.refs_0_), channel_id=1, source_target_pairs={{0,4},{4,0},{1,5},{5,1},{2,6},{6,2},{3,7},{7,3},{8,12},{12,8},{9,1... | collective-permute-start | bytes 6488072 | tf_op jit(solution)/shard_map/ppermute | solution.py:1118
  172.9 37.8 %collective-permute-start.22 = (bf16[64,2048]{1,0:T(8,128)(2,1)S(1)}, bf16[64,2048]{1,0:T(8,128)(2,1)S(1)}, u32[]{:S(2)}, u32[]{:S(2)}) collective-permute-start(bf16[64,2048]{1,0:T(8,128)(2,1)S(1)} %multiply_convert_fusion), channel_id=1, source_target_pairs={{0,24},{8,16},{16,8},{24,0},{1,25},{9,17},{17,9},{25,1},{2,26},{10... | collective-permute-start | bytes 786440 | tf_op jit(solution)/shard_map/ppermute | solution.py:1130
  174.1 36.7 %collective-permute-start.23 = (bf16[64,2048]{1,0:T(8,128)(2,1)S(1)}, bf16[64,2048]{1,0:T(8,128)(2,1)S(1)}, u32[]{:S(2)}, u32[]{:S(2)}) collective-permute-start(bf16[64,2048]{1,0:T(8,128)(2,1)S(1)} %multiply_convert_fusion), channel_id=1, source_target_pairs={{0,16},{8,24},{16,0},{24,8},{1,17},{9,25},{17,1},{25,9},{2,18},{10... | collective-permute-start | bytes 786440 | tf_op jit(solution)/shard_map/ppermute | solution.py:1130
  178.2 36.6 %collective-permute-start.24 = (bf16[64,2048]{1,0:T(8,128)(2,1)S(1)}, bf16[64,2048]{1,0:T(8,128)(2,1)S(1)}, u32[]{:S(2)}, u32[]{:S(2)}) collective-permute-start(bf16[64,2048]{1,0:T(8,128)(2,1)S(1)} %multiply_convert_fusion), channel_id=1, source_target_pairs={{0,8},{8,0},{16,24},{24,16},{1,9},{9,1},{17,25},{25,17},{2,10},{10... | collective-permute-start | bytes 786440 | tf_op jit(solution)/shard_map/ppermute | solution.py:1130
  206.2 26.8 %collective-permute-start.38 = (bf16[2,2,1056,128]{3,2,1,0:T(8,128)(2,1)}, bf16[2,2,1056,128]{3,2,1,0:T(8,128)(2,1)}, u32[]{:S(2)}, u32[]{:S(2)}) collective-permute-start(bf16[2,2,1056,128]{3,2,1,0:T(8,128)(2,1)} %slice.465), channel_id=1, source_target_pairs={{0,2},{1,3},{2,0},{3,1},{4,6},{5,7},{6,4},{7,5},{8,10},{9,11},{10,... | collective-permute-start | bytes 3244040 | tf_op jit(solution)/shard_map/ppermute | solution.py:1126
  209.2 24.8 %collective-permute-start.39 = (bf16[2,2,1056,128]{3,2,1,0:T(8,128)(2,1)}, bf16[2,2,1056,128]{3,2,1,0:T(8,128)(2,1)}, u32[]{:S(2)}, u32[]{:S(2)}) collective-permute-start(bf16[2,2,1056,128]{3,2,1,0:T(8,128)(2,1)} %slice.466), channel_id=1, source_target_pairs={{0,4},{4,0},{1,5},{5,1},{2,6},{6,2},{3,7},{7,3},{8,12},{12,8},{9,1... | collective-permute-start | bytes 3244040 | tf_op jit(solution)/shard_map/ppermute | solution.py:1118
  259.6 25.7 %collective-permute-start.44 = (bf16[64,2048]{1,0:T(8,128)(2,1)S(1)}, bf16[64,2048]{1,0:T(8,128)(2,1)S(1)}, u32[]{:S(2)}, u32[]{:S(2)}) collective-permute-start(bf16[64,2048]{1,0:T(8,128)(2,1)S(1)} %get-tuple-element.237), channel_id=1, source_target_pairs={{0,24},{8,16},{16,8},{24,0},{1,25},{9,17},{17,9},{25,1},{2,26},{10... | collective-permute-start | bytes 786440 | tf_op jit(solution)/shard_map/ppermute | solution.py:1130
  261.3 25.2 %collective-permute-start.43 = (bf16[64,2048]{1,0:T(8,128)(2,1)S(1)}, bf16[64,2048]{1,0:T(8,128)(2,1)S(1)}, u32[]{:S(2)}, u32[]{:S(2)}) collective-permute-start(bf16[64,2048]{1,0:T(8,128)(2,1)S(1)} %get-tuple-element.236), channel_id=1, source_target_pairs={{0,16},{8,24},{16,0},{24,8},{1,17},{9,25},{17,1},{25,9},{2,18},{10... | collective-permute-start | bytes 786440 | tf_op jit(solution)/shard_map/ppermute | solution.py:1130
  282.6 49.8 %collective-permute-start.74 = (bf16[4,2,1056,128]{3,2,0,1:T(8,128)(2,1)}, bf16[4,2,1056,128]{3,2,0,1:T(8,128)(2,1)}, u32[]{:S(2)}, u32[]{:S(2)}) collective-permute-start(bf16[4,2,1056,128]{3,2,0,1:T(8,128)(2,1)} %pad_maximum_fusion.1), channel_id=1, source_target_pairs={{0,4},{4,0},{1,5},{5,1},{2,6},{6,2},{3,7},{7,3},{8,12},{12,8},{9,1... | collective-permute-start | bytes 6488072 | tf_op jit(solution)/shard_map/ppermute | solution.py:1118
  285.3 51.2 %collective-permute-start.76 = (bf16[4,2,1056,128]{3,2,0,1:T(8,128)(2,1)}, bf16[4,2,1056,128]{3,2,0,1:T(8,128)(2,1)}, u32[]{:S(2)}, u32[]{:S(2)}) collective-permute-start(bf16[4,2,1056,128]{3,2,0,1:T(8,128)(2,1)} %pad_maximum_fusion.2), channel_id=1, source_target_pairs={{0,2},{1,3},{2,0},{3,1},{4,6},{5,7},{6,4},{7,5},{8,10},{9,11},{10,... | collective-permute-start | bytes 6488072 | tf_op jit(solution)/shard_map/ppermute | solution.py:1126
  312.9 26.6 %collective-permute-start.48 = (bf16[256,2048]{1,0:T(8,128)(2,1)S(1)}, bf16[256,2048]{1,0:T(8,128)(2,1)S(1)}, u32[]{:S(2)}, u32[]{:S(2)}) collective-permute-start(bf16[256,2048]{1,0:T(8,128)(2,1)S(1)} %pad_maximum_fusion.12.refs_0_), channel_id=1, source_target_pairs={{0,1},{1,0},{2,3},{3,2},{4,5},{5,4},{6,7},{7,6},{8,9},{9,8},{10,11... | collective-permute-start | bytes 3145736 | tf_op jit(solution)/shard_map/ppermute | solution.py:1122
  313.0 64.7 %all-to-all-start.3 = ((bf16[4,64,2048]{2,1,0:T(8,128)(2,1)}), bf16[4,64,2048]{2,1,0:T(8,128)(2,1)}, u32[]{:S(2)}, u32[]{:S(2)}) async-start(bf16[4,64,2048]{2,1,0:T(8,128)(2,1)} %bitcast.80), calls=%async_computation.3 | async-start | bytes 2097152 | tf_op jit(solution)/shard_map/all_to_all | solution.py:1114
  335.3 35.1 %collective-permute-start.75 = (bf16[2,2,1056,128]{3,2,0,1:T(8,128)(2,1)}, bf16[2,2,1056,128]{3,2,0,1:T(8,128)(2,1)}, u32[]{:S(2)}, u32[]{:S(2)}) collective-permute-start(bf16[2,2,1056,128]{3,2,0,1:T(8,128)(2,1)} %add_convert_fusion.3), channel_id=1, source_target_pairs={{0,2},{1,3},{2,0},{3,1},{4,6},{5,7},{6,4},{7,5},{8,10},{9,11},{10,... | collective-permute-start | bytes 3244040 | tf_op jit(solution)/shard_map/ppermute | solution.py:1126
  339.0 31.4 %collective-permute-start.77 = (bf16[2,2,1056,128]{3,2,0,1:T(8,128)(2,1)}, bf16[2,2,1056,128]{3,2,0,1:T(8,128)(2,1)}, u32[]{:S(2)}, u32[]{:S(2)}) collective-permute-start(bf16[2,2,1056,128]{3,2,0,1:T(8,128)(2,1)} %add_convert_fusion.1), channel_id=1, source_target_pairs={{0,4},{4,0},{1,5},{5,1},{2,6},{6,2},{3,7},{7,3},{8,12},{12,8},{9,1... | collective-permute-start | bytes 3244040 | tf_op jit(solution)/shard_map/ppermute | solution.py:1118
  365.2 51.9 %collective-permute-start.49 = (bf16[4,2,128,640]{3,2,1,0:T(8,128)(2,1)}, bf16[4,2,128,640]{3,2,1,0:T(8,128)(2,1)}, u32[]{:S(2)}, u32[]{:S(2)}) collective-permute-start(bf16[4,2,128,640]{3,2,1,0:T(8,128)(2,1)} %pad_maximum_fusion.5), channel_id=1, source_target_pairs={{0,4},{4,0},{1,5},{5,1},{2,6},{6,2},{3,7},{7,3},{8,12},{12,8},{9,1... | collective-permute-start | bytes 3932168 | tf_op jit(solution)/shard_map/ppermute | solution.py:1118
  367.9 49.1 %collective-permute-start.50 = (bf16[4,2,128,640]{3,2,1,0:T(8,128)(2,1)}, bf16[4,2,128,640]{3,2,1,0:T(8,128)(2,1)}, u32[]{:S(2)}, u32[]{:S(2)}) collective-permute-start(bf16[4,2,128,640]{3,2,1,0:T(8,128)(2,1)} %pad_maximum_fusion.6), channel_id=1, source_target_pairs={{0,2},{1,3},{2,0},{3,1},{4,6},{5,7},{6,4},{7,5},{8,10},{9,11},{10,... | collective-permute-start | bytes 3932168 | tf_op jit(solution)/shard_map/ppermute | solution.py:1126
  377.7 29.2 %all-to-all-start.4 = ((bf16[4,64,2048]{2,1,0:T(8,128)(2,1)}), bf16[4,64,2048]{2,1,0:T(8,128)(2,1)}, u32[]{:S(2)}, u32[]{:S(2)}) async-start(bf16[4,64,2048]{2,1,0:T(8,128)(2,1)} %bitcast.489), calls=%async_computation.4 | async-start | bytes 2097152 | tf_op jit(solution)/shard_map/all_to_all | solution.py:1114
  406.9 77.5 %all-to-all-start.5 = ((bf16[4,2,1056,128]{3,2,1,0:T(8,128)(2,1)}), bf16[4,2,1056,128]{3,2,1,0:T(8,128)(2,1)}, u32[]{:S(2)}, u32[]{:S(2)}) async-start(bf16[4,2,1056,128]{3,2,1,0:T(8,128)(2,1)} %copy.413), calls=%async_computation.5 | async-start | bytes 4325376 | tf_op jit(solution)/shard_map/all_to_all | solution.py:1114
  420.5 52.9 %collective-permute-start.71 = (bf16[2,2,128,640]{3,2,1,0:T(8,128)(2,1)}, bf16[2,2,128,640]{3,2,1,0:T(8,128)(2,1)S(1)}, u32[]{:S(2)}, u32[]{:S(2)}) collective-permute-start(bf16[2,2,128,640]{3,2,1,0:T(8,128)(2,1)} %add_convert_fusion.11), channel_id=1, source_target_pairs={{0,2},{1,3},{2,0},{3,1},{4,6},{5,7},{6,4},{7,5},{8,10},{9,11},{10,... | collective-permute-start | bytes 1966088 | tf_op jit(solution)/shard_map/ppermute | solution.py:1126
  444.5 30.3 %collective-permute-start.72 = (bf16[2,2,128,640]{3,2,1,0:T(8,128)(2,1)S(1)}, bf16[2,2,128,640]{3,2,1,0:T(8,128)(2,1)S(1)}, u32[]{:S(2)}, u32[]{:S(2)}) collective-permute-start(bf16[2,2,128,640]{3,2,1,0:T(8,128)(2,1)S(1)} %add_convert_fusion.10), channel_id=1, source_target_pairs={{0,4},{4,0},{1,5},{5,1},{2,6},{6,2},{3,7},{7,3},{8,12},{12,8},{9,1... | collective-permute-start | bytes 1966088 | tf_op jit(solution)/shard_map/ppermute | solution.py:1118
  468.6 26.9 %collective-permute-start.56 = (bf16[2,64,512]{2,1,0:T(8,128)(2,1)}, bf16[2,64,512]{2,1,0:T(8,128)(2,1)}, u32[]{:S(2)}, u32[]{:S(2)}) collective-permute-start(bf16[2,64,512]{2,1,0:T(8,128)(2,1)} %get-tuple-element.274), channel_id=1, source_target_pairs={{0,24},{8,16},{16,8},{24,0},{1,25},{9,17},{17,9},{25,1},{2,26},{10... | collective-permute-start | bytes 393224 | tf_op jit(solution)/shard_map/ppermute | solution.py:1137
  471.8 25.1 %collective-permute-start.57 = (bf16[2,64,512]{2,1,0:T(8,128)(2,1)}, bf16[2,64,512]{2,1,0:T(8,128)(2,1)}, u32[]{:S(2)}, u32[]{:S(2)}) collective-permute-start(bf16[2,64,512]{2,1,0:T(8,128)(2,1)} %get-tuple-element.191), channel_id=1, source_target_pairs={{0,16},{8,24},{16,0},{24,8},{1,17},{9,25},{17,1},{25,9},{2,18},{10... | collective-permute-start | bytes 393224 | tf_op jit(solution)/shard_map/ppermute | solution.py:1137
  474.8 24.2 %collective-permute-start.63 = (bf16[2,64,512]{2,1,0:T(8,128)(2,1)}, bf16[2,64,512]{2,1,0:T(8,128)(2,1)}, u32[]{:S(2)}, u32[]{:S(2)}) collective-permute-start(bf16[2,64,512]{2,1,0:T(8,128)(2,1)} %get-tuple-element.267), channel_id=1, source_target_pairs={{0,24},{8,16},{16,8},{24,0},{1,25},{9,17},{17,9},{25,1},{2,26},{10... | collective-permute-start | bytes 393224 | tf_op jit(solution)/shard_map/ppermute | solution.py:1137
  487.3 40.1 %all-to-all-start.6 = ((bf16[4,2,128,640]{3,2,1,0:T(8,128)(2,1)}), bf16[4,2,128,640]{3,2,1,0:T(8,128)(2,1)}, u32[]{:S(2)}, u32[]{:S(2)}) async-start(bf16[4,2,128,640]{3,2,1,0:T(8,128)(2,1)} %copy.415), calls=%async_computation.6 | async-start | bytes 2621440 | tf_op jit(solution)/shard_map/all_to_all | solution.py:1114
  (131 other events, 1437.7 us)
